TPU v7x, 32 devices: a whole 2x2x4 slice. The times are simulated.
32 devices in a mesh: dp: 8 (over y, x, core), ctx: 4 (over z).
Axes of the slice: x: 2, y: 2, z: 4, core: 2. Of those that a mesh axis runs over, the one named last changes fastest.
Arguments:
- queries: bfloat16 [8, 512, 2048], P('dp', 'ctx'), may hold values from -21 to 21
- keys: bfloat16 [8, 512, 512], P('dp', 'ctx'), may hold values from -21 to 21
- values: bfloat16 [8, 512, 512], P('dp', 'ctx'), may hold values from -6 to 6
- dout: bfloat16 [8, 512, 2048], P('dp', 'ctx'), may hold values from -6 to 6
- sinks: float32 [16], replicated, may hold values from 0 to 6
Outputs:
- grad_queries: bfloat16 [8, 512, 2048], P('dp', 'ctx')
- grad_keys: bfloat16 [8, 512, 512], P('dp', 'ctx')
- grad_values: bfloat16 [8, 512, 512], P('dp', 'ctx')
- sink_grad: float32 [16], replicated
All inputs are finite; a program needn't handle non-finite values.
Results may differ from a plain program's by a relative error of at most 0.03.
Values may be sent and summed in bfloat16 or wider, within the bound.
No kernel may reach another device: no remote copies, remote signals or barrier semaphores. Data moves between devices by JAX's collectives and lax.ppermute only.
A program may use at most 64 MiB of HBM per device.

v0:
```python
import jax
import jax.numpy as jnp
from jax import lax
from jax.sharding import PartitionSpec as P

HEADS = 16
KV_HEADS = 4
HEAD = 128
WINDOW = 128


def shifted(value, axis, steps):
    count = lax.axis_size(axis)
    leading, last = (max(0, -steps), min(count, count - steps))
    return lax.ppermute(value, axis, [(source, source + steps) for source in range(leading, last)])


def as_sent(x):
    return jax.tree.map(lambda a: a.astype(jnp.bfloat16) if a.dtype == jnp.float32 else a, x)


def block_terms(query_rows, key_rows, value_rows, grad_rows, sinks, allowed):
    group_size = HEADS // KV_HEADS
    row_count = query_rows.shape[0]
    key_count = key_rows.shape[0]
    score_scale = HEAD ** (-0.5)
    key_mask = jnp.broadcast_to(allowed[:, None, :], (row_count, group_size, key_count)).reshape(
        row_count * group_size, key_count
    )
    grad_query_list = []
    grad_key_list = []
    grad_value_list = []
    sink_list = []
    for kv_head in range(KV_HEADS):
        low = kv_head * group_size * HEAD
        high = (kv_head + 1) * group_size * HEAD
        query_group = query_rows[:, low:high].reshape(row_count * group_size, HEAD)
        grad_group = grad_rows[:, low:high].reshape(row_count * group_size, HEAD)
        key_group = key_rows[:, kv_head * HEAD : (kv_head + 1) * HEAD]
        value_group = value_rows[:, kv_head * HEAD : (kv_head + 1) * HEAD]
        scores = (
            lax.dot_general(
                query_group, key_group, (((1,), (1,)), ((), ())), preferred_element_type=jnp.float32
            )
            * score_scale
        )
        sink_rows = jnp.tile(sinks[kv_head * group_size : (kv_head + 1) * group_size], row_count)
        row_max = jnp.maximum(jnp.max(jnp.where(key_mask, scores, -jnp.inf), axis=1), sink_rows)
        weights = jnp.where(key_mask, jnp.exp(scores - row_max[:, None]), 0.0)
        row_total = jnp.exp(sink_rows - row_max) + jnp.sum(weights, axis=1)
        log_total = row_max + jnp.log(row_total)
        probabilities = jnp.where(key_mask, jnp.exp(scores - log_total[:, None]), 0.0)
        probs_low = probabilities.astype(jnp.bfloat16)
        attended = jnp.dot(probs_low, value_group, preferred_element_type=jnp.float32).astype(
            jnp.bfloat16
        )
        attended = lax.optimization_barrier(attended)
        row_delta = jnp.sum(grad_group.astype(jnp.float32) * attended.astype(jnp.float32), axis=1)
        grad_prob = lax.dot_general(
            grad_group, value_group, (((1,), (1,)), ((), ())), preferred_element_type=jnp.float32
        )
        dscore = (probabilities * (grad_prob - row_delta[:, None])).astype(jnp.bfloat16)
        grad_query = jnp.dot(dscore, key_group, preferred_element_type=jnp.float32) * score_scale
        grad_query_list.append(grad_query.reshape(row_count, group_size * HEAD))
        grad_key_list.append(
            lax.dot_general(
                dscore, query_group, (((0,), (0,)), ((), ())), preferred_element_type=jnp.float32
            )
            * score_scale
        )
        grad_value_list.append(
            lax.dot_general(
                probs_low, grad_group, (((0,), (0,)), ((), ())), preferred_element_type=jnp.float32
            )
        )
        sink_list.append(
            -jnp.sum(
                (jnp.exp(sink_rows - log_total) * row_delta).reshape(row_count, group_size), axis=0
            )
        )
    return (
        jnp.concatenate(grad_query_list, axis=1),
        jnp.concatenate(grad_key_list, axis=1),
        jnp.concatenate(grad_value_list, axis=1),
        jnp.concatenate(sink_list, axis=0),
    )


def body(queries, keys, values, dout, sinks):
    tok_rows = queries.shape[1]
    ctx_index = lax.axis_index("ctx")
    halo_keys, halo_values = shifted((keys, values), "ctx", 1)
    joined_keys = jnp.concatenate([halo_keys, keys], axis=1)
    joined_values = jnp.concatenate([halo_values, values], axis=1)
    query_pos = ctx_index * tok_rows + jnp.arange(tok_rows, dtype=jnp.int32)
    key_pos = ctx_index * tok_rows - tok_rows + jnp.arange(tok_rows + tok_rows, dtype=jnp.int32)
    allowed = (
        (key_pos[None, :] <= query_pos[:, None])
        & (key_pos[None, :] > query_pos[:, None] - WINDOW)
        & (key_pos[None, :] >= 0)
    )

    def per_sequence(query_rows, key_rows, value_rows, grad_rows):
        return block_terms(query_rows, key_rows, value_rows, grad_rows, sinks, allowed)

    grad_query, grad_key, grad_value, sink_terms = jax.vmap(per_sequence)(
        queries, joined_keys, joined_values, dout
    )
    back_keys, back_values = shifted(
        (as_sent(grad_key[:, :tok_rows]), as_sent(grad_value[:, :tok_rows])), "ctx", -1
    )
    own_keys = grad_key[:, tok_rows:]
    own_values = grad_value[:, tok_rows:]
    own_keys = jnp.concatenate(
        [own_keys[:, : tok_rows - tok_rows], own_keys[:, tok_rows - tok_rows :] + back_keys], axis=1
    )
    own_values = jnp.concatenate(
        [own_values[:, : tok_rows - tok_rows], own_values[:, tok_rows - tok_rows :] + back_values],
        axis=1,
    )
    local_sum = jnp.sum(sink_terms, axis=0)
    sink_total = lax.psum(lax.psum(local_sum, "ctx"), "dp")
    token_count = lax.axis_size("dp") * queries.shape[0] * lax.axis_size("ctx") * tok_rows
    sink_grad = sink_total / jnp.sqrt(jnp.float32(token_count))
    return (
        grad_query.astype(jnp.bfloat16),
        own_keys.astype(jnp.bfloat16),
        own_values.astype(jnp.bfloat16),
        sink_grad,
    )


def solution(mesh):
    return jax.shard_map(
        body,
        mesh=mesh,
        in_specs=(
            P("dp", "ctx", None),
            P("dp", "ctx", None),
            P("dp", "ctx", None),
            P("dp", "ctx", None),
            P(),
        ),
        out_specs=(P("dp", "ctx", None), P("dp", "ctx", None), P("dp", "ctx", None), P()),
        check_vma=False,
    )
```

profile of v0, /device:TPU:0, one launch (start us, length us, event | category | flops | bytes accessed | tf_op | source)
XLA Modules:
  0.0 82.2 jit_solution(14211904197299966016)
XLA Ops:
  0.6 5.1 %collective-permute-start = (bf16[1,128,512]{2,1,0:T(8,128)(2,1)}, bf16[1,128,512]{2,1,0:T(8,128)(2,1)S(1)}, u32[]{:S(2)}, u32[]{:S(2)}) collective-permute-start(bf16[1,128,512]{2,1,0:T(8,128)(2,1)} %param.6), channel_id=1, source_target_pairs={{0,1},{1,2},{2,3},{4,5},{5,6},{6,7},{8,9},{9,10},{10,11},{12,13},{... | collective-permute-start | bytes 393224 | tf_op jit(solution)/shard_map/ppermute | solution.py:15
  5.7 4.1 %collective-permute-start.1 = (bf16[1,128,512]{2,1,0:T(8,128)(2,1)}, bf16[1,128,512]{2,1,0:T(8,128)(2,1)}, u32[]{:S(2)}, u32[]{:S(2)}) collective-permute-start(bf16[1,128,512]{2,1,0:T(8,128)(2,1)} %param.7), channel_id=1, source_target_pairs={{0,1},{1,2},{2,3},{4,5},{5,6},{6,7},{8,9},{9,10},{10,11},{12,13},{... | collective-permute-start | bytes 393224 | tf_op jit(solution)/shard_map/ppermute | solution.py:15
  18.3 0.9 %copy-done.26 = bf16[1,128,512]{2,1,0:T(8,128)(2,1)S(1)} copy-done((bf16[1,128,512]{2,1,0:T(8,128)(2,1)S(1)}, bf16[1,128,512]{2,1,0:T(8,128)(2,1)}, u32[]{:S(2)}) %copy-start.26) | copy-done | bytes 131096
  21.0 0.7 reduce_sum.138
  21.8 0.7 reduce_max.48
  22.5 0.7 reduce_sum.141
  24.0 0.7 reduce_sum.144
  25.4 0.7 reduce_max.51
  26.9 0.9 %constant_dynamic-update-slice_fusion.3 = bf16[1,256,512]{2,1,0:T(8,128)(2,1)S(1)} fusion(bf16[1,128,512]{2,1,0:T(8,128)(2,1)} %collective-permute-done.1), kind=kLoop, calls=%fused_computation.93 | loop fusion | bytes 262144
  28.8 0.7 multiply_reduce_fusion.3
  29.6 1.4 %reduce_sum.139 = f32[1,128,4]{2,1,0:T(8,128)} reshape(f32[512]{0:T(512)} %multiply_reduce_fusion.3) | data formatting | bytes 4096 | tf_op jit(solution)/shard_map/vmap()/reduce_sum | solution.py:58
  31.0 0.9 %convolution_bitcast_fusion.3 = f32[1,256,128]{1,2,0:T(8,128)} fusion(bf16[512,128]{1,0:T(8,128)(2,1)S(1)} %reshape.1153, pred[512,256]{0,1:T(32,128)(4,1)S(1)} %copy.27, f32[512,256]{0,1:T(8,128)S(1)} %get-tuple-element.40, f32[512]{0:T(512)S(1)} %log_add_fusion.3), kind=kOutput, calls=%fused_computation.39 | convolution fusion | flops 33947648 | bytes 919552 | tf_op jit(solution)/shard_map/vmap()/dot_general | solution.py:72
  33.3 0.7 reduce_sum.142
  35.7 0.7 reduce_sum.145
  42.8 0.8 copy-done.21
  49.1 9.3 %psum.14 = f32[16]{0:T(128)S(1)} all-reduce(f32[16]{0:T(128)S(1)} %maximum_bitcast_fusion), channel_id=1, replica_groups=mesh['dp'=8,'ctx'=4] {'ctx'}, use_global_device_ids=true, to_apply=%region_16.17 | all-reduce | flops 16 | bytes 128 | tf_op jit(solution)/shard_map/psum | solution.py:122
  59.5 11.8 %psum.15 = f32[16]{0:T(128)S(1)} all-reduce(f32[16]{0:T(128)S(1)} %psum.14), channel_id=1, replica_groups=mesh['dp'=8,'ctx'=4] {'dp'}, use_global_device_ids=true, to_apply=%region_17.18 | all-reduce | flops 16 | bytes 128 | tf_op jit(solution)/shard_map/psum | solution.py:122
  71.5 1.3 %collective-permute-start.3 = (bf16[1,128,512]{1,2,0:T(8,128)(2,1)S(1)}, bf16[1,128,512]{1,2,0:T(8,128)(2,1)S(1)}, u32[]{:S(2)}, u32[]{:S(2)}) collective-permute-start(bf16[1,128,512]{1,2,0:T(8,128)(2,1)S(1)} %slice.146), channel_id=1, source_target_pairs={{1,0},{2,1},{3,2},{5,4},{6,5},{7,6},{9,8},{10,9},{11,10},{13,12},{... | collective-permute-start | bytes 393224 | tf_op jit(solution)/shard_map/ppermute | solution.py:15
  72.8 1.3 %collective-permute-start.2 = (bf16[1,128,512]{1,2,0:T(8,128)(2,1)S(1)}, bf16[1,128,512]{1,2,0:T(8,128)(2,1)S(1)}, u32[]{:S(2)}, u32[]{:S(2)}) collective-permute-start(bf16[1,128,512]{1,2,0:T(8,128)(2,1)S(1)} %slice.147), channel_id=1, source_target_pairs={{1,0},{2,1},{3,2},{5,4},{6,5},{7,6},{9,8},{10,9},{11,10},{13,12},{... | collective-permute-start | bytes 393224 | tf_op jit(solution)/shard_map/ppermute | solution.py:15
  74.5 0.8 %pad_maximum_fusion = bf16[1,128,2048]{2,1,0:T(8,128)(2,1)} fusion(bf16[1,128,512]{2,1,0:T(8,128)(2,1)S(1)} %concatenate.40, bf16[1,128,512]{2,1,0:T(8,128)(2,1)S(1)} %concatenate.39, bf16[1,128,512]{2,1,0:T(8,128)(2,1)S(1)} %concatenate.38, bf16[1,128,512]{2,1,0:T(8,128)(2,1)S(1)} %concatenate.37), kind=kLoop, calls=%fused_computation.52 | loop fusion | flops 2097152 | bytes 1048576 | tf_op jit(solution)/shard_map/vmap()/concatenate | solution.py:82
  75.9 3.5 %collective-permute-done.3 = bf16[1,128,512]{1,2,0:T(8,128)(2,1)S(1)} collective-permute-done((bf16[1,128,512]{1,2,0:T(8,128)(2,1)S(1)}, bf16[1,128,512]{1,2,0:T(8,128)(2,1)S(1)}, u32[]{:S(2)}, u32[]{:S(2)}) %collective-permute-start.3) | collective-permute-done | bytes 131104 | tf_op jit(solution)/shard_map/ppermute | solution.py:15
  79.4 0.8 copy.50
  80.2 1.2 %collective-permute-done.2 = bf16[1,128,512]{1,2,0:T(8,128)(2,1)S(1)} collective-permute-done((bf16[1,128,512]{1,2,0:T(8,128)(2,1)S(1)}, bf16[1,128,512]{1,2,0:T(8,128)(2,1)S(1)}, u32[]{:S(2)}, u32[]{:S(2)}) %collective-permute-start.2) | collective-permute-done | bytes 131104 | tf_op jit(solution)/shard_map/ppermute | solution.py:15
  81.4 0.8 copy.49
  (190 shorter events, 30.0 us)
Async XLA Ops:
  0.6 9.8 %copy-start.12 = (bf16[1,128,2048]{2,1,0:T(8,128)(2,1)S(1)}, bf16[1,128,2048]{2,1,0:T(8,128)(2,1)}, u32[]{:S(2)}) copy-start(bf16[1,128,2048]{2,1,0:T(8,128)(2,1)} %param.5) | copy-start | bytes 1572868
  0.6 17.6 %collective-permute-start = (bf16[1,128,512]{2,1,0:T(8,128)(2,1)}, bf16[1,128,512]{2,1,0:T(8,128)(2,1)S(1)}, u32[]{:S(2)}, u32[]{:S(2)}) collective-permute-start(bf16[1,128,512]{2,1,0:T(8,128)(2,1)} %param.6), channel_id=1, source_target_pairs={{0,1},{1,2},{2,3},{4,5},{5,6},{6,7},{8,9},{9,10},{10,11},{12,13},{... | collective-permute-start | bytes 393224 | tf_op jit(solution)/shard_map/ppermute | solution.py:15
  5.7 21.2 %collective-permute-start.1 = (bf16[1,128,512]{2,1,0:T(8,128)(2,1)}, bf16[1,128,512]{2,1,0:T(8,128)(2,1)}, u32[]{:S(2)}, u32[]{:S(2)}) collective-permute-start(bf16[1,128,512]{2,1,0:T(8,128)(2,1)} %param.7), channel_id=1, source_target_pairs={{0,1},{1,2},{2,3},{4,5},{5,6},{6,7},{8,9},{9,10},{10,11},{12,13},{... | collective-permute-start | bytes 393224 | tf_op jit(solution)/shard_map/ppermute | solution.py:15
  10.5 1.1 %copy-start.13 = (bf16[1,128,2048]{2,1,0:T(8,128)(2,1)S(1)}, bf16[1,128,2048]{2,1,0:T(8,128)(2,1)}, u32[]{:S(2)}) copy-start(bf16[1,128,2048]{2,1,0:T(8,128)(2,1)} %param.8) | copy-start | bytes 1572868
  10.6 8.5 %copy-start.2 = (bf16[512,128]{1,0:T(8,128)(2,1)}, bf16[512,128]{1,0:T(8,128)(2,1)S(1)}, u32[]{:S(2)}) copy-start(bf16[512,128]{1,0:T(8,128)(2,1)S(1)} %reshape.1163) | copy-start | bytes 393220
  10.7 8.7 %copy-start.4 = (bf16[512,128]{1,0:T(8,128)(2,1)}, bf16[512,128]{1,0:T(8,128)(2,1)S(1)}, u32[]{:S(2)}) copy-start(bf16[512,128]{1,0:T(8,128)(2,1)S(1)} %reshape.1159) | copy-start | bytes 393220
  10.8 8.8 %copy-start.6 = (bf16[512,128]{1,0:T(8,128)(2,1)}, bf16[512,128]{1,0:T(8,128)(2,1)S(1)}, u32[]{:S(2)}) copy-start(bf16[512,128]{1,0:T(8,128)(2,1)S(1)} %reshape.1155) | copy-start | bytes 393220
  11.6 8.3 %copy-start = (bf16[512,128]{1,0:T(8,128)(2,1)}, bf16[512,128]{1,0:T(8,128)(2,1)S(1)}, u32[]{:S(2)}) copy-start(bf16[512,128]{1,0:T(8,128)(2,1)S(1)} %reshape.1151) | copy-start | bytes 393220
  12.3 1.2 %copy-start.39 = (f32[4]{0:T(128)}, f32[4]{0:T(128)S(1)}, u32[]{:S(2)}) copy-start(f32[4]{0:T(128)S(1)} %get-tuple-element.36) | copy-start | bytes 52
  12.3 1.8 %copy-start.37 = (f32[4]{0:T(128)}, f32[4]{0:T(128)S(1)}, u32[]{:S(2)}) copy-start(f32[4]{0:T(128)S(1)} %get-tuple-element.39) | copy-start | bytes 52
  12.3 2.5 %copy-start.35 = (f32[4]{0:T(128)}, f32[4]{0:T(128)S(1)}, u32[]{:S(2)}) copy-start(f32[4]{0:T(128)S(1)} %get-tuple-element.38) | copy-start | bytes 52
  15.0 5.6 %copy-start.29 = (f32[512]{0:T(512)}, f32[512]{0:T(512)S(1)}, u32[]{:S(2)}) copy-start(f32[512]{0:T(512)S(1)} %tile.59) | copy-start | bytes 6148
  26.9 1.0 %copy-start.27 = (bf16[1,128,512]{2,1,0:T(8,128)(2,1)S(1)}, bf16[1,128,512]{2,1,0:T(8,128)(2,1)}, u32[]{:S(2)}) copy-start(bf16[1,128,512]{2,1,0:T(8,128)(2,1)} %param.7) | copy-start | bytes 393220
  27.9 1.0 %copy-start.11 = (f32[1,512,128]{2,1,0:T(8,128)S(1)}, f32[1,512,128]{2,1,0:T(8,128)}, u32[]{:S(2)}) copy-start(f32[1,512,128]{2,1,0:T(8,128)} %reshape.1166) | copy-start | bytes 786436
  32.2 1.0 %copy-start.10 = (f32[1,512,128]{2,1,0:T(8,128)S(1)}, f32[1,512,128]{2,1,0:T(8,128)}, u32[]{:S(2)}) copy-start(f32[1,512,128]{2,1,0:T(8,128)} %reshape.1167) | copy-start | bytes 786436
  34.6 1.0 %copy-start.9 = (f32[1,512,128]{2,1,0:T(8,128)S(1)}, f32[1,512,128]{2,1,0:T(8,128)}, u32[]{:S(2)}) copy-start(f32[1,512,128]{2,1,0:T(8,128)} %reshape.1168) | copy-start | bytes 786436
  37.0 1.0 %copy-start.8 = (f32[1,512,128]{2,1,0:T(8,128)S(1)}, f32[1,512,128]{2,1,0:T(8,128)}, u32[]{:S(2)}) copy-start(f32[1,512,128]{2,1,0:T(8,128)} %reshape.1169) | copy-start | bytes 786436
  41.9 1.8 %copy-start.42 = (f32[4]{0:T(128)S(1)}, f32[4]{0:T(128)}, u32[]{:S(2)}) copy-start(f32[4]{0:T(128)} %copy-done.41) | copy-start | bytes 52
  42.8 2.6 %copy-start.40 = (f32[4]{0:T(128)S(1)}, f32[4]{0:T(128)}, u32[]{:S(2)}) copy-start(f32[4]{0:T(128)} %copy-done.39) | copy-start | bytes 52
  44.5 1.1 %copy-start.23 = (f32[1,128,4]{2,1,0:T(8,128)S(1)}, f32[1,128,4]{2,1,0:T(8,128)}, u32[]{:S(2)}) copy-start(f32[1,128,4]{2,1,0:T(8,128)} %reduce_sum.145) | copy-start | bytes 6148
  46.4 0.9 %copy-start.16 = (f32[1,128,4]{2,1,0:T(8,128)S(1)}, f32[1,128,4]{2,1,0:T(8,128)}, u32[]{:S(2)}) copy-start(f32[1,128,4]{2,1,0:T(8,128)} %reduce_sum.147) | copy-start | bytes 6148
  59.3 12.1 %copy-start.14 = (f32[1,256,128]{1,2,0:T(8,128)S(1)}, f32[1,256,128]{1,2,0:T(8,128)}, u32[]{:S(2)}) copy-start(f32[1,256,128]{1,2,0:T(8,128)} %convolution_bitcast_fusion.3) | copy-start | bytes 393220
  71.5 8.0 %collective-permute-start.3 = (bf16[1,128,512]{1,2,0:T(8,128)(2,1)S(1)}, bf16[1,128,512]{1,2,0:T(8,128)(2,1)S(1)}, u32[]{:S(2)}, u32[]{:S(2)}) collective-permute-start(bf16[1,128,512]{1,2,0:T(8,128)(2,1)S(1)} %slice.146), channel_id=1, source_target_pairs={{1,0},{2,1},{3,2},{5,4},{6,5},{7,6},{9,8},{10,9},{11,10},{13,12},{... | collective-permute-start | bytes 393224 | tf_op jit(solution)/shard_map/ppermute | solution.py:15
  72.8 8.6 %collective-permute-start.2 = (bf16[1,128,512]{1,2,0:T(8,128)(2,1)S(1)}, bf16[1,128,512]{1,2,0:T(8,128)(2,1)S(1)}, u32[]{:S(2)}, u32[]{:S(2)}) collective-permute-start(bf16[1,128,512]{1,2,0:T(8,128)(2,1)S(1)} %slice.147), channel_id=1, source_target_pairs={{1,0},{2,1},{3,2},{5,4},{6,5},{7,6},{9,8},{10,9},{11,10},{13,12},{... | collective-permute-start | bytes 393224 | tf_op jit(solution)/shard_map/ppermute | solution.py:15
  (23 other events, 18.3 us)
where the time goes:
time: 83.1 us; the launch traced here: 82.2 us
  local copies, waits for them, and re-layouts  31.7 us (38%)
  blocking collectives  21.1 us (25%)
  starting transfers between devices  11.8 us (14%)
  matrix products  7.15 us (9%)
  waiting for transfers between devices  4.72 us (6%)
  other arithmetic  4.33 us (5%)
  between operations  1.42 us (2%)
    psum x2, blocking collectives, body(): sink_total = lax.psum(lax.psum(local_sum, 'ctx'), 'dp')  21.1 us
    unnamed x90, local copies, waits for them, and re-layouts  15.4 us
    ppermute x4, starting transfers between devices, shifted(): lax.ppermute(value, axis, [(source, source + steps) for source in range(l...  11.8 us
    ppermute x4, waiting for transfers between devices, shifted(): lax.ppermute(value, axis, [(source, source + steps) for source in range(l...  4.72 us
    reduce_sum x8, local copies, waits for them, and re-layouts, block_terms(): jnp.sum(grad_group.astype(jnp.float32) * attended.astype(jnp.float32), ax...  3.2 us
    reduce_sum x8, local copies, waits for them, and re-layouts, block_terms(): row_total = jnp.exp(sink_rows - row_max) + jnp.sum(weights, axis=1)  3.16 us
    reduce_max x8, local copies, waits for them, and re-layouts, block_terms(): jnp.max(jnp.where(key_mask, scores, -jnp.inf), axis=1)  3.15 us
    convert_element_type x4, local copies, waits for them, and re-layouts, block_terms(): grad_group.astype(jnp.float32) * attended.astype(jnp.float32)  2.86 us
  transfers between devices with their start and end apart: 4, of which 2 were waited for; matrix products, arithmetic and copies ran while one was open for 20% of the time, Pallas kernels for 0%

commit v1 on v0

v1 whole, which is shorter than its diff:
```python
import functools

import jax
import jax.numpy as jnp
from jax import lax
from jax.experimental import pallas as pl
from jax.experimental.pallas import tpu as pltpu
from jax.sharding import PartitionSpec as P

HEADS = 16
KV_HEADS = 4
HEAD = 128
WINDOW = 128
GROUP = HEADS // KV_HEADS
SCALE = HEAD ** (-0.5)
LOG2E = 1.4426950408889634


def shifted(value, axis, steps):
    count = lax.axis_size(axis)
    leading, last = (max(0, -steps), min(count, count - steps))
    return lax.ppermute(value, axis, [(source, source + steps) for source in range(leading, last)])


def dot(a, b, dims):
    return lax.dot_general(a, b, (dims, ((), ())), preferred_element_type=jnp.float32)


def attention_kernel(first_ref, sinks_ref, q_ref, k_ref, v_ref, do_ref, hk_ref, hv_ref,
                     dq_ref, own_ref, back_ref, sink_ref):
    batch, rows, _ = q_ref.shape
    wide = GROUP * rows
    key_pos = lax.broadcasted_iota(jnp.int32, (rows, wide), 0)
    query_pos = lax.rem(lax.broadcasted_iota(jnp.int32, (rows, wide), 1), rows)
    own = key_pos <= query_pos
    bias = jnp.where(jnp.logical_and(first_ref[0] == 1, jnp.logical_not(own)), -1e30, 0.0)
    for b in range(batch):
        for g in range(KV_HEADS):
            kv = slice(g * HEAD, (g + 1) * HEAD)
            heads = range(g * GROUP, (g + 1) * GROUP)
            query = jnp.concatenate([q_ref[b, :, h * HEAD:(h + 1) * HEAD] for h in heads], axis=0)
            grad = jnp.concatenate([do_ref[b, :, h * HEAD:(h + 1) * HEAD] for h in heads], axis=0)
            key = jnp.concatenate([k_ref[b, :, kv], hk_ref[b, :, kv]], axis=0)
            value = jnp.concatenate([v_ref[b, :, kv], hv_ref[b, :, kv]], axis=0)
            scores = dot(key, query, ((1,), (1,)))
            grad_probs = dot(value, grad, ((1,), (1,)))
            score = jnp.where(own, scores[:rows], scores[rows:]) * (SCALE * LOG2E) + bias
            grad_prob = jnp.where(own, grad_probs[:rows], grad_probs[rows:])
            sink = jnp.concatenate(
                [jnp.full((1, rows), sinks_ref[h] * LOG2E, jnp.float32) for h in heads], axis=1)
            top = jnp.maximum(jnp.max(score, axis=0, keepdims=True), sink)
            weight = jnp.exp2(score - top)
            sink_weight = jnp.exp2(sink - top)
            scale = 1.0 / (jnp.sum(weight, axis=0, keepdims=True) + sink_weight)
            prob = weight * scale
            delta = jnp.sum(prob * grad_prob, axis=0, keepdims=True)
            dscore = prob * (grad_prob - delta)
            sink_term = sink_weight * scale * delta
            for n, h in enumerate(heads):
                term = sink_term[:, n * rows:(n + 1) * rows]
                if b == 0:
                    sink_ref[h:h + 1, :] = term
                else:
                    sink_ref[h:h + 1, :] += term
            zero = jnp.zeros_like(prob)
            probs = jnp.concatenate(
                [jnp.where(own, prob, zero), jnp.where(own, zero, prob)], axis=0).astype(jnp.bfloat16)
            dscores = jnp.concatenate(
                [jnp.where(own, dscore, zero), jnp.where(own, zero, dscore)], axis=0).astype(jnp.bfloat16)
            grad_key = dot(dscores, query, ((1,), (0,))) * SCALE
            grad_value = dot(probs, grad, ((1,), (0,)))
            grad_query = (dot(dscores, key, ((0,), (0,))) * SCALE).astype(jnp.bfloat16)
            for n, h in enumerate(heads):
                dq_ref[b, :, h * HEAD:(h + 1) * HEAD] = grad_query[n * rows:(n + 1) * rows]
            vcol = slice((KV_HEADS + g) * HEAD, (KV_HEADS + g + 1) * HEAD)
            own_ref[b, :, kv] = grad_key[:rows]
            own_ref[b, :, vcol] = grad_value[:rows]
            back_ref[b, :, kv] = grad_key[rows:].astype(jnp.bfloat16)
            back_ref[b, :, vcol] = grad_value[rows:].astype(jnp.bfloat16)


def attention(first, sinks, queries, keys, values, dout, halo_keys, halo_values):
    batch, rows, width = queries.shape
    kv_width = keys.shape[2]
    vmem = pl.BlockSpec(memory_space=pltpu.VMEM)
    smem = pl.BlockSpec(memory_space=pltpu.SMEM)
    return pl.pallas_call(
        attention_kernel,
        out_shape=(
            jax.ShapeDtypeStruct((batch, rows, width), jnp.bfloat16),
            jax.ShapeDtypeStruct((batch, rows, 2 * kv_width), jnp.float32),
            jax.ShapeDtypeStruct((batch, rows, 2 * kv_width), jnp.bfloat16),
            jax.ShapeDtypeStruct((HEADS, rows), jnp.float32),
        ),
        in_specs=[smem, smem] + [vmem] * 6,
        out_specs=(vmem,) * 4,
        compiler_params=pltpu.CompilerParams(vmem_limit_bytes=32 * 1024 * 1024),
        name="attention",
    )(first, sinks, queries, keys, values, dout, halo_keys, halo_values)


def total_over(value, axis):
    count = lax.axis_size(axis)
    if count & (count - 1):
        return lax.psum(value, axis)
    step = 1
    while step < count:
        value = value + lax.ppermute(value, axis, [(i, i ^ step) for i in range(count)])
        step *= 2
    return value


def body(queries, keys, values, dout, sinks):
    batch, rows, _ = queries.shape
    assert rows == WINDOW
    first = (lax.axis_index("ctx") == 0).astype(jnp.int32).reshape(1)
    halo_keys = shifted(keys, "ctx", 1)
    halo_values = shifted(values, "ctx", 1)
    grad_query, own, back, sink_terms = attention(
        first, sinks, queries, keys, values, dout, halo_keys, halo_values)
    arrived = shifted(back, "ctx", -1)
    total = total_over(total_over(sink_terms, "dp"), "ctx")
    joined = (own + arrived.astype(jnp.float32)).astype(jnp.bfloat16)
    kv_width = keys.shape[2]
    positions = lax.axis_size("dp") * batch * lax.axis_size("ctx") * rows
    sink_grad = -jnp.sum(total, axis=1) / jnp.sqrt(jnp.float32(positions))
    return grad_query, joined[:, :, :kv_width], joined[:, :, kv_width:], sink_grad


def solution(mesh):
    whole = P("dp", "ctx", None)
    return jax.shard_map(
        body,
        mesh=mesh,
        in_specs=(whole, whole, whole, whole, P()),
        out_specs=(whole, whole, whole, P()),
        check_vma=False,
    )
```

time: 83.1 us -> 44.2 us (0.53)
  local copies, waits for them, and re-layouts: 31.7 us -> 4.61 us
  blocking collectives: 21.1 us -> 0 us
  waiting for transfers between devices: 4.72 us -> 16.2 us
  matrix products: 7.15 us -> 0 us
  starting transfers between devices: 11.8 us -> 18.1 us
  Pallas kernels: 0 us -> 3.62 us
  other arithmetic: 4.33 us -> 0.71 us
    psum x2 -> x0, blocking collectives: 21.1 us -> none  [body(): sink_total = lax.psum(lax.psum(local_sum, 'ctx'), 'dp')]
    unnamed x90 -> x10, local copies, waits for them, and re-layouts: 15.4 us -> 3.89 us
    ppermute x0 -> x5, starting transfers between devices: none -> 8.39 us  [total_over(): lax.ppermute(value, axis, [(i, i ^ step) for i in range(count)])]
    ppermute x0 -> x5, waiting for transfers between devices: none -> 7.52 us  [total_over(): lax.ppermute(value, axis, [(i, i ^ step) for i in range(count)])]
    dot_general x24 -> x0, matrix products: 7.15 us -> none  [the longest x4 1.74 us: block_terms(): lax.dot_general(probs_low, grad_group, (((0,), (0,)), ((), ())), preferre...]
    reduce_sum x16 -> x0, local copies, waits for them, and re-layouts: 6.36 us -> none  [the longest x8 3.2 us: block_terms(): jnp.sum(grad_group.astype(jnp.float32) * attended.astype(jnp.float32), ax...]
    ppermute x4 -> x3, waiting for transfers between devices: 4.72 us -> 8.69 us  [shifted(): lax.ppermute(value, axis, [(source, source + steps) for source in range(l...]
    pallas_call x0 -> x1, Pallas kernels: none -> 3.62 us  [attention(): pl.pallas_call(attention_kernel, out_shape=(jax.ShapeDtypeStruct((batch,...]
  transfers between devices with their start and end apart: 4 -> 8, of which waited for: 2 -> 7; matrix products, arithmetic and copies ran while one was open for 20% -> 1% of each run, Pallas kernels for 0% -> 0%
where the time goes in v1:
time: 44.2 us; the launch traced here: 43.9 us
  starting transfers between devices  18.1 us (41%)
  waiting for transfers between devices  16.2 us (37%)
  local copies, waits for them, and re-layouts  4.61 us (10%)
  Pallas kernels  3.62 us (8%)
  other arithmetic  0.71 us (2%)
  between operations  0.7 us (2%)
    ppermute x3, starting transfers between devices, shifted(): lax.ppermute(value, axis, [(source, source + steps) for source in range(l...  9.7 us
    ppermute x3, waiting for transfers between devices, shifted(): lax.ppermute(value, axis, [(source, source + steps) for source in range(l...  8.69 us
    ppermute x5, starting transfers between devices, total_over(): lax.ppermute(value, axis, [(i, i ^ step) for i in range(count)])  8.39 us
    ppermute x5, waiting for transfers between devices, total_over(): lax.ppermute(value, axis, [(i, i ^ step) for i in range(count)])  7.52 us
    unnamed x10, local copies, waits for them, and re-layouts  3.89 us
    pallas_call x1, Pallas kernels, attention(): pl.pallas_call(attention_kernel, out_shape=(jax.ShapeDtypeStruct((batch,...  3.62 us
  transfers between devices with their start and end apart: 8, of which 7 were waited for; matrix products, arithmetic and copies ran while one was open for 1% of the time, Pallas kernels for 0%

profile of v1, /device:TPU:0, one launch (start us, length us, event | category | flops | bytes accessed | tf_op | source)
XLA Modules:
  0.0 43.9 jit_solution(5932916151858795354)
XLA Ops:
  0.6 4.9 %collective-permute-start = (bf16[1,128,512]{2,1,0:T(8,128)(2,1)}, bf16[1,128,512]{2,1,0:T(8,128)(2,1)S(1)}, u32[]{:S(2)}, u32[]{:S(2)}) collective-permute-start(bf16[1,128,512]{2,1,0:T(8,128)(2,1)} %k_ref.1), channel_id=1, source_target_pairs={{0,1},{1,2},{2,3},{4,5},{5,6},{6,7},{8,9},{9,10},{10,11},{12,13},{... | collective-permute-start | bytes 393224 | tf_op jit(solution)/shard_map/ppermute | solution.py:22
  5.6 3.5 %collective-permute-start.1 = (bf16[1,128,512]{2,1,0:T(8,128)(2,1)}, bf16[1,128,512]{2,1,0:T(8,128)(2,1)S(1)}, u32[]{:S(2)}, u32[]{:S(2)}) collective-permute-start(bf16[1,128,512]{2,1,0:T(8,128)(2,1)} %v_ref.1), channel_id=1, source_target_pairs={{0,1},{1,2},{2,3},{4,5},{5,6},{6,7},{8,9},{9,10},{10,11},{12,13},{... | collective-permute-start | bytes 393224 | tf_op jit(solution)/shard_map/ppermute | solution.py:22
  9.1 0.0 collective-permute-done.hk_ref
  9.1 2.8 %collective-permute-done.1.hv_ref = bf16[1,128,512]{2,1,0:T(8,128)(2,1)S(1)} collective-permute-done((bf16[1,128,512]{2,1,0:T(8,128)(2,1)}, bf16[1,128,512]{2,1,0:T(8,128)(2,1)S(1)}, u32[]{:S(2)}, u32[]{:S(2)}) %collective-permute-start.1) | collective-permute-done | bytes 131104 | tf_op jit(solution)/shard_map/ppermute | solution.py:22
  11.9 1.0 %copy-done = bf16[1,128,2048]{2,1,0:T(8,128)(2,1)S(1)} copy-done((bf16[1,128,2048]{2,1,0:T(8,128)(2,1)S(1)}, bf16[1,128,2048]{2,1,0:T(8,128)(2,1)}, u32[]{:S(2)}) %copy-start) | copy-done | bytes 524312
  12.9 1.0 %copy-done.1 = bf16[1,128,2048]{2,1,0:T(8,128)(2,1)S(1)} copy-done((bf16[1,128,2048]{2,1,0:T(8,128)(2,1)S(1)}, bf16[1,128,2048]{2,1,0:T(8,128)(2,1)}, u32[]{:S(2)}) %copy-start.1) | copy-done | bytes 524312
  14.0 0.9 %copy-done.2 = bf16[1,128,512]{2,1,0:T(8,128)(2,1)S(1)} copy-done((bf16[1,128,512]{2,1,0:T(8,128)(2,1)S(1)}, bf16[1,128,512]{2,1,0:T(8,128)(2,1)}, u32[]{:S(2)}) %copy-start.2) | copy-done | bytes 131096
  14.9 0.9 %copy-done.3 = bf16[1,128,512]{2,1,0:T(8,128)(2,1)S(1)} copy-done((bf16[1,128,512]{2,1,0:T(8,128)(2,1)S(1)}, bf16[1,128,512]{2,1,0:T(8,128)(2,1)}, u32[]{:S(2)}) %copy-start.3) | copy-done | bytes 131096
  15.8 3.6 %attention.1 = (bf16[1,128,2048]{2,1,0:T(8,128)(2,1)}, f32[1,128,1024]{2,1,0:T(8,128)S(1)}, bf16[1,128,1024]{2,1,0:T(8,128)(2,1)S(1)}, f32[16,128]{1,0:T(8,128)S(1)}) custom-call(s32[1]{0:T(128)} %bitcast.first_ref, f32[16]{0:T(128)S(1)} %copy-done.4, bf16[1,128,2048]{2,1,0:T(8,128)(2,1)S(1)} %copy-done, bf16[1,128,512]{2,1,0:T(8,128)(2,1)S(1)} %copy-done.2, ...), custom_call_target="tpu_custom_call" | custom-call | tf_op jit(solution)/shard_map/attention/pallas_call | solution.py:87
  19.4 1.2 %collective-permute-done.3 = f32[16,128]{1,0:T(8,128)S(1)} collective-permute-done((f32[16,128]{1,0:T(8,128)S(1)}, f32[16,128]{1,0:T(8,128)S(1)}, u32[]{:S(2)}, u32[]{:S(2)}) %collective-permute-start.3) | collective-permute-done | bytes 8224 | tf_op jit(solution)/shard_map/ppermute | solution.py:108
  20.6 1.5 %collective-permute-start.4 = (f32[16,128]{1,0:T(8,128)S(1)}, f32[16,128]{1,0:T(8,128)S(1)}, u32[]{:S(2)}, u32[]{:S(2)}) collective-permute-start(f32[16,128]{1,0:T(8,128)S(1)} %add.19), channel_id=1, source_target_pairs={{0,8},{4,12},{8,0},{12,4},{16,24},{20,28},{24,16},{28,20},{1,9},{5... | collective-permute-start | bytes 24584 | tf_op jit(solution)/shard_map/ppermute | solution.py:108
  22.1 2.2 %collective-permute-done.4 = f32[16,128]{1,0:T(8,128)S(1)} collective-permute-done((f32[16,128]{1,0:T(8,128)S(1)}, f32[16,128]{1,0:T(8,128)S(1)}, u32[]{:S(2)}, u32[]{:S(2)}) %collective-permute-start.4) | collective-permute-done | bytes 8224 | tf_op jit(solution)/shard_map/ppermute | solution.py:108
  24.2 1.5 %collective-permute-start.5 = (f32[16,128]{1,0:T(8,128)S(1)}, f32[16,128]{1,0:T(8,128)S(1)}, u32[]{:S(2)}, u32[]{:S(2)}) collective-permute-start(f32[16,128]{1,0:T(8,128)S(1)} %add.20), channel_id=1, source_target_pairs={{0,16},{4,20},{8,24},{12,28},{16,0},{20,4},{24,8},{28,12},{1,17},{... | collective-permute-start | bytes 24584 | tf_op jit(solution)/shard_map/ppermute | solution.py:108
  25.7 2.1 %collective-permute-done.5 = f32[16,128]{1,0:T(8,128)S(1)} collective-permute-done((f32[16,128]{1,0:T(8,128)S(1)}, f32[16,128]{1,0:T(8,128)S(1)}, u32[]{:S(2)}, u32[]{:S(2)}) %collective-permute-start.5) | collective-permute-done | bytes 8224 | tf_op jit(solution)/shard_map/ppermute | solution.py:108
  27.9 2.3 %collective-permute-start.6 = (f32[16,128]{1,0:T(8,128)S(1)}, f32[16,128]{1,0:T(8,128)S(1)}, u32[]{:S(2)}, u32[]{:S(2)}) collective-permute-start(f32[16,128]{1,0:T(8,128)S(1)} %add.21), channel_id=1, source_target_pairs={{0,1},{1,0},{2,3},{3,2},{4,5},{5,4},{6,7},{7,6},{8,9},{9,8},{10,11... | collective-permute-start | bytes 24584 | tf_op jit(solution)/shard_map/ppermute | solution.py:108
  30.2 1.6 %collective-permute-done.6 = f32[16,128]{1,0:T(8,128)S(1)} collective-permute-done((f32[16,128]{1,0:T(8,128)S(1)}, f32[16,128]{1,0:T(8,128)S(1)}, u32[]{:S(2)}, u32[]{:S(2)}) %collective-permute-start.6) | collective-permute-done | bytes 8224 | tf_op jit(solution)/shard_map/ppermute | solution.py:108
  31.9 3.0 %collective-permute-start.7 = (f32[16,128]{1,0:T(8,128)S(1)}, f32[16,128]{1,0:T(8,128)S(1)}, u32[]{:S(2)}, u32[]{:S(2)}) collective-permute-start(f32[16,128]{1,0:T(8,128)S(1)} %add.22), channel_id=1, source_target_pairs={{0,2},{1,3},{2,0},{3,1},{4,6},{5,7},{6,4},{7,5},{8,10},{9,11},{10,... | collective-permute-start | bytes 24584 | tf_op jit(solution)/shard_map/ppermute | solution.py:108
  34.9 1.3 %collective-permute-start.2 = (bf16[1,128,1024]{2,1,0:T(8,128)(2,1)S(1)}, bf16[1,128,1024]{2,1,0:T(8,128)(2,1)S(1)}, u32[]{:S(2)}, u32[]{:S(2)}) collective-permute-start(bf16[1,128,1024]{2,1,0:T(8,128)(2,1)S(1)} %get-tuple-element.10), channel_id=1, source_target_pairs={{1,0},{2,1},{3,2},{5,4},{6,5},{7,6},{9,8},{10,9},{11,10},{13,12},{... | collective-permute-start | bytes 786440 | tf_op jit(solution)/shard_map/ppermute | solution.py:22
  36.2 0.4 collective-permute-done.7
  36.6 0.1 add_reduce_fusion
  36.7 0.5 %negate_multiply_fusion = f32[16]{0:T(128)} fusion(f32[16]{0:T(128)S(1)} %add_reduce_fusion), kind=kLoop, calls=%fused_computation.2 | loop fusion | flops 32 | bytes 128 | tf_op jit(solution)/shard_map/div | solution.py:126
  37.2 5.9 %collective-permute-done.2 = bf16[1,128,1024]{2,1,0:T(8,128)(2,1)S(1)} collective-permute-done((bf16[1,128,1024]{2,1,0:T(8,128)(2,1)S(1)}, bf16[1,128,1024]{2,1,0:T(8,128)(2,1)S(1)}, u32[]{:S(2)}, u32[]{:S(2)}) %collective-permute-start.2) | collective-permute-done | bytes 262176 | tf_op jit(solution)/shard_map/ppermute | solution.py:22
  43.1 0.1 add_convert_fusion
  43.2 0.7 %fusion = (bf16[1,128,512]{2,1,0:T(8,128)(2,1)}, bf16[1,128,512]{2,1,0:T(8,128)(2,1)}) fusion(bf16[1,128,1024]{2,1,0:T(8,128)(2,1)S(1)} %add_convert_fusion), kind=kLoop, calls=%fused_computation.3 | loop fusion | bytes 524288 | tf_op jit(solution)/shard_map/slice | solution.py:127
  (11 shorter events, 0.0 us)
Async XLA Ops:
  0.6 8.5 %collective-permute-start = (bf16[1,128,512]{2,1,0:T(8,128)(2,1)}, bf16[1,128,512]{2,1,0:T(8,128)(2,1)S(1)}, u32[]{:S(2)}, u32[]{:S(2)}) collective-permute-start(bf16[1,128,512]{2,1,0:T(8,128)(2,1)} %k_ref.1), channel_id=1, source_target_pairs={{0,1},{1,2},{2,3},{4,5},{5,6},{6,7},{8,9},{9,10},{10,11},{12,13},{... | collective-permute-start | bytes 393224 | tf_op jit(solution)/shard_map/ppermute | solution.py:22
  5.6 6.3 %collective-permute-start.1 = (bf16[1,128,512]{2,1,0:T(8,128)(2,1)}, bf16[1,128,512]{2,1,0:T(8,128)(2,1)S(1)}, u32[]{:S(2)}, u32[]{:S(2)}) collective-permute-start(bf16[1,128,512]{2,1,0:T(8,128)(2,1)} %v_ref.1), channel_id=1, source_target_pairs={{0,1},{1,2},{2,3},{4,5},{5,6},{6,7},{8,9},{9,10},{10,11},{12,13},{... | collective-permute-start | bytes 393224 | tf_op jit(solution)/shard_map/ppermute | solution.py:22
  9.1 2.8 %copy-start.4 = (f32[16]{0:T(128)S(1)}, f32[16]{0:T(128)}, u32[]{:S(2)}) copy-start(f32[16]{0:T(128)} %sinks_ref.1) | copy-start | bytes 196
  11.9 1.0 %copy-start = (bf16[1,128,2048]{2,1,0:T(8,128)(2,1)S(1)}, bf16[1,128,2048]{2,1,0:T(8,128)(2,1)}, u32[]{:S(2)}) copy-start(bf16[1,128,2048]{2,1,0:T(8,128)(2,1)} %q_ref.1) | copy-start | bytes 1572868
  12.9 1.0 %copy-start.1 = (bf16[1,128,2048]{2,1,0:T(8,128)(2,1)S(1)}, bf16[1,128,2048]{2,1,0:T(8,128)(2,1)}, u32[]{:S(2)}) copy-start(bf16[1,128,2048]{2,1,0:T(8,128)(2,1)} %do_ref.1) | copy-start | bytes 1572868
  14.0 0.9 %copy-start.2 = (bf16[1,128,512]{2,1,0:T(8,128)(2,1)S(1)}, bf16[1,128,512]{2,1,0:T(8,128)(2,1)}, u32[]{:S(2)}) copy-start(bf16[1,128,512]{2,1,0:T(8,128)(2,1)} %k_ref.1) | copy-start | bytes 393220
  14.9 0.9 %copy-start.3 = (bf16[1,128,512]{2,1,0:T(8,128)(2,1)S(1)}, bf16[1,128,512]{2,1,0:T(8,128)(2,1)}, u32[]{:S(2)}) copy-start(bf16[1,128,512]{2,1,0:T(8,128)(2,1)} %v_ref.1) | copy-start | bytes 393220
  19.4 1.2 %collective-permute-start.3 = (f32[16,128]{1,0:T(8,128)S(1)}, f32[16,128]{1,0:T(8,128)S(1)}, u32[]{:S(2)}, u32[]{:S(2)}) collective-permute-start(f32[16,128]{1,0:T(8,128)S(1)} %get-tuple-element.11), channel_id=1, source_target_pairs={{0,4},{4,0},{8,12},{12,8},{16,20},{20,16},{24,28},{28,24},{1,5},{5... | collective-permute-start | bytes 24584 | tf_op jit(solution)/shard_map/ppermute | solution.py:108
  20.6 3.7 %collective-permute-start.4 = (f32[16,128]{1,0:T(8,128)S(1)}, f32[16,128]{1,0:T(8,128)S(1)}, u32[]{:S(2)}, u32[]{:S(2)}) collective-permute-start(f32[16,128]{1,0:T(8,128)S(1)} %add.19), channel_id=1, source_target_pairs={{0,8},{4,12},{8,0},{12,4},{16,24},{20,28},{24,16},{28,20},{1,9},{5... | collective-permute-start | bytes 24584 | tf_op jit(solution)/shard_map/ppermute | solution.py:108
  24.2 3.7 %collective-permute-start.5 = (f32[16,128]{1,0:T(8,128)S(1)}, f32[16,128]{1,0:T(8,128)S(1)}, u32[]{:S(2)}, u32[]{:S(2)}) collective-permute-start(f32[16,128]{1,0:T(8,128)S(1)} %add.20), channel_id=1, source_target_pairs={{0,16},{4,20},{8,24},{12,28},{16,0},{20,4},{24,8},{28,12},{1,17},{... | collective-permute-start | bytes 24584 | tf_op jit(solution)/shard_map/ppermute | solution.py:108
  27.9 4.0 %collective-permute-start.6 = (f32[16,128]{1,0:T(8,128)S(1)}, f32[16,128]{1,0:T(8,128)S(1)}, u32[]{:S(2)}, u32[]{:S(2)}) collective-permute-start(f32[16,128]{1,0:T(8,128)S(1)} %add.21), channel_id=1, source_target_pairs={{0,1},{1,0},{2,3},{3,2},{4,5},{5,4},{6,7},{7,6},{8,9},{9,8},{10,11... | collective-permute-start | bytes 24584 | tf_op jit(solution)/shard_map/ppermute | solution.py:108
  31.9 4.8 %collective-permute-start.7 = (f32[16,128]{1,0:T(8,128)S(1)}, f32[16,128]{1,0:T(8,128)S(1)}, u32[]{:S(2)}, u32[]{:S(2)}) collective-permute-start(f32[16,128]{1,0:T(8,128)S(1)} %add.22), channel_id=1, source_target_pairs={{0,2},{1,3},{2,0},{3,1},{4,6},{5,7},{6,4},{7,5},{8,10},{9,11},{10,... | collective-permute-start | bytes 24584 | tf_op jit(solution)/shard_map/ppermute | solution.py:108
  34.9 8.3 %collective-permute-start.2 = (bf16[1,128,1024]{2,1,0:T(8,128)(2,1)S(1)}, bf16[1,128,1024]{2,1,0:T(8,128)(2,1)S(1)}, u32[]{:S(2)}, u32[]{:S(2)}) collective-permute-start(bf16[1,128,1024]{2,1,0:T(8,128)(2,1)S(1)} %get-tuple-element.10), channel_id=1, source_target_pairs={{1,0},{2,1},{3,2},{5,4},{6,5},{7,6},{9,8},{10,9},{11,10},{13,12},{... | collective-permute-start | bytes 786440 | tf_op jit(solution)/shard_map/ppermute | solution.py:22

commit v2 on v1

v2 whole, which is shorter than its diff:
```python
import functools

import jax
import jax.numpy as jnp
from jax import lax
from jax.experimental import pallas as pl
from jax.experimental.pallas import tpu as pltpu
from jax.sharding import PartitionSpec as P

HEADS = 16
KV_HEADS = 4
HEAD = 128
WINDOW = 128
GROUP = HEADS // KV_HEADS
SCALE = HEAD ** (-0.5)
LOG2E = 1.4426950408889634
VMEM = pl.BlockSpec(memory_space=pltpu.VMEM)
SMEM = pl.BlockSpec(memory_space=pltpu.SMEM)
HBM = pl.BlockSpec(memory_space=pltpu.HBM)


def dot(a, b, dims):
    return lax.dot_general(a, b, (dims, ((), ())), preferred_element_type=jnp.float32)


def struct(shape, dtype):
    return jax.ShapeDtypeStruct(shape, dtype)


def call(kernel, name, out_shape, in_specs, args, flops, scratch=()):
    args = [
        pltpu.with_memory_space_constraint(a, pltpu.HBM) if spec is HBM else a
        for a, spec in zip(args, in_specs, strict=True)
    ]
    moved = sum(a.size * a.dtype.itemsize for a in (*args, *out_shape))
    return pl.pallas_call(
        kernel,
        out_shape=out_shape,
        in_specs=in_specs,
        out_specs=(VMEM,) * len(out_shape),
        scratch_shapes=scratch,
        compiler_params=pltpu.CompilerParams(vmem_limit_bytes=32 * 1024 * 1024),
        cost_estimate=pl.CostEstimate(flops=flops, bytes_accessed=moved, transcendentals=0),
        name=name,
    )(*args)


def own_mask(rows, width):
    key_pos = lax.broadcasted_iota(jnp.int32, (rows, width), 0)
    query_pos = lax.rem(lax.broadcasted_iota(jnp.int32, (rows, width), 1), rows)
    return key_pos <= query_pos


def stacked(ref, b, heads):
    return jnp.concatenate([ref[b, :, h * HEAD:(h + 1) * HEAD] for h in heads], axis=0)


def split(own, value):
    zero = jnp.zeros_like(value)
    return jnp.concatenate(
        [jnp.where(own, value, zero), jnp.where(own, zero, value)], axis=0).astype(jnp.bfloat16)


def groups(ref):
    batch, rows, _ = ref.shape
    for b in range(batch):
        for g in range(KV_HEADS):
            heads = range(g * GROUP, (g + 1) * GROUP)
            yield b, heads, slice(g * HEAD, (g + 1) * HEAD), slice(g * GROUP * rows, (g + 1) * GROUP * rows)


def load_kernel(first_ref, sinks_in, q_in, k_in, v_in, do_in,
                q_ref, k_ref, v_ref, do_ref, s_ref, dp_ref, bias_ref, sink_ref, sinks_ref, sems):
    _, rows, _ = q_ref.shape
    copies = [
        pltpu.make_async_copy(source, target, sems.at[n])
        for n, (source, target) in enumerate(
            ((k_in, k_ref), (q_in, q_ref), (v_in, v_ref), (do_in, do_ref), (sinks_in, sinks_ref)))
    ]
    for copy in copies:
        copy.start()
    bias_ref[...] = jnp.full(bias_ref.shape, jnp.where(first_ref[0] == 1, -1e30, 0.0), jnp.float32)
    copies[0].wait()
    copies[1].wait()
    for b, heads, kv, cols in groups(q_ref):
        s_ref[b, :, cols] = dot(k_ref[b, :, kv], stacked(q_ref, b, heads), ((1,), (1,)))
    copies[2].wait()
    copies[3].wait()
    for b, heads, kv, cols in groups(q_ref):
        dp_ref[b, :, cols] = dot(v_ref[b, :, kv], stacked(do_ref, b, heads), ((1,), (1,)))
    copies[4].wait()
    for h in range(HEADS):
        sink_ref[:, h * rows:(h + 1) * rows] = jnp.full((1, rows), sinks_ref[h] * LOG2E, jnp.float32)


def softmax_kernel(bias_ref, sink_ref, q_ref, hk_ref, s_ref, p_ref, sp_ref):
    _, rows, _ = q_ref.shape
    own = own_mask(rows, GROUP * rows)
    for b, heads, kv, cols in groups(q_ref):
        before = dot(hk_ref[b, :, kv], stacked(q_ref, b, heads), ((1,), (1,))) + bias_ref[...]
        score = jnp.where(own, s_ref[b, :, cols], before) * (SCALE * LOG2E)
        sink = sink_ref[:, cols]
        top = jnp.maximum(jnp.max(score, axis=0, keepdims=True), sink)
        weight = jnp.exp2(score - top)
        sink_weight = jnp.exp2(sink - top)
        scale = 1.0 / (jnp.sum(weight, axis=0, keepdims=True) + sink_weight)
        p_ref[b, :, cols] = weight * scale
        sp_ref[b, :, cols] = sink_weight * scale


def sink_kernel(do_ref, hv_ref, p_ref, sp_ref, dp_ref, gp_ref, delta_ref, sink_ref):
    _, rows, _ = do_ref.shape
    own = own_mask(rows, GROUP * rows)
    for b, heads, kv, cols in groups(do_ref):
        before = dot(hv_ref[b, :, kv], stacked(do_ref, b, heads), ((1,), (1,)))
        grad_prob = jnp.where(own, dp_ref[b, :, cols], before)
        gp_ref[b, :, cols] = grad_prob
        delta = jnp.sum(p_ref[b, :, cols] * grad_prob, axis=0, keepdims=True)
        delta_ref[b, :, cols] = delta
        terms = sp_ref[b, :, cols] * delta
        for n, h in enumerate(heads):
            term = terms[:, n * rows:(n + 1) * rows]
            if b == 0:
                sink_ref[h:h + 1, :] = term
            else:
                sink_ref[h:h + 1, :] += term


def grad_kernel(q_ref, do_ref, k_ref, hk_ref, p_ref, gp_ref, delta_ref, dq_ref, own_ref, back_ref):
    _, rows, _ = q_ref.shape
    width = KV_HEADS * HEAD
    own = own_mask(rows, GROUP * rows)
    for b, heads, kv, cols in groups(q_ref):
        prob = p_ref[b, :, cols]
        dscores = split(own, prob * (gp_ref[b, :, cols] - delta_ref[b, :, cols]))
        grad_key = dot(dscores, stacked(q_ref, b, heads), ((1,), (0,))) * SCALE
        grad_value = dot(split(own, prob), stacked(do_ref, b, heads), ((1,), (0,)))
        vcol = slice(width + kv.start, width + kv.stop)
        own_ref[b, :, kv] = grad_key[:rows]
        own_ref[b, :, vcol] = grad_value[:rows]
        back_ref[b, :, kv] = grad_key[rows:].astype(jnp.bfloat16)
        back_ref[b, :, vcol] = grad_value[rows:].astype(jnp.bfloat16)
        key = jnp.concatenate([k_ref[b, :, kv], hk_ref[b, :, kv]], axis=0)
        grad_query = (dot(dscores, key, ((0,), (0,))) * SCALE).astype(jnp.bfloat16)
        for n, h in enumerate(heads):
            dq_ref[b, :, h * HEAD:(h + 1) * HEAD] = grad_query[n * rows:(n + 1) * rows]


def finish_kernel(factor, own_ref, back_ref, total_ref, other_ref, dk_ref, dv_ref, sink_ref):
    width = dk_ref.shape[2]
    joined = (own_ref[...] + back_ref[...].astype(jnp.float32)).astype(jnp.bfloat16)
    dk_ref[...] = joined[:, :, :width]
    dv_ref[...] = joined[:, :, width:]
    total = total_ref[...] + other_ref[...]
    ones = jnp.ones((8, total.shape[1]), jnp.float32)
    sums = lax.dot_general(ones, total, (((1,), (1,)), ((), ())), precision=lax.Precision.HIGHEST,
                           preferred_element_type=jnp.float32)
    sink_ref[...] = sums[:1] * factor


def ring(value, axis, steps):
    count = lax.axis_size(axis)
    return lax.ppermute(value, axis, [(i, (i + steps) % count) for i in range(count)])


def exchange(value, over, across):
    dp, ctx = lax.axis_size("dp"), lax.axis_size("ctx")
    pairs = [(d * ctx + c, (d ^ over) * ctx + (c ^ across)) for d in range(dp) for c in range(ctx)]
    return lax.ppermute(value, ("dp", "ctx"), pairs)


def total_steps():
    dp, ctx = lax.axis_size("dp"), lax.axis_size("ctx")
    over = [1 << n for n in range(dp.bit_length() - 1)]
    across = [1 << n for n in range(ctx.bit_length() - 1)]
    cross = over[0] if over else 0
    return ([(over[0], 0)] if over else []) + [(cross, a) for a in reversed(across)] + [
        (cross | o, 0) for o in over[1:]]


def body(queries, keys, values, dout, sinks):
    batch, rows, width = queries.shape
    kv_width = keys.shape[2]
    dp, ctx = lax.axis_size("dp"), lax.axis_size("ctx")
    assert rows == WINDOW and dp & (dp - 1) == 0 and ctx & (ctx - 1) == 0
    bf16, f32 = jnp.bfloat16, jnp.float32
    square = struct((batch, rows, HEADS * rows), f32)
    line = struct((batch, 1, HEADS * rows), f32)
    kv_bf16 = struct((batch, rows, kv_width), bf16)
    product = 2 * batch * HEADS * rows * rows * HEAD

    first = (lax.axis_index("ctx") == 0).astype(jnp.int32).reshape(1)
    halo_keys = ring(keys, "ctx", 1)
    halo_values = ring(values, "ctx", 1)
    q, k, v, do, score, grad_prob, bias, sink = call(
        load_kernel, "load",
        (struct(queries.shape, bf16), kv_bf16, kv_bf16, struct(dout.shape, bf16), square, square,
         struct((1, GROUP * rows), f32), struct((1, HEADS * rows), f32)),
        [SMEM] + [HBM] * 5, (first, sinks, queries, keys, values, dout), 2 * product,
        scratch=[pltpu.SMEM((HEADS,), f32), pltpu.SemaphoreType.DMA((5,))])
    prob, sink_prob = call(
        softmax_kernel, "softmax", (square, line),
        [VMEM] * 5, (bias, sink, q, halo_keys, score), product)
    grad_prob, delta, total = call(
        sink_kernel, "sink", (square, line, struct((HEADS, rows), f32)),
        [VMEM] * 5, (do, halo_values, prob, sink_prob, grad_prob), product)
    grad_query, own, back = call(
        grad_kernel, "grad",
        (struct(queries.shape, bf16), struct((batch, rows, 2 * kv_width), f32),
         struct((batch, rows, 2 * kv_width), bf16)),
        [VMEM] * 7, (q, do, k, halo_keys, prob, grad_prob, delta), 6 * product)
    back = ring(back, "ctx", -1)
    *steps, last = total_steps()
    for over, across in steps:
        total = total + exchange(total, over, across)
    other = exchange(total, *last)
    factor = -1.0 / (dp * batch * ctx * rows) ** 0.5
    grad_keys, grad_values, sink_grad = call(
        functools.partial(finish_kernel, factor), "finish",
        (kv_bf16, kv_bf16, struct((1, HEADS), f32)),
        [VMEM] * 4, (own, back, total, other), 0)
    return grad_query, grad_keys, grad_values, sink_grad.reshape(HEADS)


def solution(mesh):
    whole = P("dp", "ctx", None)
    return jax.shard_map(
        body,
        mesh=mesh,
        in_specs=(whole, whole, whole, whole, P()),
        out_specs=(whole, whole, whole, P()),
        check_vma=False,
    )
```

time: 44.2 us -> 31.6 us (0.71)
  starting transfers between devices: 18.1 us -> 9.35 us
  local copies, waits for them, and re-layouts: 4.61 us -> 0 us
  Pallas kernels: 3.62 us -> 6 us
  waiting for transfers between devices: 16.2 us -> 15.4 us
  other arithmetic: 0.71 us -> 0.01 us
    ppermute x8, starting transfers between devices: 18.1 us -> 9.35 us  [the longest x3 6.39 us: ring(): lax.ppermute(value, axis, [(i, (i + steps) % count) for i in range(count)])]
    unnamed x10 -> x0, local copies, waits for them, and re-layouts: 3.89 us -> none
    pallas_call x1 -> x5, Pallas kernels: 3.62 us -> 6 us  [call(): pl.pallas_call(kernel, out_shape=out_shape, in_specs=in_specs, out_specs=...]
    ppermute x8, waiting for transfers between devices: 16.2 us -> 15.4 us  [the longest x5 11.5 us: exchange(): return lax.ppermute(value, ('dp', 'ctx'), pairs)]
    slice x1 -> x0, local copies, waits for them, and re-layouts: 0.72 us -> none  [body(): joined[:, :, kv_width:]]
    div x1 -> x0, other arithmetic: 0.52 us -> none  [body(): sink_grad = -jnp.sum(total, axis=1) / jnp.sqrt(jnp.float32(positions))]
  transfers between devices with their start and end apart: 8 -> 8, of which waited for: 7 -> 7; matrix products, arithmetic and copies ran while one was open for 1% -> 0% of each run, Pallas kernels for 0% -> 10%
where the time goes in v2:
time: 31.6 us; the launch traced here: 31.4 us
  waiting for transfers between devices  15.4 us (49%)
  starting transfers between devices  9.35 us (30%)
  Pallas kernels  6 us (19%)
  between operations  0.66 us (2%)
    ppermute x5, waiting for transfers between devices, exchange(): return lax.ppermute(value, ('dp', 'ctx'), pairs)  11.5 us
    ppermute x3, starting transfers between devices, ring(): lax.ppermute(value, axis, [(i, (i + steps) % count) for i in range(count)])  6.39 us
    pallas_call x5, Pallas kernels, call(): pl.pallas_call(kernel, out_shape=out_shape, in_specs=in_specs, out_specs=...  6 us
    ppermute x3, waiting for transfers between devices, ring(): lax.ppermute(value, axis, [(i, (i + steps) % count) for i in range(count)])  3.89 us
    ppermute x5, starting transfers between devices, exchange(): return lax.ppermute(value, ('dp', 'ctx'), pairs)  2.96 us
  transfers between devices with their start and end apart: 8, of which 7 were waited for; matrix products, arithmetic and copies ran while one was open for 0% of the time, Pallas kernels for 10%

profile of v2, /device:TPU:0, one launch (start us, length us, event | category | flops | bytes accessed | tf_op | source)
XLA Modules:
  0.0 31.4 jit_solution(14703180077805847440)
XLA Ops:
  0.6 3.1 %collective-permute-start = (bf16[1,128,512]{2,1,0:T(8,128)(2,1)}, bf16[1,128,512]{2,1,0:T(8,128)(2,1)S(1)}, u32[]{:S(2)}, u32[]{:S(2)}) collective-permute-start(bf16[1,128,512]{2,1,0:T(8,128)(2,1)} %k_in.1), channel_id=1, source_target_pairs={{0,1},{1,2},{2,3},{3,0},{4,5},{5,6},{6,7},{7,4},{8,9},{9,10},{10,1... | collective-permute-start | bytes 393224 | tf_op jit(solution)/shard_map/ppermute | solution.py:163
  3.7 1.6 %collective-permute-start.1 = (bf16[1,128,512]{2,1,0:T(8,128)(2,1)}, bf16[1,128,512]{2,1,0:T(8,128)(2,1)S(1)}, u32[]{:S(2)}, u32[]{:S(2)}) collective-permute-start(bf16[1,128,512]{2,1,0:T(8,128)(2,1)} %v_in.1), channel_id=1, source_target_pairs={{0,1},{1,2},{2,3},{3,0},{4,5},{5,6},{6,7},{7,4},{8,9},{9,10},{10,1... | collective-permute-start | bytes 393224 | tf_op jit(solution)/shard_map/ppermute | solution.py:163
  5.3 2.4 %load.1 = (bf16[1,128,2048]{2,1,0:T(8,128)(2,1)S(1)}, bf16[1,128,512]{2,1,0:T(8,128)(2,1)S(1)}, bf16[1,128,512]{2,1,0:T(8,128)(2,1)}, bf16[1,128,2048]{2,1,0:T(8...) custom-call(s32[1]{0:T(128)} %bitcast.first_ref, ...), custom_call_target="tpu_custom_call" | custom-call | flops 134217728 | bytes 4728900 | tf_op jit(solution)/shard_map/load/pallas_call | solution.py:36
  7.7 2.5 %collective-permute-done.hk_ref = bf16[1,128,512]{2,1,0:T(8,128)(2,1)S(1)} collective-permute-done((bf16[1,128,512]{2,1,0:T(8,128)(2,1)}, bf16[1,128,512]{2,1,0:T(8,128)(2,1)S(1)}, u32[]{:S(2)}, u32[]{:S(2)}) %collective-permute-start) | collective-permute-done | bytes 131104 | tf_op jit(solution)/shard_map/ppermute | solution.py:163
  10.3 0.6 %softmax.1 = (f32[1,128,2048]{2,1,0:T(8,128)S(1)}, f32[1,1,2048]{2,1,0:T(1,128)S(1)}) custom-call(f32[1,512]{1,0:T(1,128)S(1)} %get-tuple-element.25.bias_ref, f32[1,2048]{1,0:T(1,128)S(1)} %get-tuple-element.26.sink_ref, bf16[1,128,2048]{2,1,0:T(8,128)(2,1)S(1)} %get-tuple-element.22.q_ref, bf16[1,128,512]{2,1,0:T(8,128)(2,1)S(1)} %collective-permute-done.hk_ref, ...), custom_call_target="tpu_custom_call" | custom-call | flops 67108864 | bytes 2770944 | tf_op jit(solution)/shard_map/softmax/pallas_call | solution.py:36
  10.9 1.4 %collective-permute-done.1.hv_ref = bf16[1,128,512]{2,1,0:T(8,128)(2,1)S(1)} collective-permute-done((bf16[1,128,512]{2,1,0:T(8,128)(2,1)}, bf16[1,128,512]{2,1,0:T(8,128)(2,1)S(1)}, u32[]{:S(2)}, u32[]{:S(2)}) %collective-permute-start.1) | collective-permute-done | bytes 131104 | tf_op jit(solution)/shard_map/ppermute | solution.py:163
  12.2 0.4 %sink.1 = (f32[1,128,2048]{2,1,0:T(8,128)S(1)}, f32[1,1,2048]{2,1,0:T(1,128)S(1)}, f32[16,128]{1,0:T(8,128)S(1)}) custom-call(bf16[1,128,2048]{2,1,0:T(8,128)(2,1)S(1)} %get-tuple-element.23.do_ref, bf16[1,128,512]{2,1,0:T(8,128)(2,1)S(1)} %collective-permute-done.1.hv_ref, f32[1,128,2048]{2,1,0:T(8,128)S(1)} %get-tuple-element.28.p_ref, ...), custom_call_target="tpu_custom_call" | custom-call | flops 67108864 | bytes 3825664 | tf_op jit(solution)/shard_map/sink/pallas_call | solution.py:36
  12.6 1.8 %grad.1 = (bf16[1,128,2048]{2,1,0:T(8,128)(2,1)}, f32[1,128,1024]{2,1,0:T(8,128)S(1)}, bf16[1,128,1024]{2,1,0:T(8,128)(2,1)S(1)}) custom-call(bf16[1,128,2048]{2,1,0:T(8,128)(2,1)S(1)} %get-tuple-element.22.q_ref, bf16[1,128,2048]{2,1,0:T(8,128)(2,1)S(1)} %get-tuple-element.23.do_ref, bf16[1,128,512]{2,1,0:T(8,128)(2,1)S(1)} %get-tuple-element.24.k_ref, ...), custom_call_target="tpu_custom_call" | custom-call | flops 402653184 | bytes 4726784 | tf_op jit(solution)/shard_map/grad/pallas_call | solution.py:36
  14.4 1.7 %collective-permute-start.2 = (bf16[1,128,1024]{2,1,0:T(8,128)(2,1)S(1)}, bf16[1,128,1024]{2,1,0:T(8,128)(2,1)S(1)}, u32[]{:S(2)}, u32[]{:S(2)}) collective-permute-start(bf16[1,128,1024]{2,1,0:T(8,128)(2,1)S(1)} %get-tuple-element.35), channel_id=1, source_target_pairs={{0,3},{1,0},{2,1},{3,2},{4,7},{5,4},{6,5},{7,6},{8,11},{9,8},{10,9... | collective-permute-start | bytes 786440 | tf_op jit(solution)/shard_map/ppermute | solution.py:163
  16.2 0.0 collective-permute-start.3
  16.2 1.2 %collective-permute-done.3 = f32[16,128]{1,0:T(8,128)S(1)} collective-permute-done((f32[16,128]{1,0:T(8,128)S(1)}, f32[16,128]{1,0:T(8,128)S(1)}, u32[]{:S(2)}, u32[]{:S(2)}) %collective-permute-start.3) | collective-permute-done | bytes 8224 | tf_op jit(solution)/shard_map/ppermute | solution.py:169
  17.4 0.0 collective-permute-start.4
  17.4 4.1 %collective-permute-done.4 = f32[16,128]{1,0:T(8,128)S(1)} collective-permute-done((f32[16,128]{1,0:T(8,128)S(1)}, f32[16,128]{1,0:T(8,128)S(1)}, u32[]{:S(2)}, u32[]{:S(2)}) %collective-permute-start.4) | collective-permute-done | bytes 8224 | tf_op jit(solution)/shard_map/ppermute | solution.py:169
  21.5 0.5 %collective-permute-start.5 = (f32[16,128]{1,0:T(8,128)S(1)}, f32[16,128]{1,0:T(8,128)S(1)}, u32[]{:S(2)}, u32[]{:S(2)}) collective-permute-start(f32[16,128]{1,0:T(8,128)S(1)} %add.13), channel_id=1, source_target_pairs={{0,5},{1,4},{2,7},{3,6},{4,1},{5,0},{6,3},{7,2},{8,13},{9,12},{10,... | collective-permute-start | bytes 24584 | tf_op jit(solution)/shard_map/ppermute | solution.py:169
  22.0 2.6 %collective-permute-done.5 = f32[16,128]{1,0:T(8,128)S(1)} collective-permute-done((f32[16,128]{1,0:T(8,128)S(1)}, f32[16,128]{1,0:T(8,128)S(1)}, u32[]{:S(2)}, u32[]{:S(2)}) %collective-permute-start.5) | collective-permute-done | bytes 8224 | tf_op jit(solution)/shard_map/ppermute | solution.py:169
  24.5 1.2 %collective-permute-start.6 = (f32[16,128]{1,0:T(8,128)S(1)}, f32[16,128]{1,0:T(8,128)S(1)}, u32[]{:S(2)}, u32[]{:S(2)}) collective-permute-start(f32[16,128]{1,0:T(8,128)S(1)} %add.14), channel_id=1, source_target_pairs={{0,12},{1,13},{2,14},{3,15},{4,8},{5,9},{6,10},{7,11},{8,4},{9,5},... | collective-permute-start | bytes 24584 | tf_op jit(solution)/shard_map/ppermute | solution.py:169
  25.7 1.9 %collective-permute-done.6 = f32[16,128]{1,0:T(8,128)S(1)} collective-permute-done((f32[16,128]{1,0:T(8,128)S(1)}, f32[16,128]{1,0:T(8,128)S(1)}, u32[]{:S(2)}, u32[]{:S(2)}) %collective-permute-start.6) | collective-permute-done | bytes 8224 | tf_op jit(solution)/shard_map/ppermute | solution.py:169
  27.6 1.2 %collective-permute-start.7 = (f32[16,128]{1,0:T(8,128)S(1)}, f32[16,128]{1,0:T(8,128)S(1)}, u32[]{:S(2)}, u32[]{:S(2)}) collective-permute-start(f32[16,128]{1,0:T(8,128)S(1)} %add.15.total_ref), channel_id=1, source_target_pairs={{0,20},{1,21},{2,22},{3,23},{4,16},{5,17},{6,18},{7,19},{8,28},{9,... | collective-permute-start | bytes 24584 | tf_op jit(solution)/shard_map/ppermute | solution.py:169
  28.9 1.8 %collective-permute-done.7.other_ref = f32[16,128]{1,0:T(8,128)S(1)} collective-permute-done((f32[16,128]{1,0:T(8,128)S(1)}, f32[16,128]{1,0:T(8,128)S(1)}, u32[]{:S(2)}, u32[]{:S(2)}) %collective-permute-start.7) | collective-permute-done | bytes 8224 | tf_op jit(solution)/shard_map/ppermute | solution.py:169
  30.7 0.0 collective-permute-done.2.back_ref
  30.7 0.7 %finish.1 = (bf16[1,128,512]{2,1,0:T(8,128)(2,1)}, bf16[1,128,512]{2,1,0:T(8,128)(2,1)}, f32[1,16]{1,0:T(1,128)}) custom-call(f32[1,128,1024]{2,1,0:T(8,128)S(1)} %get-tuple-element.34.own_ref, bf16[1,128,1024]{2,1,0:T(8,128)(2,1)S(1)} %collective-permute-done.2.back_ref, f32[16,128]{1,0:T(8,128)S(1)} %add.15.total_ref, ...), custom_call_target="tpu_custom_call" | custom-call | bytes 1065024 | tf_op jit(solution)/shard_map/finish/pallas_call | solution.py:36
  (4 shorter events, 0.0 us)
Async XLA Ops:
  0.6 9.6 %collective-permute-start = (bf16[1,128,512]{2,1,0:T(8,128)(2,1)}, bf16[1,128,512]{2,1,0:T(8,128)(2,1)S(1)}, u32[]{:S(2)}, u32[]{:S(2)}) collective-permute-start(bf16[1,128,512]{2,1,0:T(8,128)(2,1)} %k_in.1), channel_id=1, source_target_pairs={{0,1},{1,2},{2,3},{3,0},{4,5},{5,6},{6,7},{7,4},{8,9},{9,10},{10,1... | collective-permute-start | bytes 393224 | tf_op jit(solution)/shard_map/ppermute | solution.py:163
  3.7 8.5 %collective-permute-start.1 = (bf16[1,128,512]{2,1,0:T(8,128)(2,1)}, bf16[1,128,512]{2,1,0:T(8,128)(2,1)S(1)}, u32[]{:S(2)}, u32[]{:S(2)}) collective-permute-start(bf16[1,128,512]{2,1,0:T(8,128)(2,1)} %v_in.1), channel_id=1, source_target_pairs={{0,1},{1,2},{2,3},{3,0},{4,5},{5,6},{6,7},{7,4},{8,9},{9,10},{10,1... | collective-permute-start | bytes 393224 | tf_op jit(solution)/shard_map/ppermute | solution.py:163
  14.4 16.2 %collective-permute-start.2 = (bf16[1,128,1024]{2,1,0:T(8,128)(2,1)S(1)}, bf16[1,128,1024]{2,1,0:T(8,128)(2,1)S(1)}, u32[]{:S(2)}, u32[]{:S(2)}) collective-permute-start(bf16[1,128,1024]{2,1,0:T(8,128)(2,1)S(1)} %get-tuple-element.35), channel_id=1, source_target_pairs={{0,3},{1,0},{2,1},{3,2},{4,7},{5,4},{6,5},{7,6},{8,11},{9,8},{10,9... | collective-permute-start | bytes 786440 | tf_op jit(solution)/shard_map/ppermute | solution.py:163
  16.2 1.2 %collective-permute-start.3 = (f32[16,128]{1,0:T(8,128)S(1)}, f32[16,128]{1,0:T(8,128)S(1)}, u32[]{:S(2)}, u32[]{:S(2)}) collective-permute-start(f32[16,128]{1,0:T(8,128)S(1)} %get-tuple-element.36), channel_id=1, source_target_pairs={{0,4},{1,5},{2,6},{3,7},{4,0},{5,1},{6,2},{7,3},{8,12},{9,13},{10,... | collective-permute-start | bytes 24584 | tf_op jit(solution)/shard_map/ppermute | solution.py:169
  17.4 4.1 %collective-permute-start.4 = (f32[16,128]{1,0:T(8,128)S(1)}, f32[16,128]{1,0:T(8,128)S(1)}, u32[]{:S(2)}, u32[]{:S(2)}) collective-permute-start(f32[16,128]{1,0:T(8,128)S(1)} %add.12), channel_id=1, source_target_pairs={{0,6},{1,7},{2,4},{3,5},{4,2},{5,3},{6,0},{7,1},{8,14},{9,15},{10,... | collective-permute-start | bytes 24584 | tf_op jit(solution)/shard_map/ppermute | solution.py:169
  21.5 3.1 %collective-permute-start.5 = (f32[16,128]{1,0:T(8,128)S(1)}, f32[16,128]{1,0:T(8,128)S(1)}, u32[]{:S(2)}, u32[]{:S(2)}) collective-permute-start(f32[16,128]{1,0:T(8,128)S(1)} %add.13), channel_id=1, source_target_pairs={{0,5},{1,4},{2,7},{3,6},{4,1},{5,0},{6,3},{7,2},{8,13},{9,12},{10,... | collective-permute-start | bytes 24584 | tf_op jit(solution)/shard_map/ppermute | solution.py:169
  24.5 3.1 %collective-permute-start.6 = (f32[16,128]{1,0:T(8,128)S(1)}, f32[16,128]{1,0:T(8,128)S(1)}, u32[]{:S(2)}, u32[]{:S(2)}) collective-permute-start(f32[16,128]{1,0:T(8,128)S(1)} %add.14), channel_id=1, source_target_pairs={{0,12},{1,13},{2,14},{3,15},{4,8},{5,9},{6,10},{7,11},{8,4},{9,5},... | collective-permute-start | bytes 24584 | tf_op jit(solution)/shard_map/ppermute | solution.py:169
  27.6 3.1 %collective-permute-start.7 = (f32[16,128]{1,0:T(8,128)S(1)}, f32[16,128]{1,0:T(8,128)S(1)}, u32[]{:S(2)}, u32[]{:S(2)}) collective-permute-start(f32[16,128]{1,0:T(8,128)S(1)} %add.15.total_ref), channel_id=1, source_target_pairs={{0,20},{1,21},{2,22},{3,23},{4,16},{5,17},{6,18},{7,19},{8,28},{9,... | collective-permute-start | bytes 24584 | tf_op jit(solution)/shard_map/ppermute | solution.py:169

commit v3 on v2

--- a/solution.py
+++ b/solution.py
@@ -16,6 +16,7 @@
 LOG2E = 1.4426950408889634
 VMEM = pl.BlockSpec(memory_space=pltpu.VMEM)
 SMEM = pl.BlockSpec(memory_space=pltpu.SMEM)
+ANY = pl.BlockSpec(memory_space=pl.ANY)
 HBM = pl.BlockSpec(memory_space=pltpu.HBM)
 
 
@@ -144,6 +145,10 @@
         grad_query = (dot(dscores, key, ((0,), (0,))) * SCALE).astype(jnp.bfloat16)
         for n, h in enumerate(heads):
             dq_ref[b, :, h * HEAD:(h + 1) * HEAD] = grad_query[n * rows:(n + 1) * rows]
+
+
+def add_kernel(a_ref, b_ref, *refs):
+    refs[-1][...] = a_ref[...] + b_ref[...]
 
 
 def finish_kernel(factor, own_ref, back_ref, total_ref, other_ref, dk_ref, dv_ref, sink_ref):
@@ -209,10 +214,17 @@
         (struct(queries.shape, bf16), struct((batch, rows, 2 * kv_width), f32),
          struct((batch, rows, 2 * kv_width), bf16)),
         [VMEM] * 7, (q, do, k, halo_keys, prob, grad_prob, delta), 6 * product)
+    token = back
     back = ring(back, "ctx", -1)
     *steps, last = total_steps()
-    for over, across in steps:
-        total = total + exchange(total, over, across)
+    for n, (over, across) in enumerate(steps):
+        received = exchange(total, over, across)
+        if n == 1:
+            total, = call(add_kernel, "add", (struct(total.shape, f32),), [VMEM] * 2 + [ANY], (total, received, token), 0)
+        elif n == 2:
+            total, = call(add_kernel, "add", (struct(total.shape, f32),), [VMEM] * 2, (total, received), 10 ** 10)
+        else:
+            total = total + received
     other = exchange(total, *last)
     factor = -1.0 / (dp * batch * ctx * rows) ** 0.5
     grad_keys, grad_values, sink_grad = call(

time: 31.6 us -> 28 us (0.89)
  waiting for transfers between devices: 15.4 us -> 11.1 us
  starting transfers between devices: 9.35 us -> 10.1 us
    ppermute x5, waiting for transfers between devices: 11.5 us -> 7.19 us  [exchange(): return lax.ppermute(value, ('dp', 'ctx'), pairs)]
    ppermute x5, starting transfers between devices: 2.96 us -> 3.43 us  [exchange(): return lax.ppermute(value, ('dp', 'ctx'), pairs)]
    pallas_call x5 -> x7, Pallas kernels: 6 us -> 6.01 us  [call(): pl.pallas_call(kernel, out_shape=out_shape, in_specs=in_specs, out_specs=...]
  transfers between devices with their start and end apart: 8 -> 8, of which waited for: 7 -> 7; matrix products, arithmetic and copies ran while one was open for 0% -> 0% of each run, Pallas kernels for 10% -> 18%
where the time goes in v3:
time: 28 us; the launch traced here: 27.8 us
  waiting for transfers between devices  11.1 us (40%)
  starting transfers between devices  10.1 us (36%)
  Pallas kernels  6.01 us (21%)
  between operations  0.67 us (2%)
    ppermute x5, waiting for transfers between devices, exchange(): return lax.ppermute(value, ('dp', 'ctx'), pairs)  7.19 us
    ppermute x3, starting transfers between devices, ring(): lax.ppermute(value, axis, [(i, (i + steps) % count) for i in range(count)])  6.63 us
    pallas_call x7, Pallas kernels, call(): pl.pallas_call(kernel, out_shape=out_shape, in_specs=in_specs, out_specs=...  6.01 us
    ppermute x3, waiting for transfers between devices, ring(): lax.ppermute(value, axis, [(i, (i + steps) % count) for i in range(count)])  3.89 us
    ppermute x5, starting transfers between devices, exchange(): return lax.ppermute(value, ('dp', 'ctx'), pairs)  3.43 us
  transfers between devices with their start and end apart: 8, of which 7 were waited for; matrix products, arithmetic and copies ran while one was open for 0% of the time, Pallas kernels for 18%

profile of v3, /device:TPU:0, one launch (start us, length us, event | category | flops | bytes accessed | tf_op | source)
XLA Modules:
  0.0 27.8 jit_solution(13142432302846650006)
XLA Ops:
  0.6 3.1 %collective-permute-start = (bf16[1,128,512]{2,1,0:T(8,128)(2,1)}, bf16[1,128,512]{2,1,0:T(8,128)(2,1)S(1)}, u32[]{:S(2)}, u32[]{:S(2)}) collective-permute-start(bf16[1,128,512]{2,1,0:T(8,128)(2,1)} %k_in.1), channel_id=1, source_target_pairs={{0,1},{1,2},{2,3},{3,0},{4,5},{5,6},{6,7},{7,4},{8,9},{9,10},{10,1... | collective-permute-start | bytes 393224 | tf_op jit(solution)/shard_map/ppermute | solution.py:168
  3.7 1.6 %collective-permute-start.1 = (bf16[1,128,512]{2,1,0:T(8,128)(2,1)}, bf16[1,128,512]{2,1,0:T(8,128)(2,1)S(1)}, u32[]{:S(2)}, u32[]{:S(2)}) collective-permute-start(bf16[1,128,512]{2,1,0:T(8,128)(2,1)} %v_in.1), channel_id=1, source_target_pairs={{0,1},{1,2},{2,3},{3,0},{4,5},{5,6},{6,7},{7,4},{8,9},{9,10},{10,1... | collective-permute-start | bytes 393224 | tf_op jit(solution)/shard_map/ppermute | solution.py:168
  5.3 2.4 %load.1 = (bf16[1,128,2048]{2,1,0:T(8,128)(2,1)S(1)}, bf16[1,128,512]{2,1,0:T(8,128)(2,1)S(1)}, bf16[1,128,512]{2,1,0:T(8,128)(2,1)}, bf16[1,128,2048]{2,1,0:T(8...) custom-call(s32[1]{0:T(128)} %bitcast.first_ref, ...), custom_call_target="tpu_custom_call" | custom-call | flops 134217728 | bytes 4728900 | tf_op jit(solution)/shard_map/load/pallas_call | solution.py:37
  7.7 2.5 %collective-permute-done.hk_ref = bf16[1,128,512]{2,1,0:T(8,128)(2,1)S(1)} collective-permute-done((bf16[1,128,512]{2,1,0:T(8,128)(2,1)}, bf16[1,128,512]{2,1,0:T(8,128)(2,1)S(1)}, u32[]{:S(2)}, u32[]{:S(2)}) %collective-permute-start) | collective-permute-done | bytes 131104 | tf_op jit(solution)/shard_map/ppermute | solution.py:168
  10.3 0.6 %softmax.1 = (f32[1,128,2048]{2,1,0:T(8,128)S(1)}, f32[1,1,2048]{2,1,0:T(1,128)S(1)}) custom-call(f32[1,512]{1,0:T(1,128)S(1)} %get-tuple-element.25.bias_ref, f32[1,2048]{1,0:T(1,128)S(1)} %get-tuple-element.26.sink_ref, bf16[1,128,2048]{2,1,0:T(8,128)(2,1)S(1)} %get-tuple-element.22.q_ref, bf16[1,128,512]{2,1,0:T(8,128)(2,1)S(1)} %collective-permute-done.hk_ref, ...), custom_call_target="tpu_custom_call" | custom-call | flops 67108864 | bytes 2770944 | tf_op jit(solution)/shard_map/softmax/pallas_call | solution.py:37
  10.9 1.4 %collective-permute-done.1.hv_ref = bf16[1,128,512]{2,1,0:T(8,128)(2,1)S(1)} collective-permute-done((bf16[1,128,512]{2,1,0:T(8,128)(2,1)}, bf16[1,128,512]{2,1,0:T(8,128)(2,1)S(1)}, u32[]{:S(2)}, u32[]{:S(2)}) %collective-permute-start.1) | collective-permute-done | bytes 131104 | tf_op jit(solution)/shard_map/ppermute | solution.py:168
  12.2 0.4 %sink.1 = (f32[1,128,2048]{2,1,0:T(8,128)S(1)}, f32[1,1,2048]{2,1,0:T(1,128)S(1)}, f32[16,128]{1,0:T(8,128)S(1)}) custom-call(bf16[1,128,2048]{2,1,0:T(8,128)(2,1)S(1)} %get-tuple-element.23.do_ref, bf16[1,128,512]{2,1,0:T(8,128)(2,1)S(1)} %collective-permute-done.1.hv_ref, f32[1,128,2048]{2,1,0:T(8,128)S(1)} %get-tuple-element.28.p_ref, ...), custom_call_target="tpu_custom_call" | custom-call | flops 67108864 | bytes 3825664 | tf_op jit(solution)/shard_map/sink/pallas_call | solution.py:37
  12.6 0.1 collective-permute-start.3
  12.7 1.2 %collective-permute-done.3 = f32[16,128]{1,0:T(8,128)S(1)} collective-permute-done((f32[16,128]{1,0:T(8,128)S(1)}, f32[16,128]{1,0:T(8,128)S(1)}, u32[]{:S(2)}, u32[]{:S(2)}) %collective-permute-start.3) | collective-permute-done | bytes 8224 | tf_op jit(solution)/shard_map/ppermute | solution.py:174
  13.9 0.5 %collective-permute-start.4 = (f32[16,128]{1,0:T(8,128)S(1)}, f32[16,128]{1,0:T(8,128)S(1)}, u32[]{:S(2)}, u32[]{:S(2)}) collective-permute-start(f32[16,128]{1,0:T(8,128)S(1)} %add.8.a_ref), channel_id=1, source_target_pairs={{0,6},{1,7},{2,4},{3,5},{4,2},{5,3},{6,0},{7,1},{8,14},{9,15},{10,... | collective-permute-start | bytes 24584 | tf_op jit(solution)/shard_map/ppermute | solution.py:174
  14.4 1.8 %grad.1 = (bf16[1,128,2048]{2,1,0:T(8,128)(2,1)}, f32[1,128,1024]{2,1,0:T(8,128)S(1)}, bf16[1,128,1024]{2,1,0:T(8,128)(2,1)S(1)}) custom-call(bf16[1,128,2048]{2,1,0:T(8,128)(2,1)S(1)} %get-tuple-element.22.q_ref, bf16[1,128,2048]{2,1,0:T(8,128)(2,1)S(1)} %get-tuple-element.23.do_ref, bf16[1,128,512]{2,1,0:T(8,128)(2,1)S(1)} %get-tuple-element.24.k_ref, ...), custom_call_target="tpu_custom_call" | custom-call | flops 402653184 | bytes 4726784 | tf_op jit(solution)/shard_map/grad/pallas_call | solution.py:37
  16.2 1.6 %collective-permute-done.4.b_ref = f32[16,128]{1,0:T(8,128)S(1)} collective-permute-done((f32[16,128]{1,0:T(8,128)S(1)}, f32[16,128]{1,0:T(8,128)S(1)}, u32[]{:S(2)}, u32[]{:S(2)}) %collective-permute-start.4) | collective-permute-done | bytes 8224 | tf_op jit(solution)/shard_map/ppermute | solution.py:174
  17.8 0.0 collective-permute-start.5
  17.8 2.0 %collective-permute-start.2 = (bf16[1,128,1024]{2,1,0:T(8,128)(2,1)S(1)}, bf16[1,128,1024]{2,1,0:T(8,128)(2,1)S(1)}, u32[]{:S(2)}, u32[]{:S(2)}) collective-permute-start(bf16[1,128,1024]{2,1,0:T(8,128)(2,1)S(1)} %get-tuple-element.35.refs_0_), channel_id=1, source_target_pairs={{0,3},{1,0},{2,1},{3,2},{4,7},{5,4},{6,5},{7,6},{8,11},{9,8},{10,9... | collective-permute-start | bytes 786440 | tf_op jit(solution)/shard_map/ppermute | solution.py:168
  19.8 1.1 %collective-permute-done.5.b_ref = f32[16,128]{1,0:T(8,128)S(1)} collective-permute-done((f32[16,128]{1,0:T(8,128)S(1)}, f32[16,128]{1,0:T(8,128)S(1)}, u32[]{:S(2)}, u32[]{:S(2)}) %collective-permute-start.5) | collective-permute-done | bytes 8224 | tf_op jit(solution)/shard_map/ppermute | solution.py:174
  20.9 1.3 %collective-permute-start.6 = (f32[16,128]{1,0:T(8,128)S(1)}, f32[16,128]{1,0:T(8,128)S(1)}, u32[]{:S(2)}, u32[]{:S(2)}) collective-permute-start(f32[16,128]{1,0:T(8,128)S(1)} %add.11), channel_id=1, source_target_pairs={{0,12},{1,13},{2,14},{3,15},{4,8},{5,9},{6,10},{7,11},{8,4},{9,5},... | collective-permute-start | bytes 24584 | tf_op jit(solution)/shard_map/ppermute | solution.py:174
  22.2 1.8 %collective-permute-done.6 = f32[16,128]{1,0:T(8,128)S(1)} collective-permute-done((f32[16,128]{1,0:T(8,128)S(1)}, f32[16,128]{1,0:T(8,128)S(1)}, u32[]{:S(2)}, u32[]{:S(2)}) %collective-permute-start.6) | collective-permute-done | bytes 8224 | tf_op jit(solution)/shard_map/ppermute | solution.py:174
  24.0 1.6 %collective-permute-start.7 = (f32[16,128]{1,0:T(8,128)S(1)}, f32[16,128]{1,0:T(8,128)S(1)}, u32[]{:S(2)}, u32[]{:S(2)}) collective-permute-start(f32[16,128]{1,0:T(8,128)S(1)} %add.9.total_ref), channel_id=1, source_target_pairs={{0,20},{1,21},{2,22},{3,23},{4,16},{5,17},{6,18},{7,19},{8,28},{9,... | collective-permute-start | bytes 24584 | tf_op jit(solution)/shard_map/ppermute | solution.py:174
  25.6 1.5 %collective-permute-done.7.other_ref = f32[16,128]{1,0:T(8,128)S(1)} collective-permute-done((f32[16,128]{1,0:T(8,128)S(1)}, f32[16,128]{1,0:T(8,128)S(1)}, u32[]{:S(2)}, u32[]{:S(2)}) %collective-permute-start.7) | collective-permute-done | bytes 8224 | tf_op jit(solution)/shard_map/ppermute | solution.py:174
  27.1 0.0 collective-permute-done.2.back_ref
  27.1 0.7 %finish.1 = (bf16[1,128,512]{2,1,0:T(8,128)(2,1)}, bf16[1,128,512]{2,1,0:T(8,128)(2,1)}, f32[1,16]{1,0:T(1,128)}) custom-call(f32[1,128,1024]{2,1,0:T(8,128)S(1)} %get-tuple-element.34.own_ref, bf16[1,128,1024]{2,1,0:T(8,128)(2,1)S(1)} %collective-permute-done.2.back_ref, f32[16,128]{1,0:T(8,128)S(1)} %add.9.total_ref, ...), custom_call_target="tpu_custom_call" | custom-call | bytes 1065024 | tf_op jit(solution)/shard_map/finish/pallas_call | solution.py:37
  (4 shorter events, 0.0 us)
Async XLA Ops:
  0.6 9.6 %collective-permute-start = (bf16[1,128,512]{2,1,0:T(8,128)(2,1)}, bf16[1,128,512]{2,1,0:T(8,128)(2,1)S(1)}, u32[]{:S(2)}, u32[]{:S(2)}) collective-permute-start(bf16[1,128,512]{2,1,0:T(8,128)(2,1)} %k_in.1), channel_id=1, source_target_pairs={{0,1},{1,2},{2,3},{3,0},{4,5},{5,6},{6,7},{7,4},{8,9},{9,10},{10,1... | collective-permute-start | bytes 393224 | tf_op jit(solution)/shard_map/ppermute | solution.py:168
  3.7 8.5 %collective-permute-start.1 = (bf16[1,128,512]{2,1,0:T(8,128)(2,1)}, bf16[1,128,512]{2,1,0:T(8,128)(2,1)S(1)}, u32[]{:S(2)}, u32[]{:S(2)}) collective-permute-start(bf16[1,128,512]{2,1,0:T(8,128)(2,1)} %v_in.1), channel_id=1, source_target_pairs={{0,1},{1,2},{2,3},{3,0},{4,5},{5,6},{6,7},{7,4},{8,9},{9,10},{10,1... | collective-permute-start | bytes 393224 | tf_op jit(solution)/shard_map/ppermute | solution.py:168
  12.6 1.2 %collective-permute-start.3 = (f32[16,128]{1,0:T(8,128)S(1)}, f32[16,128]{1,0:T(8,128)S(1)}, u32[]{:S(2)}, u32[]{:S(2)}) collective-permute-start(f32[16,128]{1,0:T(8,128)S(1)} %get-tuple-element.36), channel_id=1, source_target_pairs={{0,4},{1,5},{2,6},{3,7},{4,0},{5,1},{6,2},{7,3},{8,12},{9,13},{10,... | collective-permute-start | bytes 24584 | tf_op jit(solution)/shard_map/ppermute | solution.py:174
  13.9 4.0 %collective-permute-start.4 = (f32[16,128]{1,0:T(8,128)S(1)}, f32[16,128]{1,0:T(8,128)S(1)}, u32[]{:S(2)}, u32[]{:S(2)}) collective-permute-start(f32[16,128]{1,0:T(8,128)S(1)} %add.8.a_ref), channel_id=1, source_target_pairs={{0,6},{1,7},{2,4},{3,5},{4,2},{5,3},{6,0},{7,1},{8,14},{9,15},{10,... | collective-permute-start | bytes 24584 | tf_op jit(solution)/shard_map/ppermute | solution.py:174
  17.8 3.1 %collective-permute-start.5 = (f32[16,128]{1,0:T(8,128)S(1)}, f32[16,128]{1,0:T(8,128)S(1)}, u32[]{:S(2)}, u32[]{:S(2)}) collective-permute-start(f32[16,128]{1,0:T(8,128)S(1)} %add.10.a_ref), channel_id=1, source_target_pairs={{0,5},{1,4},{2,7},{3,6},{4,1},{5,0},{6,3},{7,2},{8,13},{9,12},{10,... | collective-permute-start | bytes 24584 | tf_op jit(solution)/shard_map/ppermute | solution.py:174
  17.8 9.2 %collective-permute-start.2 = (bf16[1,128,1024]{2,1,0:T(8,128)(2,1)S(1)}, bf16[1,128,1024]{2,1,0:T(8,128)(2,1)S(1)}, u32[]{:S(2)}, u32[]{:S(2)}) collective-permute-start(bf16[1,128,1024]{2,1,0:T(8,128)(2,1)S(1)} %get-tuple-element.35.refs_0_), channel_id=1, source_target_pairs={{0,3},{1,0},{2,1},{3,2},{4,7},{5,4},{6,5},{7,6},{8,11},{9,8},{10,9... | collective-permute-start | bytes 786440 | tf_op jit(solution)/shard_map/ppermute | solution.py:168
  20.9 3.1 %collective-permute-start.6 = (f32[16,128]{1,0:T(8,128)S(1)}, f32[16,128]{1,0:T(8,128)S(1)}, u32[]{:S(2)}, u32[]{:S(2)}) collective-permute-start(f32[16,128]{1,0:T(8,128)S(1)} %add.11), channel_id=1, source_target_pairs={{0,12},{1,13},{2,14},{3,15},{4,8},{5,9},{6,10},{7,11},{8,4},{9,5},... | collective-permute-start | bytes 24584 | tf_op jit(solution)/shard_map/ppermute | solution.py:174
  24.0 3.1 %collective-permute-start.7 = (f32[16,128]{1,0:T(8,128)S(1)}, f32[16,128]{1,0:T(8,128)S(1)}, u32[]{:S(2)}, u32[]{:S(2)}) collective-permute-start(f32[16,128]{1,0:T(8,128)S(1)} %add.9.total_ref), channel_id=1, source_target_pairs={{0,20},{1,21},{2,22},{3,23},{4,16},{5,17},{6,18},{7,19},{8,28},{9,... | collective-permute-start | bytes 24584 | tf_op jit(solution)/shard_map/ppermute | solution.py:174

commit v4 on v2

v4 whole, which is shorter than its diff:
```python
import functools
import math

import jax
import jax.numpy as jnp
from jax import lax
from jax.experimental import pallas as pl
from jax.experimental.pallas import tpu as pltpu
from jax.sharding import PartitionSpec as P

HEADS = 16
KV_HEADS = 4
HEAD = 128
WINDOW = 128
GROUP = HEADS // KV_HEADS
SCALE = HEAD ** (-0.5)
LOG2E = 1.4426950408889634
VMEM = pl.BlockSpec(memory_space=pltpu.VMEM)
SMEM = pl.BlockSpec(memory_space=pltpu.SMEM)
ANY = pl.BlockSpec(memory_space=pl.ANY)
HBM = pl.BlockSpec(memory_space=pltpu.HBM)


def dot(a, b, dims):
    return lax.dot_general(a, b, (dims, ((), ())), preferred_element_type=jnp.float32)


def struct(shape, dtype):
    return jax.ShapeDtypeStruct(shape, dtype)


def call(kernel, name, out_shape, in_specs, args, flops, scratch=(), out_specs=None):
    args = [
        pltpu.with_memory_space_constraint(a, pltpu.HBM) if spec is HBM else a
        for a, spec in zip(args, in_specs, strict=True)
    ]
    moved = sum(math.prod(a.shape) * a.dtype.itemsize for a in (*args, *out_shape))
    return pl.pallas_call(
        kernel,
        out_shape=out_shape,
        in_specs=in_specs,
        out_specs=out_specs or (VMEM,) * len(out_shape),
        scratch_shapes=scratch,
        compiler_params=pltpu.CompilerParams(vmem_limit_bytes=32 * 1024 * 1024),
        cost_estimate=pl.CostEstimate(flops=flops, bytes_accessed=moved, transcendentals=0),
        name=name,
    )(*args)


def own_mask(rows, width):
    key_pos = lax.broadcasted_iota(jnp.int32, (rows, width), 0)
    query_pos = lax.rem(lax.broadcasted_iota(jnp.int32, (rows, width), 1), rows)
    return key_pos <= query_pos


def stacked(ref, b, heads):
    return jnp.concatenate([ref[b, :, h * HEAD:(h + 1) * HEAD] for h in heads], axis=0)


def split(own, value):
    zero = jnp.zeros_like(value)
    return jnp.concatenate(
        [jnp.where(own, value, zero), jnp.where(own, zero, value)], axis=0).astype(jnp.bfloat16)


def groups(ref):
    batch, rows, _ = ref.shape
    for b in range(batch):
        for g in range(KV_HEADS):
            heads = range(g * GROUP, (g + 1) * GROUP)
            yield b, heads, slice(g * HEAD, (g + 1) * HEAD), slice(g * GROUP * rows, (g + 1) * GROUP * rows)


def load_kernel(first_ref, sinks_in, q_in, k_in, v_in, do_in,
                q_ref, k_ref, v_ref, do_ref, s_ref, dp_ref, bias_ref, sink_ref, sinks_ref, sems):
    _, rows, _ = q_ref.shape
    copies = [
        pltpu.make_async_copy(source, target, sems.at[n])
        for n, (source, target) in enumerate(
            ((k_in, k_ref), (q_in, q_ref), (v_in, v_ref), (do_in, do_ref), (sinks_in, sinks_ref)))
    ]
    for copy in copies:
        copy.start()
    bias_ref[...] = jnp.full(bias_ref.shape, jnp.where(first_ref[0] == 1, -1e30, 0.0), jnp.float32)
    copies[0].wait()
    copies[1].wait()
    for b, heads, kv, cols in groups(q_ref):
        s_ref[b, :, cols] = dot(k_ref[b, :, kv], stacked(q_ref, b, heads), ((1,), (1,)))
    copies[2].wait()
    copies[3].wait()
    for b, heads, kv, cols in groups(q_ref):
        dp_ref[b, :, cols] = dot(v_ref[b, :, kv], stacked(do_ref, b, heads), ((1,), (1,)))
    copies[4].wait()
    for h in range(HEADS):
        sink_ref[:, h * rows:(h + 1) * rows] = jnp.full((1, rows), sinks_ref[h] * LOG2E, jnp.float32)


def softmax_kernel(bias_ref, sink_ref, q_ref, do_ref, hk_ref, s_ref, p_ref, sp_ref, dv_ref, back_ref):
    _, rows, _ = q_ref.shape
    own = own_mask(rows, GROUP * rows)
    for b, heads, kv, cols in groups(q_ref):
        before = dot(hk_ref[b, :, kv], stacked(q_ref, b, heads), ((1,), (1,))) + bias_ref[...]
        score = jnp.where(own, s_ref[b, :, cols], before) * (SCALE * LOG2E)
        sink = sink_ref[:, cols]
        top = jnp.maximum(jnp.max(score, axis=0, keepdims=True), sink)
        weight = jnp.exp2(score - top)
        sink_weight = jnp.exp2(sink - top)
        scale = 1.0 / (jnp.sum(weight, axis=0, keepdims=True) + sink_weight)
        prob = weight * scale
        p_ref[b, :, cols] = prob
        sp_ref[b, :, cols] = sink_weight * scale
        grad_value = dot(split(own, prob), stacked(do_ref, b, heads), ((1,), (0,)))
        dv_ref[b, :, kv] = grad_value[:rows]
        back_ref[b, :, kv] = grad_value[rows:].astype(jnp.bfloat16)


def grad_kernel(q_ref, do_ref, k_ref, hk_ref, hv_ref, p_ref, sp_ref, dp_ref, back_dv_ref,
                terms_out, dq_ref, dk_ref, back_ref, gp_ref, delta_ref, sink_ref, terms_ref, sem):
    _, rows, _ = q_ref.shape
    width = KV_HEADS * HEAD
    own = own_mask(rows, GROUP * rows)
    sink_ref[...] = jnp.zeros_like(sink_ref)
    for b, heads, kv, cols in groups(do_ref):
        before = dot(hv_ref[b, :, kv], stacked(do_ref, b, heads), ((1,), (1,)))
        grad_prob = jnp.where(own, dp_ref[b, :, cols], before)
        gp_ref[b, :, cols] = grad_prob
        delta = jnp.sum(p_ref[b, :, cols] * grad_prob, axis=0, keepdims=True)
        delta_ref[b, :, cols] = delta
        terms = sp_ref[b, :, cols] * delta
        for n, h in enumerate(heads):
            sink_ref[h:h + 1, :] += terms[:, n * rows:(n + 1) * rows]
    ones = jnp.ones((terms_ref.shape[0], rows), jnp.bfloat16)
    terms = sink_ref[...]
    high = terms.astype(jnp.bfloat16)
    rest = terms - high.astype(jnp.float32)
    middle = rest.astype(jnp.bfloat16)
    low = (rest - middle.astype(jnp.float32)).astype(jnp.bfloat16)
    terms_ref[...] = sum(dot(ones, part, ((1,), (1,))) for part in (low, middle, high))
    copy = pltpu.make_async_copy(terms_ref, terms_out, sem)
    copy.start()
    back_ref[:, :, width:] = back_dv_ref[...]
    for b, heads, kv, cols in groups(q_ref):
        dscores = split(own, p_ref[b, :, cols] * (gp_ref[b, :, cols] - delta_ref[b, :, cols]))
        grad_key = dot(dscores, stacked(q_ref, b, heads), ((1,), (0,))) * SCALE
        dk_ref[b, :, kv] = grad_key[:rows]
        back_ref[b, :, kv] = grad_key[rows:].astype(jnp.bfloat16)
        key = jnp.concatenate([k_ref[b, :, kv], hk_ref[b, :, kv]], axis=0)
        grad_query = (dot(dscores, key, ((0,), (0,))) * SCALE).astype(jnp.bfloat16)
        for n, h in enumerate(heads):
            dq_ref[b, :, h * HEAD:(h + 1) * HEAD] = grad_query[n * rows:(n + 1) * rows]
    copy.wait()


def finish_kernel(factor, own_dk_ref, own_dv_ref, back_ref, terms_ref, dk_ref, dv_ref, sink_ref):
    width = dk_ref.shape[2]
    dk_ref[...] = (own_dk_ref[...] + back_ref[:, :, :width].astype(jnp.float32)).astype(jnp.bfloat16)
    dv_ref[...] = (own_dv_ref[...] + back_ref[:, :, width:].astype(jnp.float32)).astype(jnp.bfloat16)
    sink_ref[...] = jnp.sum(terms_ref[...], axis=0, keepdims=True)[:, :HEADS] * factor


def ring(value, axis, steps):
    count = lax.axis_size(axis)
    return lax.ppermute(value, axis, [(i, (i + steps) % count) for i in range(count)])


def shift(value, axis):
    count = lax.axis_size(axis)
    return lax.ppermute(value, axis, [(i, i + 1) for i in range(count - 1)])


def body(queries, keys, values, dout, sinks):
    batch, rows, width = queries.shape
    kv_width = keys.shape[2]
    dp, ctx = lax.axis_size("dp"), lax.axis_size("ctx")
    assert rows == WINDOW and dp & (dp - 1) == 0 and ctx & (ctx - 1) == 0
    bf16, f32 = jnp.bfloat16, jnp.float32
    square = struct((batch, rows, HEADS * rows), f32)
    line = struct((batch, 1, HEADS * rows), f32)
    kv_bf16 = struct((batch, rows, kv_width), bf16)
    kv_f32 = struct((batch, rows, kv_width), f32)
    product = 2 * batch * HEADS * rows * rows * HEAD

    first = (lax.axis_index("ctx") == 0).astype(jnp.int32).reshape(1)
    halo_keys = ring(keys, "ctx", 1)
    halo_values = shift(values, "ctx")
    q, k, v, do, score, grad_prob, bias, sink = call(
        load_kernel, "load",
        (struct(queries.shape, bf16), kv_bf16, kv_bf16, struct(dout.shape, bf16), square, square,
         struct((1, GROUP * rows), f32), struct((1, HEADS * rows), f32)),
        [SMEM] + [HBM] * 5, (first, sinks, queries, keys, values, dout), 2 * product,
        scratch=[pltpu.SMEM((HEADS,), f32), pltpu.SemaphoreType.DMA((5,))])
    prob, sink_prob, own_values, back_values = call(
        softmax_kernel, "softmax", (square, line, kv_f32, kv_bf16),
        [VMEM] * 6, (bias, sink, q, do, halo_keys, score), 3 * product)
    terms, grad_query, own_keys, back = call(
        grad_kernel, "grad",
        (struct((dp * ctx, HEADS), f32), pltpu.VMEM(queries.shape, bf16), kv_f32,
         struct((batch, rows, 2 * kv_width), bf16)),
        [VMEM] * 9, (q, do, k, halo_keys, halo_values, prob, sink_prob, grad_prob, back_values), 5 * product,
        scratch=[pltpu.VMEM(square.shape, f32), pltpu.VMEM(line.shape, f32), pltpu.VMEM((HEADS, rows), f32),
                 pltpu.VMEM((dp * ctx, HEADS), f32), pltpu.SemaphoreType.DMA],
        out_specs=(HBM, VMEM, VMEM, VMEM))
    back = ring(back, "ctx", -1)
    terms = lax.all_to_all(terms, ("dp", "ctx"), 0, 0, tiled=True)
    factor = -1.0 / (dp * batch * ctx * rows) ** 0.5
    grad_keys, grad_values, sink_grad = call(
        functools.partial(finish_kernel, factor), "finish",
        (kv_bf16, kv_bf16, struct((1, HEADS), f32)),
        [VMEM] * 4, (own_keys, own_values, back, terms), 0)
    return grad_query, grad_keys, grad_values, sink_grad.reshape(HEADS)


def solution(mesh):
    whole = P("dp", "ctx", None)
    return jax.shard_map(
        body,
        mesh=mesh,
        in_specs=(whole, whole, whole, whole, P()),
        out_specs=(whole, whole, whole, P()),
        check_vma=False,
    )
```

time: 31.6 us -> 26.5 us (0.84)
  waiting for transfers between devices: 15.4 us -> 6.31 us
  starting transfers between devices: 9.35 us -> 12.5 us
  local copies, waits for them, and re-layouts: 0 us -> 0.8 us
    ppermute x5 -> x1, waiting for transfers between devices: 11.5 us -> 0.01 us  [shift(): return lax.ppermute(value, axis, [(i, i + 1) for i in range(count - 1)])]
    all_to_all x0 -> x1, waiting for transfers between devices: none -> 6.3 us  [body(): terms = lax.all_to_all(terms, ('dp', 'ctx'), 0, 0, tiled=True)]
    ppermute x3 -> x2, waiting for transfers between devices: 3.89 us -> 0.01 us  [ring(): lax.ppermute(value, axis, [(i, (i + steps) % count) for i in range(count)])]
    all_to_all x0 -> x1, starting transfers between devices: none -> 3.08 us  [body(): terms = lax.all_to_all(terms, ('dp', 'ctx'), 0, 0, tiled=True)]
    unnamed x0 -> x1, local copies, waits for them, and re-layouts: none -> 0.8 us
    ppermute x5 -> x1, starting transfers between devices: 2.96 us -> 3.48 us  [shift(): return lax.ppermute(value, axis, [(i, i + 1) for i in range(count - 1)])]
    ppermute x3 -> x2, starting transfers between devices: 6.39 us -> 6 us  [ring(): lax.ppermute(value, axis, [(i, (i + steps) % count) for i in range(count)])]
    pallas_call x5 -> x4, Pallas kernels: 6 us -> 5.95 us  [call(): pl.pallas_call(kernel, out_shape=out_shape, in_specs=in_specs, out_specs=...]
  transfers between devices with their start and end apart: 8 -> 4, of which waited for: 7 -> 1; matrix products, arithmetic and copies ran while one was open for 0% -> 3% of each run, Pallas kernels for 10% -> 15%
where the time goes in v4:
time: 26.5 us; the launch traced here: 26.3 us
  starting transfers between devices  12.5 us (47%)
  waiting for transfers between devices  6.31 us (24%)
  Pallas kernels  5.95 us (22%)
  local copies, waits for them, and re-layouts  0.8 us (3%)
  between operations  0.7 us (3%)
    all_to_all x1, waiting for transfers between devices, body(): terms = lax.all_to_all(terms, ('dp', 'ctx'), 0, 0, tiled=True)  6.3 us
    ppermute x2, starting transfers between devices, ring(): lax.ppermute(value, axis, [(i, (i + steps) % count) for i in range(count)])  6 us
    pallas_call x4, Pallas kernels, call(): pl.pallas_call(kernel, out_shape=out_shape, in_specs=in_specs, out_specs=...  5.95 us
    ppermute x1, starting transfers between devices, shift(): return lax.ppermute(value, axis, [(i, i + 1) for i in range(count - 1)])  3.48 us
    all_to_all x1, starting transfers between devices, body(): terms = lax.all_to_all(terms, ('dp', 'ctx'), 0, 0, tiled=True)  3.08 us
    unnamed x1, local copies, waits for them, and re-layouts  0.8 us
  transfers between devices with their start and end apart: 4, of which 1 were waited for; matrix products, arithmetic and copies ran while one was open for 3% of the time, Pallas kernels for 15%

profile of v4, /device:TPU:0, one launch (start us, length us, event | category | flops | bytes accessed | tf_op | source)
XLA Modules:
  0.0 26.3 jit_solution(6051366733878183768)
XLA Ops:
  0.6 3.1 %collective-permute-start = (bf16[1,128,512]{2,1,0:T(8,128)(2,1)}, bf16[1,128,512]{2,1,0:T(8,128)(2,1)S(1)}, u32[]{:S(2)}, u32[]{:S(2)}) collective-permute-start(bf16[1,128,512]{2,1,0:T(8,128)(2,1)} %k_in.1), channel_id=1, source_target_pairs={{0,1},{1,2},{2,3},{3,0},{4,5},{5,6},{6,7},{7,4},{8,9},{9,10},{10,1... | collective-permute-start | bytes 393224 | tf_op jit(solution)/shard_map/ppermute | solution.py:163
  3.7 3.5 %collective-permute-start.1 = (bf16[1,128,512]{2,1,0:T(8,128)(2,1)}, bf16[1,128,512]{2,1,0:T(8,128)(2,1)S(1)}, u32[]{:S(2)}, u32[]{:S(2)}) collective-permute-start(bf16[1,128,512]{2,1,0:T(8,128)(2,1)} %v_in.1), channel_id=1, source_target_pairs={{0,1},{1,2},{2,3},{4,5},{5,6},{6,7},{8,9},{9,10},{10,11},{12,13},{... | collective-permute-start | bytes 393224 | tf_op jit(solution)/shard_map/ppermute | solution.py:168
  7.2 2.4 %load.1 = (bf16[1,128,2048]{2,1,0:T(8,128)(2,1)S(1)}, bf16[1,128,512]{2,1,0:T(8,128)(2,1)S(1)}, bf16[1,128,512]{2,1,0:T(8,128)(2,1)}, bf16[1,128,2048]{2,1,0:T(8...) custom-call(s32[1]{0:T(128)} %bitcast.first_ref, ...), custom_call_target="tpu_custom_call" | custom-call | flops 134217728 | bytes 4728900 | tf_op jit(solution)/shard_map/load/pallas_call | solution.py:38
  9.6 0.0 collective-permute-done.hk_ref
  9.7 1.4 %softmax.1 = (f32[1,128,2048]{2,1,0:T(8,128)S(1)}, f32[1,1,2048]{2,1,0:T(1,128)S(1)}, f32[1,128,512]{2,1,0:T(8,128)S(1)}, bf16[1,128,512]{2,1,0:T(8,128)(2,1)S(1)}) custom-call(f32[1,512]{1,0:T(1,128)S(1)} %get-tuple-element.25.bias_ref, f32[1,2048]{1,0:T(1,128)S(1)} %get-tuple-element.26.sink_ref, bf16[1,128,2048]{2,1,0:T(8,128)(2,1)S(1)} %get-tuple-element.22.q_ref, ...), custom_call_target="tpu_custom_call" | custom-call | flops 201326592 | bytes 3688448 | tf_op jit(solution)/shard_map/softmax/pallas_call | solution.py:38
  11.1 0.0 collective-permute-done.1.hv_ref
  11.1 1.3 %grad.1 = (f32[32,16]{1,0:T(8,128)}, bf16[1,128,2048]{2,1,0:T(8,128)(2,1)S(1)}, f32[1,128,512]{2,1,0:T(8,128)S(1)}, bf16[1,128,1024]{2,1,0:T(8,128)(2,1)S(1)}) custom-call(bf16[1,128,2048]{2,1,0:T(8,128)(2,1)S(1)} %get-tuple-element.22.q_ref, bf16[1,128,2048]{2,1,0:T(8,128)(2,1)S(1)} %get-tuple-element.23.do_ref, ...), custom_call_target="tpu_custom_call" | custom-call | flops 335544320 | bytes 4728832 | tf_op jit(solution)/shard_map/grad/pallas_call | solution.py:38
  12.5 2.9 %collective-permute-start.2 = (bf16[1,128,1024]{2,1,0:T(8,128)(2,1)S(1)}, bf16[1,128,1024]{2,1,0:T(8,128)(2,1)S(1)}, u32[]{:S(2)}, u32[]{:S(2)}) collective-permute-start(bf16[1,128,1024]{2,1,0:T(8,128)(2,1)S(1)} %get-tuple-element.35), channel_id=1, source_target_pairs={{0,3},{1,0},{2,1},{3,2},{4,7},{5,4},{6,5},{7,6},{8,11},{9,8},{10,9... | collective-permute-start | bytes 786440 | tf_op jit(solution)/shard_map/ppermute | solution.py:163
  15.4 3.1 %all-to-all-start = ((f32[32,1,16]{2,1,0:T(1,128)}), f32[32,1,16]{2,1,0:T(1,128)S(1)}, u32[]{:S(2)}, u32[]{:S(2)}) async-start(f32[32,1,16]{2,1,0:T(1,128)} %bitcast.2), calls=%async_computation | async-start | bytes 32768 | tf_op jit(solution)/shard_map/all_to_all | solution.py:204
  18.5 0.8 %copy.10 = bf16[1,128,2048]{2,1,0:T(8,128)(2,1)} copy(bf16[1,128,2048]{2,1,0:T(8,128)(2,1)S(1)} %get-tuple-element.40) | data formatting | bytes 1048576
  19.3 6.3 %all-to-all-done = f32[32,1,16]{2,1,0:T(1,128)S(1)} async-done(((f32[32,1,16]{2,1,0:T(1,128)}), f32[32,1,16]{2,1,0:T(1,128)S(1)}, u32[]{:S(2)}, u32[]{:S(2)}) %all-to-all-start) | async-done | bytes 2080 | tf_op jit(solution)/shard_map/all_to_all | solution.py:204
  25.6 0.0 collective-permute-done.2.back_ref
  25.6 0.7 %finish.1 = (bf16[1,128,512]{2,1,0:T(8,128)(2,1)}, bf16[1,128,512]{2,1,0:T(8,128)(2,1)}, f32[1,16]{1,0:T(1,128)}) custom-call(f32[1,128,512]{2,1,0:T(8,128)S(1)} %get-tuple-element.33.own_dk_ref, f32[1,128,512]{2,1,0:T(8,128)S(1)} %get-tuple-element.34.own_dv_ref, bf16[1,128,1024]{2,1,0:T(8,128)(2,1)S(1)} %collective-permute-done.2.back_ref, ...), custom_call_target="tpu_custom_call" | custom-call | bytes 1050688 | tf_op jit(solution)/shard_map/finish/pallas_call | solution.py:38
Async XLA Ops:
  0.6 9.0 %collective-permute-start = (bf16[1,128,512]{2,1,0:T(8,128)(2,1)}, bf16[1,128,512]{2,1,0:T(8,128)(2,1)S(1)}, u32[]{:S(2)}, u32[]{:S(2)}) collective-permute-start(bf16[1,128,512]{2,1,0:T(8,128)(2,1)} %k_in.1), channel_id=1, source_target_pairs={{0,1},{1,2},{2,3},{3,0},{4,5},{5,6},{6,7},{7,4},{8,9},{9,10},{10,1... | collective-permute-start | bytes 393224 | tf_op jit(solution)/shard_map/ppermute | solution.py:163
  3.7 7.4 %collective-permute-start.1 = (bf16[1,128,512]{2,1,0:T(8,128)(2,1)}, bf16[1,128,512]{2,1,0:T(8,128)(2,1)S(1)}, u32[]{:S(2)}, u32[]{:S(2)}) collective-permute-start(bf16[1,128,512]{2,1,0:T(8,128)(2,1)} %v_in.1), channel_id=1, source_target_pairs={{0,1},{1,2},{2,3},{4,5},{5,6},{6,7},{8,9},{9,10},{10,11},{12,13},{... | collective-permute-start | bytes 393224 | tf_op jit(solution)/shard_map/ppermute | solution.py:168
  12.5 13.1 %collective-permute-start.2 = (bf16[1,128,1024]{2,1,0:T(8,128)(2,1)S(1)}, bf16[1,128,1024]{2,1,0:T(8,128)(2,1)S(1)}, u32[]{:S(2)}, u32[]{:S(2)}) collective-permute-start(bf16[1,128,1024]{2,1,0:T(8,128)(2,1)S(1)} %get-tuple-element.35), channel_id=1, source_target_pairs={{0,3},{1,0},{2,1},{3,2},{4,7},{5,4},{6,5},{7,6},{8,11},{9,8},{10,9... | collective-permute-start | bytes 786440 | tf_op jit(solution)/shard_map/ppermute | solution.py:163
  15.4 10.2 %all-to-all-start = ((f32[32,1,16]{2,1,0:T(1,128)}), f32[32,1,16]{2,1,0:T(1,128)S(1)}, u32[]{:S(2)}, u32[]{:S(2)}) async-start(f32[32,1,16]{2,1,0:T(1,128)} %bitcast.2), calls=%async_computation | async-start | bytes 32768 | tf_op jit(solution)/shard_map/all_to_all | solution.py:204

commit v5 on v4

--- a/solution.py
+++ b/solution.py
@@ -114,10 +114,9 @@
         back_ref[b, :, kv] = grad_value[rows:].astype(jnp.bfloat16)
 
 
-def grad_kernel(q_ref, do_ref, k_ref, hk_ref, hv_ref, p_ref, sp_ref, dp_ref, back_dv_ref,
+def grad_kernel(q_ref, do_ref, k_ref, hk_ref, hv_ref, p_ref, sp_ref, dp_ref,
                 terms_out, dq_ref, dk_ref, back_ref, gp_ref, delta_ref, sink_ref, terms_ref, sem):
     _, rows, _ = q_ref.shape
-    width = KV_HEADS * HEAD
     own = own_mask(rows, GROUP * rows)
     sink_ref[...] = jnp.zeros_like(sink_ref)
     for b, heads, kv, cols in groups(do_ref):
@@ -138,7 +137,6 @@
     terms_ref[...] = sum(dot(ones, part, ((1,), (1,))) for part in (low, middle, high))
     copy = pltpu.make_async_copy(terms_ref, terms_out, sem)
     copy.start()
-    back_ref[:, :, width:] = back_dv_ref[...]
     for b, heads, kv, cols in groups(q_ref):
         dscores = split(own, p_ref[b, :, cols] * (gp_ref[b, :, cols] - delta_ref[b, :, cols]))
         grad_key = dot(dscores, stacked(q_ref, b, heads), ((1,), (0,))) * SCALE
@@ -151,11 +149,17 @@
     copy.wait()
 
 
-def finish_kernel(factor, own_dk_ref, own_dv_ref, back_ref, terms_ref, dk_ref, dv_ref, sink_ref):
-    width = dk_ref.shape[2]
-    dk_ref[...] = (own_dk_ref[...] + back_ref[:, :, :width].astype(jnp.float32)).astype(jnp.bfloat16)
-    dv_ref[...] = (own_dv_ref[...] + back_ref[:, :, width:].astype(jnp.float32)).astype(jnp.bfloat16)
-    sink_ref[...] = jnp.sum(terms_ref[...], axis=0, keepdims=True)[:, :HEADS] * factor
+def join_kernel(own_ref, back_ref, out_ref):
+    out_ref[...] = (own_ref[...] + back_ref[...].astype(jnp.float32)).astype(jnp.bfloat16)
+
+
+def total_kernel(factor, terms_ref, _, total_ref):
+    total_ref[...] = jnp.sum(terms_ref[...], axis=0, keepdims=True) * factor
+
+
+def finish_kernel(own_ref, back_ref, total_ref, out_ref, sink_ref):
+    join_kernel(own_ref, back_ref, out_ref)
+    sink_ref[...] = total_ref[...]
 
 
 def ring(value, axis, steps):
@@ -177,7 +181,6 @@
     square = struct((batch, rows, HEADS * rows), f32)
     line = struct((batch, 1, HEADS * rows), f32)
     kv_bf16 = struct((batch, rows, kv_width), bf16)
-    kv_f32 = struct((batch, rows, kv_width), f32)
     product = 2 * batch * HEADS * rows * rows * HEAD
 
     first = (lax.axis_index("ctx") == 0).astype(jnp.int32).reshape(1)
@@ -190,23 +193,28 @@
         [SMEM] + [HBM] * 5, (first, sinks, queries, keys, values, dout), 2 * product,
         scratch=[pltpu.SMEM((HEADS,), f32), pltpu.SemaphoreType.DMA((5,))])
     prob, sink_prob, own_values, back_values = call(
-        softmax_kernel, "softmax", (square, line, kv_f32, kv_bf16),
+        softmax_kernel, "softmax",
+        (pltpu.VMEM(square.shape, f32), pltpu.VMEM(line.shape, f32), pltpu.VMEM(keys.shape, f32),
+         pltpu.VMEM(keys.shape, bf16)),
         [VMEM] * 6, (bias, sink, q, do, halo_keys, score), 3 * product)
-    terms, grad_query, own_keys, back = call(
+    back_values = ring(back_values, "ctx", -1)
+    terms, grad_query, own_keys, back_keys = call(
         grad_kernel, "grad",
-        (struct((dp * ctx, HEADS), f32), pltpu.VMEM(queries.shape, bf16), kv_f32,
-         struct((batch, rows, 2 * kv_width), bf16)),
-        [VMEM] * 9, (q, do, k, halo_keys, halo_values, prob, sink_prob, grad_prob, back_values), 5 * product,
+        (struct((dp * ctx, HEADS), f32), pltpu.VMEM(queries.shape, bf16), pltpu.VMEM(keys.shape, f32),
+         pltpu.VMEM(keys.shape, bf16)),
+        [VMEM] * 8, (q, do, k, halo_keys, halo_values, prob, sink_prob, grad_prob), 5 * product,
         scratch=[pltpu.VMEM(square.shape, f32), pltpu.VMEM(line.shape, f32), pltpu.VMEM((HEADS, rows), f32),
                  pltpu.VMEM((dp * ctx, HEADS), f32), pltpu.SemaphoreType.DMA],
         out_specs=(HBM, VMEM, VMEM, VMEM))
-    back = ring(back, "ctx", -1)
+    back_keys = ring(back_keys, "ctx", -1)
     terms = lax.all_to_all(terms, ("dp", "ctx"), 0, 0, tiled=True)
+    grad_values, = call(join_kernel, "join", (kv_bf16,), [VMEM] * 2, (own_values, back_values), 0)
     factor = -1.0 / (dp * batch * ctx * rows) ** 0.5
-    grad_keys, grad_values, sink_grad = call(
-        functools.partial(finish_kernel, factor), "finish",
-        (kv_bf16, kv_bf16, struct((1, HEADS), f32)),
-        [VMEM] * 4, (own_keys, own_values, back, terms), 0)
+    total, = call(
+        functools.partial(total_kernel, factor), "total", (struct((1, HEADS), f32),), [VMEM, HBM],
+        (terms, grad_values), 10 ** 10)
+    grad_keys, sink_grad = call(
+        finish_kernel, "finish", (kv_bf16, struct((1, HEADS), f32)), [VMEM] * 3, (own_keys, back_keys, total), 0)
     return grad_query, grad_keys, grad_values, sink_grad.reshape(HEADS)
 
 

time: 26.5 us -> 25.9 us (0.977)
  waiting for transfers between devices: 6.31 us -> 2.06 us
  starting transfers between devices: 12.5 us -> 15.6 us
  Pallas kernels: 5.95 us -> 6.59 us
    all_to_all x1, waiting for transfers between devices: 6.3 us -> 2.05 us  [body(): terms = lax.all_to_all(terms, ('dp', 'ctx'), 0, 0, tiled=True)]
    ppermute x2 -> x3, starting transfers between devices: 6 us -> 9.25 us  [ring(): lax.ppermute(value, axis, [(i, (i + steps) % count) for i in range(count)])]
    pallas_call x4 -> x6, Pallas kernels: 5.95 us -> 6.59 us  [call(): pl.pallas_call(kernel, out_shape=out_shape, in_specs=in_specs, out_specs=...]
  transfers between devices with their start and end apart: 4 -> 5, of which waited for: 1 -> 1; matrix products, arithmetic and copies ran while one was open for 3% -> 3% of each run, Pallas kernels for 15% -> 23%
where the time goes in v5:
time: 25.9 us; the launch traced here: 25.7 us
  starting transfers between devices  15.6 us (60%)
  Pallas kernels  6.59 us (25%)
  waiting for transfers between devices  2.06 us (8%)
  local copies, waits for them, and re-layouts  0.79 us (3%)
  between operations  0.7 us (3%)
    ppermute x3, starting transfers between devices, ring(): lax.ppermute(value, axis, [(i, (i + steps) % count) for i in range(count)])  9.25 us
    pallas_call x6, Pallas kernels, call(): pl.pallas_call(kernel, out_shape=out_shape, in_specs=in_specs, out_specs=...  6.59 us
    ppermute x1, starting transfers between devices, shift(): return lax.ppermute(value, axis, [(i, i + 1) for i in range(count - 1)])  3.48 us
    all_to_all x1, starting transfers between devices, body(): terms = lax.all_to_all(terms, ('dp', 'ctx'), 0, 0, tiled=True)  2.83 us
    all_to_all x1, waiting for transfers between devices, body(): terms = lax.all_to_all(terms, ('dp', 'ctx'), 0, 0, tiled=True)  2.05 us
    unnamed x1, local copies, waits for them, and re-layouts  0.79 us
  transfers between devices with their start and end apart: 5, of which 1 were waited for; matrix products, arithmetic and copies ran while one was open for 3% of the time, Pallas kernels for 23%

profile of v5, /device:TPU:0, one launch (start us, length us, event | category | flops | bytes accessed | tf_op | source)
XLA Modules:
  0.0 25.7 jit_solution(10551079291066138548)
XLA Ops:
  0.6 3.1 %collective-permute-start = (bf16[1,128,512]{2,1,0:T(8,128)(2,1)}, bf16[1,128,512]{2,1,0:T(8,128)(2,1)S(1)}, u32[]{:S(2)}, u32[]{:S(2)}) collective-permute-start(bf16[1,128,512]{2,1,0:T(8,128)(2,1)} %k_in.1), channel_id=1, source_target_pairs={{0,1},{1,2},{2,3},{3,0},{4,5},{5,6},{6,7},{7,4},{8,9},{9,10},{10,1... | collective-permute-start | bytes 393224 | tf_op jit(solution)/shard_map/ppermute | solution.py:167
  3.7 3.5 %collective-permute-start.1 = (bf16[1,128,512]{2,1,0:T(8,128)(2,1)}, bf16[1,128,512]{2,1,0:T(8,128)(2,1)S(1)}, u32[]{:S(2)}, u32[]{:S(2)}) collective-permute-start(bf16[1,128,512]{2,1,0:T(8,128)(2,1)} %v_in.1), channel_id=1, source_target_pairs={{0,1},{1,2},{2,3},{4,5},{5,6},{6,7},{8,9},{9,10},{10,11},{12,13},{... | collective-permute-start | bytes 393224 | tf_op jit(solution)/shard_map/ppermute | solution.py:172
  7.2 2.4 %load.1 = (bf16[1,128,2048]{2,1,0:T(8,128)(2,1)S(1)}, bf16[1,128,512]{2,1,0:T(8,128)(2,1)S(1)}, bf16[1,128,512]{2,1,0:T(8,128)(2,1)}, bf16[1,128,2048]{2,1,0:T(8...) custom-call(s32[1]{0:T(128)} %bitcast.first_ref, ...), custom_call_target="tpu_custom_call" | custom-call | flops 134217728 | bytes 4728900 | tf_op jit(solution)/shard_map/load/pallas_call | solution.py:38
  9.6 0.0 collective-permute-done.hk_ref
  9.7 1.4 %softmax.1 = (f32[1,128,2048]{2,1,0:T(8,128)S(1)}, f32[1,1,2048]{2,1,0:T(1,128)S(1)}, f32[1,128,512]{2,1,0:T(8,128)S(1)}, bf16[1,128,512]{2,1,0:T(8,128)(2,1)S(1)}) custom-call(f32[1,512]{1,0:T(1,128)S(1)} %get-tuple-element.24.bias_ref, f32[1,2048]{1,0:T(1,128)S(1)} %get-tuple-element.25.sink_ref, bf16[1,128,2048]{2,1,0:T(8,128)(2,1)S(1)} %get-tuple-element.21.q_ref, ...), custom_call_target="tpu_custom_call" | custom-call | flops 201326592 | bytes 3688448 | tf_op jit(solution)/shard_map/softmax/pallas_call | solution.py:38
  11.1 2.5 %collective-permute-start.3 = (bf16[1,128,512]{2,1,0:T(8,128)(2,1)S(1)}, bf16[1,128,512]{2,1,0:T(8,128)(2,1)S(1)}, u32[]{:S(2)}, u32[]{:S(2)}) collective-permute-start(bf16[1,128,512]{2,1,0:T(8,128)(2,1)S(1)} %get-tuple-element.35), channel_id=1, source_target_pairs={{0,3},{1,0},{2,1},{3,2},{4,7},{5,4},{6,5},{7,6},{8,11},{9,8},{10,9... | collective-permute-start | bytes 393224 | tf_op jit(solution)/shard_map/ppermute | solution.py:167
  13.6 0.0 collective-permute-done.1.hv_ref
  13.6 1.3 %grad.1 = (f32[32,16]{1,0:T(8,128)}, bf16[1,128,2048]{2,1,0:T(8,128)(2,1)S(1)}, f32[1,128,512]{2,1,0:T(8,128)S(1)}, bf16[1,128,512]{2,1,0:T(8,128)(2,1)S(1)}) custom-call(bf16[1,128,2048]{2,1,0:T(8,128)(2,1)S(1)} %get-tuple-element.21.q_ref, bf16[1,128,2048]{2,1,0:T(8,128)(2,1)S(1)} %get-tuple-element.22.do_ref, ...), custom_call_target="tpu_custom_call" | custom-call | flops 335544320 | bytes 4466688 | tf_op jit(solution)/shard_map/grad/pallas_call | solution.py:38
  14.9 2.8 %all-to-all-start = ((f32[32,1,16]{2,1,0:T(1,128)}), f32[32,1,16]{2,1,0:T(1,128)S(1)}, u32[]{:S(2)}, u32[]{:S(2)}) async-start(f32[32,1,16]{2,1,0:T(1,128)} %bitcast.2), calls=%async_computation | async-start | bytes 32768 | tf_op jit(solution)/shard_map/all_to_all | solution.py:210
  17.8 3.7 %collective-permute-start.2 = (bf16[1,128,512]{2,1,0:T(8,128)(2,1)S(1)}, bf16[1,128,512]{2,1,0:T(8,128)(2,1)S(1)}, u32[]{:S(2)}, u32[]{:S(2)}) collective-permute-start(bf16[1,128,512]{2,1,0:T(8,128)(2,1)S(1)} %get-tuple-element.32), channel_id=1, source_target_pairs={{0,3},{1,0},{2,1},{3,2},{4,7},{5,4},{6,5},{7,6},{8,11},{9,8},{10,9... | collective-permute-start | bytes 393224 | tf_op jit(solution)/shard_map/ppermute | solution.py:167
  21.5 0.8 %copy.10 = bf16[1,128,2048]{2,1,0:T(8,128)(2,1)} copy(bf16[1,128,2048]{2,1,0:T(8,128)(2,1)S(1)} %get-tuple-element.38) | data formatting | bytes 1048576
  22.3 0.0 collective-permute-done.3.back_ref
  22.3 0.7 %join.1._ = bf16[1,128,512]{2,1,0:T(8,128)(2,1)} custom-call(f32[1,128,512]{2,1,0:T(8,128)S(1)} %get-tuple-element.34.own_ref, bf16[1,128,512]{2,1,0:T(8,128)(2,1)S(1)} %collective-permute-done.3.back_ref), custom_call_target="tpu_custom_call" | custom-call | bytes 524288 | tf_op jit(solution)/shard_map/join/pallas_call | solution.py:38
  22.9 2.0 %all-to-all-done = f32[32,1,16]{2,1,0:T(1,128)S(1)} async-done(((f32[32,1,16]{2,1,0:T(1,128)}), f32[32,1,16]{2,1,0:T(1,128)S(1)}, u32[]{:S(2)}, u32[]{:S(2)}) %all-to-all-start) | async-done | bytes 2080 | tf_op jit(solution)/shard_map/all_to_all | solution.py:210
  25.0 0.0 collective-permute-done.2.back_ref
  25.0 0.7 %finish.1 = (bf16[1,128,512]{2,1,0:T(8,128)(2,1)}, f32[1,16]{1,0:T(1,128)}) custom-call(f32[1,128,512]{2,1,0:T(8,128)S(1)} %get-tuple-element.31.own_ref, bf16[1,128,512]{2,1,0:T(8,128)(2,1)S(1)} %collective-permute-done.2.back_ref, f32[1,16]{1,0:T(1,128)S(1)} %total.1.total_ref), custom_call_target="tpu_custom_call" | custom-call | bytes 524416 | tf_op jit(solution)/shard_map/finish/pallas_call | solution.py:38
  (1 shorter events, 0.0 us)
Async XLA Ops:
  0.6 9.0 %collective-permute-start = (bf16[1,128,512]{2,1,0:T(8,128)(2,1)}, bf16[1,128,512]{2,1,0:T(8,128)(2,1)S(1)}, u32[]{:S(2)}, u32[]{:S(2)}) collective-permute-start(bf16[1,128,512]{2,1,0:T(8,128)(2,1)} %k_in.1), channel_id=1, source_target_pairs={{0,1},{1,2},{2,3},{3,0},{4,5},{5,6},{6,7},{7,4},{8,9},{9,10},{10,1... | collective-permute-start | bytes 393224 | tf_op jit(solution)/shard_map/ppermute | solution.py:167
  3.7 9.9 %collective-permute-start.1 = (bf16[1,128,512]{2,1,0:T(8,128)(2,1)}, bf16[1,128,512]{2,1,0:T(8,128)(2,1)S(1)}, u32[]{:S(2)}, u32[]{:S(2)}) collective-permute-start(bf16[1,128,512]{2,1,0:T(8,128)(2,1)} %v_in.1), channel_id=1, source_target_pairs={{0,1},{1,2},{2,3},{4,5},{5,6},{6,7},{8,9},{9,10},{10,11},{12,13},{... | collective-permute-start | bytes 393224 | tf_op jit(solution)/shard_map/ppermute | solution.py:172
  11.1 11.1 %collective-permute-start.3 = (bf16[1,128,512]{2,1,0:T(8,128)(2,1)S(1)}, bf16[1,128,512]{2,1,0:T(8,128)(2,1)S(1)}, u32[]{:S(2)}, u32[]{:S(2)}) collective-permute-start(bf16[1,128,512]{2,1,0:T(8,128)(2,1)S(1)} %get-tuple-element.35), channel_id=1, source_target_pairs={{0,3},{1,0},{2,1},{3,2},{4,7},{5,4},{6,5},{7,6},{8,11},{9,8},{10,9... | collective-permute-start | bytes 393224 | tf_op jit(solution)/shard_map/ppermute | solution.py:167
  14.9 10.0 %all-to-all-start = ((f32[32,1,16]{2,1,0:T(1,128)}), f32[32,1,16]{2,1,0:T(1,128)S(1)}, u32[]{:S(2)}, u32[]{:S(2)}) async-start(f32[32,1,16]{2,1,0:T(1,128)} %bitcast.2), calls=%async_computation | async-start | bytes 32768 | tf_op jit(solution)/shard_map/all_to_all | solution.py:210
  17.8 7.2 %collective-permute-start.2 = (bf16[1,128,512]{2,1,0:T(8,128)(2,1)S(1)}, bf16[1,128,512]{2,1,0:T(8,128)(2,1)S(1)}, u32[]{:S(2)}, u32[]{:S(2)}) collective-permute-start(bf16[1,128,512]{2,1,0:T(8,128)(2,1)S(1)} %get-tuple-element.32), channel_id=1, source_target_pairs={{0,3},{1,0},{2,1},{3,2},{4,7},{5,4},{6,5},{7,6},{8,11},{9,8},{10,9... | collective-permute-start | bytes 393224 | tf_op jit(solution)/shard_map/ppermute | solution.py:167

commit v6 on v5

--- a/solution.py
+++ b/solution.py
@@ -58,9 +58,9 @@
 
 
 def split(own, value):
-    zero = jnp.zeros_like(value)
-    return jnp.concatenate(
-        [jnp.where(own, value, zero), jnp.where(own, zero, value)], axis=0).astype(jnp.bfloat16)
+    value = value.astype(jnp.bfloat16)
+    part = value * own.astype(jnp.float32).astype(jnp.bfloat16)
+    return jnp.concatenate([part, value - part], axis=0)
 
 
 def groups(ref):
@@ -98,62 +98,82 @@
 def softmax_kernel(bias_ref, sink_ref, q_ref, do_ref, hk_ref, s_ref, p_ref, sp_ref, dv_ref, back_ref):
     _, rows, _ = q_ref.shape
     own = own_mask(rows, GROUP * rows)
-    for b, heads, kv, cols in groups(q_ref):
+    parts = list(groups(q_ref))
+    for b, heads, kv, cols in parts:
         before = dot(hk_ref[b, :, kv], stacked(q_ref, b, heads), ((1,), (1,))) + bias_ref[...]
-        score = jnp.where(own, s_ref[b, :, cols], before) * (SCALE * LOG2E)
-        sink = sink_ref[:, cols]
-        top = jnp.maximum(jnp.max(score, axis=0, keepdims=True), sink)
-        weight = jnp.exp2(score - top)
-        sink_weight = jnp.exp2(sink - top)
-        scale = 1.0 / (jnp.sum(weight, axis=0, keepdims=True) + sink_weight)
-        prob = weight * scale
+        p_ref[b, :, cols] = jnp.where(own, s_ref[b, :, cols], before) * (SCALE * LOG2E)
+    tops = [jnp.maximum(jnp.max(p_ref[b, :, cols], axis=0, keepdims=True), sink_ref[:, cols])
+            for b, _, _, cols in parts]
+    sums = []
+    for (b, _, _, cols), top in zip(parts, tops):
+        weight = jnp.exp2(p_ref[b, :, cols] - top)
+        p_ref[b, :, cols] = weight
+        sums.append(jnp.sum(weight, axis=0, keepdims=True))
+    scales = []
+    for (b, _, _, cols), top, total in zip(parts, tops, sums):
+        sink_weight = jnp.exp2(sink_ref[:, cols] - top)
+        scales.append(1.0 / (total + sink_weight))
+        sp_ref[b, :, cols] = sink_weight * scales[-1]
+    probs = []
+    for (b, _, _, cols), scale in zip(parts, scales):
+        prob = p_ref[b, :, cols] * scale
         p_ref[b, :, cols] = prob
-        sp_ref[b, :, cols] = sink_weight * scale
-        grad_value = dot(split(own, prob), stacked(do_ref, b, heads), ((1,), (0,)))
+        probs.append(split(own, prob))
+    for (b, heads, kv, cols), prob in zip(parts, probs):
+        grad_value = dot(prob, stacked(do_ref, b, heads), ((1,), (0,)))
         dv_ref[b, :, kv] = grad_value[:rows]
         back_ref[b, :, kv] = grad_value[rows:].astype(jnp.bfloat16)
 
 
-def grad_kernel(q_ref, do_ref, k_ref, hk_ref, hv_ref, p_ref, sp_ref, dp_ref,
-                terms_out, dq_ref, dk_ref, back_ref, gp_ref, delta_ref, sink_ref, terms_ref, sem):
+def grad_kernel(q_ref, do_ref, hv_ref, p_ref, sp_ref, dp_ref,
+                terms_out, ds_ref, dk_ref, back_ref, gp_ref, sink_ref, terms_ref, sem):
     _, rows, _ = q_ref.shape
     own = own_mask(rows, GROUP * rows)
-    sink_ref[...] = jnp.zeros_like(sink_ref)
-    for b, heads, kv, cols in groups(do_ref):
+    parts = list(groups(q_ref))
+    for b, heads, kv, cols in parts:
         before = dot(hv_ref[b, :, kv], stacked(do_ref, b, heads), ((1,), (1,)))
-        grad_prob = jnp.where(own, dp_ref[b, :, cols], before)
-        gp_ref[b, :, cols] = grad_prob
-        delta = jnp.sum(p_ref[b, :, cols] * grad_prob, axis=0, keepdims=True)
-        delta_ref[b, :, cols] = delta
+        gp_ref[b, :, cols] = jnp.where(own, dp_ref[b, :, cols], before)
+    deltas = [jnp.sum(p_ref[b, :, cols] * gp_ref[b, :, cols], axis=0, keepdims=True) for b, _, _, cols in parts]
+    for (b, heads, _, cols), delta in zip(parts, deltas):
         terms = sp_ref[b, :, cols] * delta
         for n, h in enumerate(heads):
-            sink_ref[h:h + 1, :] += terms[:, n * rows:(n + 1) * rows]
-    ones = jnp.ones((terms_ref.shape[0], rows), jnp.bfloat16)
+            term = terms[:, n * rows:(n + 1) * rows]
+            sink_ref[h:h + 1, :] = term if b == 0 else sink_ref[h:h + 1, :] + term
     terms = sink_ref[...]
     high = terms.astype(jnp.bfloat16)
     rest = terms - high.astype(jnp.float32)
     middle = rest.astype(jnp.bfloat16)
     low = (rest - middle.astype(jnp.float32)).astype(jnp.bfloat16)
-    terms_ref[...] = sum(dot(ones, part, ((1,), (1,))) for part in (low, middle, high))
+    split_terms = jnp.concatenate([low, middle, high], axis=1)
+    ones = jnp.ones((terms_ref.shape[0], split_terms.shape[1]), jnp.bfloat16)
+    terms_ref[...] = dot(ones, split_terms, ((1,), (1,)))
     copy = pltpu.make_async_copy(terms_ref, terms_out, sem)
     copy.start()
-    for b, heads, kv, cols in groups(q_ref):
-        dscores = split(own, p_ref[b, :, cols] * (gp_ref[b, :, cols] - delta_ref[b, :, cols]))
-        grad_key = dot(dscores, stacked(q_ref, b, heads), ((1,), (0,))) * SCALE
+    for (b, _, _, cols), delta in zip(parts, deltas):
+        ds_ref[b, :, cols] = split(own, p_ref[b, :, cols] * (gp_ref[b, :, cols] - delta))
+    for b, heads, kv, cols in parts:
+        grad_key = dot(ds_ref[b, :, cols], stacked(q_ref, b, heads), ((1,), (0,))) * SCALE
         dk_ref[b, :, kv] = grad_key[:rows]
         back_ref[b, :, kv] = grad_key[rows:].astype(jnp.bfloat16)
-        key = jnp.concatenate([k_ref[b, :, kv], hk_ref[b, :, kv]], axis=0)
-        grad_query = (dot(dscores, key, ((0,), (0,))) * SCALE).astype(jnp.bfloat16)
+    copy.wait()
+
+
+def query_kernel(k_ref, hk_ref, ds_ref, dq_ref):
+    _, rows, _ = dq_ref.shape
+    parts = list(groups(dq_ref))
+    keys = [jnp.concatenate([k_ref[b, :, kv], hk_ref[b, :, kv]], axis=0) for b, _, kv, _ in parts]
+    products = [dot(ds_ref[b, :, cols], key, ((0,), (0,))) for (b, _, _, cols), key in zip(parts, keys)]
+    for (b, heads, _, _), product in zip(parts, products):
         for n, h in enumerate(heads):
-            dq_ref[b, :, h * HEAD:(h + 1) * HEAD] = grad_query[n * rows:(n + 1) * rows]
-    copy.wait()
+            dq_ref[b, :, h * HEAD:(h + 1) * HEAD] = (product[n * rows:(n + 1) * rows] * SCALE).astype(jnp.bfloat16)
 
 
 def join_kernel(own_ref, back_ref, out_ref):
     out_ref[...] = (own_ref[...] + back_ref[...].astype(jnp.float32)).astype(jnp.bfloat16)
 
 
-def total_kernel(factor, terms_ref, _, total_ref):
+def total_kernel(factor, terms_ref, *refs):
+    total_ref = refs[-1]
     total_ref[...] = jnp.sum(terms_ref[...], axis=0, keepdims=True) * factor
 
 
@@ -198,21 +218,22 @@
          pltpu.VMEM(keys.shape, bf16)),
         [VMEM] * 6, (bias, sink, q, do, halo_keys, score), 3 * product)
     back_values = ring(back_values, "ctx", -1)
-    terms, grad_query, own_keys, back_keys = call(
+    terms, dscores, own_keys, back_keys = call(
         grad_kernel, "grad",
-        (struct((dp * ctx, HEADS), f32), pltpu.VMEM(queries.shape, bf16), pltpu.VMEM(keys.shape, f32),
+        (struct((dp * ctx, HEADS), f32), pltpu.VMEM((batch, 2 * rows, HEADS * rows), bf16), pltpu.VMEM(keys.shape, f32),
          pltpu.VMEM(keys.shape, bf16)),
-        [VMEM] * 8, (q, do, k, halo_keys, halo_values, prob, sink_prob, grad_prob), 5 * product,
-        scratch=[pltpu.VMEM(square.shape, f32), pltpu.VMEM(line.shape, f32), pltpu.VMEM((HEADS, rows), f32),
+        [VMEM] * 6, (q, do, halo_values, prob, sink_prob, grad_prob), 3 * product,
+        scratch=[pltpu.VMEM(square.shape, f32), pltpu.VMEM((HEADS, rows), f32),
                  pltpu.VMEM((dp * ctx, HEADS), f32), pltpu.SemaphoreType.DMA],
         out_specs=(HBM, VMEM, VMEM, VMEM))
     back_keys = ring(back_keys, "ctx", -1)
     terms = lax.all_to_all(terms, ("dp", "ctx"), 0, 0, tiled=True)
+    grad_query, = call(query_kernel, "query", (struct(queries.shape, bf16),), [VMEM] * 3, (k, halo_keys, dscores), 2 * product)
     grad_values, = call(join_kernel, "join", (kv_bf16,), [VMEM] * 2, (own_values, back_values), 0)
     factor = -1.0 / (dp * batch * ctx * rows) ** 0.5
     total, = call(
-        functools.partial(total_kernel, factor), "total", (struct((1, HEADS), f32),), [VMEM, HBM],
-        (terms, grad_values), 10 ** 10)
+        functools.partial(total_kernel, factor), "total", (struct((1, HEADS), f32),), [VMEM, HBM, HBM],
+        (terms, grad_values, grad_query), 10 ** 10)
     grad_keys, sink_grad = call(
         finish_kernel, "finish", (kv_bf16, struct((1, HEADS), f32)), [VMEM] * 3, (own_keys, back_keys, total), 0)
     return grad_query, grad_keys, grad_values, sink_grad.reshape(HEADS)

time: 25.9 us -> 25.5 us (0.985)
  local copies, waits for them, and re-layouts: 0.79 us -> 0 us
  Pallas kernels: 6.59 us -> 7.3 us
  waiting for transfers between devices: 2.06 us -> 1.56 us
    unnamed x1 -> x0, local copies, waits for them, and re-layouts: 0.79 us -> none
    pallas_call x6 -> x7, Pallas kernels: 6.59 us -> 7.3 us  [call(): pl.pallas_call(kernel, out_shape=out_shape, in_specs=in_specs, out_specs=...]
    all_to_all x1, waiting for transfers between devices: 2.05 us -> 1.55 us  [body(): terms = lax.all_to_all(terms, ('dp', 'ctx'), 0, 0, tiled=True)]
  transfers between devices with their start and end apart: 5 -> 5, of which waited for: 1 -> 1; matrix products, arithmetic and copies ran while one was open for 3% -> 0% of each run, Pallas kernels for 23% -> 26%
where the time goes in v6:
time: 25.5 us; the launch traced here: 25.4 us
  starting transfers between devices  15.8 us (62%)
  Pallas kernels  7.3 us (29%)
  waiting for transfers between devices  1.56 us (6%)
  between operations  0.69 us (3%)
    ppermute x3, starting transfers between devices, ring(): lax.ppermute(value, axis, [(i, (i + steps) % count) for i in range(count)])  9.26 us
    pallas_call x7, Pallas kernels, call(): pl.pallas_call(kernel, out_shape=out_shape, in_specs=in_specs, out_specs=...  7.3 us
    ppermute x1, starting transfers between devices, shift(): return lax.ppermute(value, axis, [(i, i + 1) for i in range(count - 1)])  3.48 us
    all_to_all x1, starting transfers between devices, body(): terms = lax.all_to_all(terms, ('dp', 'ctx'), 0, 0, tiled=True)  3.07 us
    all_to_all x1, waiting for transfers between devices, body(): terms = lax.all_to_all(terms, ('dp', 'ctx'), 0, 0, tiled=True)  1.55 us
  transfers between devices with their start and end apart: 5, of which 1 were waited for; matrix products, arithmetic and copies ran while one was open for 0% of the time, Pallas kernels for 26%

profile of v6, /device:TPU:0, one launch (start us, length us, event | category | flops | bytes accessed | tf_op | source)
XLA Modules:
  0.0 25.4 jit_solution(5726813304540793903)
XLA Ops:
  0.6 3.1 %collective-permute-start = (bf16[1,128,512]{2,1,0:T(8,128)(2,1)}, bf16[1,128,512]{2,1,0:T(8,128)(2,1)S(1)}, u32[]{:S(2)}, u32[]{:S(2)}) collective-permute-start(bf16[1,128,512]{2,1,0:T(8,128)(2,1)} %k_in.1), channel_id=1, source_target_pairs={{0,1},{1,2},{2,3},{3,0},{4,5},{5,6},{6,7},{7,4},{8,9},{9,10},{10,1... | collective-permute-start | bytes 393224 | tf_op jit(solution)/shard_map/ppermute | solution.py:187
  3.7 3.5 %collective-permute-start.1 = (bf16[1,128,512]{2,1,0:T(8,128)(2,1)}, bf16[1,128,512]{2,1,0:T(8,128)(2,1)S(1)}, u32[]{:S(2)}, u32[]{:S(2)}) collective-permute-start(bf16[1,128,512]{2,1,0:T(8,128)(2,1)} %v_in.1), channel_id=1, source_target_pairs={{0,1},{1,2},{2,3},{4,5},{5,6},{6,7},{8,9},{9,10},{10,11},{12,13},{... | collective-permute-start | bytes 393224 | tf_op jit(solution)/shard_map/ppermute | solution.py:192
  7.2 2.4 %load.1 = (bf16[1,128,2048]{2,1,0:T(8,128)(2,1)S(1)}, bf16[1,128,512]{2,1,0:T(8,128)(2,1)S(1)}, bf16[1,128,512]{2,1,0:T(8,128)(2,1)}, bf16[1,128,2048]{2,1,0:T(8...) custom-call(s32[1]{0:T(128)} %bitcast.first_ref, ...), custom_call_target="tpu_custom_call" | custom-call | flops 134217728 | bytes 4728900 | tf_op jit(solution)/shard_map/load/pallas_call | solution.py:38
  9.6 0.0 collective-permute-done.hk_ref
  9.7 1.0 %softmax.1 = (f32[1,128,2048]{2,1,0:T(8,128)S(1)}, f32[1,1,2048]{2,1,0:T(1,128)S(1)}, f32[1,128,512]{2,1,0:T(8,128)S(1)}, bf16[1,128,512]{2,1,0:T(8,128)(2,1)S(1)}) custom-call(f32[1,512]{1,0:T(1,128)S(1)} %get-tuple-element.24.bias_ref, f32[1,2048]{1,0:T(1,128)S(1)} %get-tuple-element.25.sink_ref, bf16[1,128,2048]{2,1,0:T(8,128)(2,1)S(1)} %get-tuple-element.22.q_ref, ...), custom_call_target="tpu_custom_call" | custom-call | flops 201326592 | bytes 3688448 | tf_op jit(solution)/shard_map/softmax/pallas_call | solution.py:38
  10.7 2.5 %collective-permute-start.3 = (bf16[1,128,512]{2,1,0:T(8,128)(2,1)S(1)}, bf16[1,128,512]{2,1,0:T(8,128)(2,1)S(1)}, u32[]{:S(2)}, u32[]{:S(2)}) collective-permute-start(bf16[1,128,512]{2,1,0:T(8,128)(2,1)S(1)} %get-tuple-element.35), channel_id=1, source_target_pairs={{0,3},{1,0},{2,1},{3,2},{4,7},{5,4},{6,5},{7,6},{8,11},{9,8},{10,9... | collective-permute-start | bytes 393224 | tf_op jit(solution)/shard_map/ppermute | solution.py:187
  13.2 0.0 collective-permute-done.1.hv_ref
  13.2 1.2 %grad.1 = (f32[32,16]{1,0:T(8,128)}, bf16[1,256,2048]{2,1,0:T(8,128)(2,1)S(1)}, f32[1,128,512]{2,1,0:T(8,128)S(1)}, bf16[1,128,512]{2,1,0:T(8,128)(2,1)S(1)}) custom-call(bf16[1,128,2048]{2,1,0:T(8,128)(2,1)S(1)} %get-tuple-element.22.q_ref, bf16[1,128,2048]{2,1,0:T(8,128)(2,1)S(1)} %get-tuple-element.23.do_ref, ...), custom_call_target="tpu_custom_call" | custom-call | flops 201326592 | bytes 4728832 | tf_op jit(solution)/shard_map/grad/pallas_call | solution.py:38
  14.4 3.1 %all-to-all-start = ((f32[32,1,16]{2,1,0:T(1,128)}), f32[32,1,16]{2,1,0:T(1,128)S(1)}, u32[]{:S(2)}, u32[]{:S(2)}) async-start(f32[32,1,16]{2,1,0:T(1,128)} %bitcast.2), calls=%async_computation | async-start | bytes 32768 | tf_op jit(solution)/shard_map/all_to_all | solution.py:230
  17.5 3.7 %collective-permute-start.2 = (bf16[1,128,512]{2,1,0:T(8,128)(2,1)S(1)}, bf16[1,128,512]{2,1,0:T(8,128)(2,1)S(1)}, u32[]{:S(2)}, u32[]{:S(2)}) collective-permute-start(bf16[1,128,512]{2,1,0:T(8,128)(2,1)S(1)} %get-tuple-element.32), channel_id=1, source_target_pairs={{0,3},{1,0},{2,1},{3,2},{4,7},{5,4},{6,5},{7,6},{8,11},{9,8},{10,9... | collective-permute-start | bytes 393224 | tf_op jit(solution)/shard_map/ppermute | solution.py:187
  21.1 1.3 %query.1.refs_1_ = bf16[1,128,2048]{2,1,0:T(8,128)(2,1)} custom-call(bf16[1,128,512]{2,1,0:T(8,128)(2,1)S(1)} %get-tuple-element.21.k_ref, bf16[1,128,512]{2,1,0:T(8,128)(2,1)S(1)} %collective-permute-done.hk_ref, bf16[1,256,2048]{2,1,0:T(8,128)(2,1)S(1)} %get-tuple-element.30.ds_ref), custom_call_target="tpu_custom_call" | custom-call | flops 134217728 | bytes 1835008 | tf_op jit(solution)/shard_map/query/pallas_call | solution.py:38
  22.4 0.0 collective-permute-done.3.back_ref
  22.4 0.7 %join.1.refs_0_ = bf16[1,128,512]{2,1,0:T(8,128)(2,1)} custom-call(f32[1,128,512]{2,1,0:T(8,128)S(1)} %get-tuple-element.34.own_ref, bf16[1,128,512]{2,1,0:T(8,128)(2,1)S(1)} %collective-permute-done.3.back_ref), custom_call_target="tpu_custom_call" | custom-call | bytes 524288 | tf_op jit(solution)/shard_map/join/pallas_call | solution.py:38
  23.1 1.5 %all-to-all-done = f32[32,1,16]{2,1,0:T(1,128)S(1)} async-done(((f32[32,1,16]{2,1,0:T(1,128)}), f32[32,1,16]{2,1,0:T(1,128)S(1)}, u32[]{:S(2)}, u32[]{:S(2)}) %all-to-all-start) | async-done | bytes 2080 | tf_op jit(solution)/shard_map/all_to_all | solution.py:230
  24.7 0.0 collective-permute-done.2.back_ref
  24.7 0.7 %finish.1 = (bf16[1,128,512]{2,1,0:T(8,128)(2,1)}, f32[1,16]{1,0:T(1,128)}) custom-call(f32[1,128,512]{2,1,0:T(8,128)S(1)} %get-tuple-element.31.own_ref, bf16[1,128,512]{2,1,0:T(8,128)(2,1)S(1)} %collective-permute-done.2.back_ref, f32[1,16]{1,0:T(1,128)S(1)} %total.1.total_ref), custom_call_target="tpu_custom_call" | custom-call | bytes 524416 | tf_op jit(solution)/shard_map/finish/pallas_call | solution.py:38
  (1 shorter events, 0.0 us)
Async XLA Ops:
  0.6 9.0 %collective-permute-start = (bf16[1,128,512]{2,1,0:T(8,128)(2,1)}, bf16[1,128,512]{2,1,0:T(8,128)(2,1)S(1)}, u32[]{:S(2)}, u32[]{:S(2)}) collective-permute-start(bf16[1,128,512]{2,1,0:T(8,128)(2,1)} %k_in.1), channel_id=1, source_target_pairs={{0,1},{1,2},{2,3},{3,0},{4,5},{5,6},{6,7},{7,4},{8,9},{9,10},{10,1... | collective-permute-start | bytes 393224 | tf_op jit(solution)/shard_map/ppermute | solution.py:187
  3.7 9.5 %collective-permute-start.1 = (bf16[1,128,512]{2,1,0:T(8,128)(2,1)}, bf16[1,128,512]{2,1,0:T(8,128)(2,1)S(1)}, u32[]{:S(2)}, u32[]{:S(2)}) collective-permute-start(bf16[1,128,512]{2,1,0:T(8,128)(2,1)} %v_in.1), channel_id=1, source_target_pairs={{0,1},{1,2},{2,3},{4,5},{5,6},{6,7},{8,9},{9,10},{10,11},{12,13},{... | collective-permute-start | bytes 393224 | tf_op jit(solution)/shard_map/ppermute | solution.py:192
  10.7 11.8 %collective-permute-start.3 = (bf16[1,128,512]{2,1,0:T(8,128)(2,1)S(1)}, bf16[1,128,512]{2,1,0:T(8,128)(2,1)S(1)}, u32[]{:S(2)}, u32[]{:S(2)}) collective-permute-start(bf16[1,128,512]{2,1,0:T(8,128)(2,1)S(1)} %get-tuple-element.35), channel_id=1, source_target_pairs={{0,3},{1,0},{2,1},{3,2},{4,7},{5,4},{6,5},{7,6},{8,11},{9,8},{10,9... | collective-permute-start | bytes 393224 | tf_op jit(solution)/shard_map/ppermute | solution.py:187
  14.4 10.3 %all-to-all-start = ((f32[32,1,16]{2,1,0:T(1,128)}), f32[32,1,16]{2,1,0:T(1,128)S(1)}, u32[]{:S(2)}, u32[]{:S(2)}) async-start(f32[32,1,16]{2,1,0:T(1,128)} %bitcast.2), calls=%async_computation | async-start | bytes 32768 | tf_op jit(solution)/shard_map/all_to_all | solution.py:230
  17.5 7.2 %collective-permute-start.2 = (bf16[1,128,512]{2,1,0:T(8,128)(2,1)S(1)}, bf16[1,128,512]{2,1,0:T(8,128)(2,1)S(1)}, u32[]{:S(2)}, u32[]{:S(2)}) collective-permute-start(bf16[1,128,512]{2,1,0:T(8,128)(2,1)S(1)} %get-tuple-element.32), channel_id=1, source_target_pairs={{0,3},{1,0},{2,1},{3,2},{4,7},{5,4},{6,5},{7,6},{8,11},{9,8},{10,9... | collective-permute-start | bytes 393224 | tf_op jit(solution)/shard_map/ppermute | solution.py:187

commit v7 on v6

--- a/solution.py
+++ b/solution.py
@@ -17,7 +17,6 @@
 LOG2E = 1.4426950408889634
 VMEM = pl.BlockSpec(memory_space=pltpu.VMEM)
 SMEM = pl.BlockSpec(memory_space=pltpu.SMEM)
-ANY = pl.BlockSpec(memory_space=pl.ANY)
 HBM = pl.BlockSpec(memory_space=pltpu.HBM)
 
 
@@ -72,7 +71,7 @@
 
 
 def load_kernel(first_ref, sinks_in, q_in, k_in, v_in, do_in,
-                q_ref, k_ref, v_ref, do_ref, s_ref, dp_ref, bias_ref, sink_ref, sinks_ref, sems):
+                q_ref, k_ref, do_ref, s_ref, dp_ref, bias_ref, sink_ref, v_ref, sinks_ref, sems):
     _, rows, _ = q_ref.shape
     copies = [
         pltpu.make_async_copy(source, target, sems.at[n])
@@ -196,7 +195,7 @@
     batch, rows, width = queries.shape
     kv_width = keys.shape[2]
     dp, ctx = lax.axis_size("dp"), lax.axis_size("ctx")
-    assert rows == WINDOW and dp & (dp - 1) == 0 and ctx & (ctx - 1) == 0
+    assert rows == WINDOW
     bf16, f32 = jnp.bfloat16, jnp.float32
     square = struct((batch, rows, HEADS * rows), f32)
     line = struct((batch, 1, HEADS * rows), f32)
@@ -206,12 +205,12 @@
     first = (lax.axis_index("ctx") == 0).astype(jnp.int32).reshape(1)
     halo_keys = ring(keys, "ctx", 1)
     halo_values = shift(values, "ctx")
-    q, k, v, do, score, grad_prob, bias, sink = call(
+    q, k, do, score, grad_prob, bias, sink = call(
         load_kernel, "load",
-        (struct(queries.shape, bf16), kv_bf16, kv_bf16, struct(dout.shape, bf16), square, square,
+        (struct(queries.shape, bf16), kv_bf16, struct(dout.shape, bf16), square, square,
          struct((1, GROUP * rows), f32), struct((1, HEADS * rows), f32)),
         [SMEM] + [HBM] * 5, (first, sinks, queries, keys, values, dout), 2 * product,
-        scratch=[pltpu.SMEM((HEADS,), f32), pltpu.SemaphoreType.DMA((5,))])
+        scratch=[pltpu.VMEM(values.shape, bf16), pltpu.SMEM((HEADS,), f32), pltpu.SemaphoreType.DMA((5,))])
     prob, sink_prob, own_values, back_values = call(
         softmax_kernel, "softmax",
         (pltpu.VMEM(square.shape, f32), pltpu.VMEM(line.shape, f32), pltpu.VMEM(keys.shape, f32),
@@ -220,7 +219,7 @@
     back_values = ring(back_values, "ctx", -1)
     terms, dscores, own_keys, back_keys = call(
         grad_kernel, "grad",
-        (struct((dp * ctx, HEADS), f32), pltpu.VMEM((batch, 2 * rows, HEADS * rows), bf16), pltpu.VMEM(keys.shape, f32),
+        (pltpu.HBM((dp * ctx, HEADS), f32), pltpu.VMEM((batch, 2 * rows, HEADS * rows), bf16), pltpu.VMEM(keys.shape, f32),
          pltpu.VMEM(keys.shape, bf16)),
         [VMEM] * 6, (q, do, halo_values, prob, sink_prob, grad_prob), 3 * product,
         scratch=[pltpu.VMEM(square.shape, f32), pltpu.VMEM((HEADS, rows), f32),

time: 25.5 us -> 25.5 us (level)
  Pallas kernels: 7.3 us -> 6.6 us
  waiting for transfers between devices: 1.56 us -> 1.99 us
    pallas_call x7, Pallas kernels: 7.3 us -> 6.6 us  [call(): pl.pallas_call(kernel, out_shape=out_shape, in_specs=in_specs, out_specs=...]
    ppermute x3, waiting for transfers between devices: 0.01 us -> 0.45 us  [ring(): lax.ppermute(value, axis, [(i, (i + steps) % count) for i in range(count)])]
  transfers between devices with their start and end apart: 5 -> 5, of which waited for: 1 -> 2; matrix products, arithmetic and copies ran while one was open for 0% -> 0% of each run, Pallas kernels for 26% -> 23%
where the time goes in v7:
time: 25.5 us; the launch traced here: 25.3 us
  starting transfers between devices  16 us (63%)
  Pallas kernels  6.6 us (26%)
  waiting for transfers between devices  1.99 us (8%)
  between operations  0.69 us (3%)
    ppermute x3, starting transfers between devices, ring(): lax.ppermute(value, axis, [(i, (i + steps) % count) for i in range(count)])  9.47 us
    pallas_call x7, Pallas kernels, call(): pl.pallas_call(kernel, out_shape=out_shape, in_specs=in_specs, out_specs=...  6.6 us
    ppermute x1, starting transfers between devices, shift(): return lax.ppermute(value, axis, [(i, i + 1) for i in range(count - 1)])  3.48 us
    all_to_all x1, starting transfers between devices, body(): terms = lax.all_to_all(terms, ('dp', 'ctx'), 0, 0, tiled=True)  3.09 us
    all_to_all x1, waiting for transfers between devices, body(): terms = lax.all_to_all(terms, ('dp', 'ctx'), 0, 0, tiled=True)  1.53 us
  transfers between devices with their start and end apart: 5, of which 2 were waited for; matrix products, arithmetic and copies ran while one was open for 0% of the time, Pallas kernels for 23%

profile of v7, /device:TPU:0, one launch (start us, length us, event | category | flops | bytes accessed | tf_op | source)
XLA Modules:
  0.0 25.3 jit_solution(10568366314384501234)
XLA Ops:
  0.6 3.1 %collective-permute-start = (bf16[1,128,512]{2,1,0:T(8,128)(2,1)}, bf16[1,128,512]{2,1,0:T(8,128)(2,1)S(1)}, u32[]{:S(2)}, u32[]{:S(2)}) collective-permute-start(bf16[1,128,512]{2,1,0:T(8,128)(2,1)} %k_in.1), channel_id=1, source_target_pairs={{0,1},{1,2},{2,3},{3,0},{4,5},{5,6},{6,7},{7,4},{8,9},{9,10},{10,1... | collective-permute-start | bytes 393224 | tf_op jit(solution)/shard_map/ppermute | solution.py:186
  3.7 3.5 %collective-permute-start.1 = (bf16[1,128,512]{2,1,0:T(8,128)(2,1)}, bf16[1,128,512]{2,1,0:T(8,128)(2,1)S(1)}, u32[]{:S(2)}, u32[]{:S(2)}) collective-permute-start(bf16[1,128,512]{2,1,0:T(8,128)(2,1)} %v_in.1), channel_id=1, source_target_pairs={{0,1},{1,2},{2,3},{4,5},{5,6},{6,7},{8,9},{9,10},{10,11},{12,13},{... | collective-permute-start | bytes 393224 | tf_op jit(solution)/shard_map/ppermute | solution.py:191
  7.2 1.8 %load.1 = (bf16[1,128,2048]{2,1,0:T(8,128)(2,1)S(1)}, bf16[1,128,512]{2,1,0:T(8,128)(2,1)S(1)}, bf16[1,128,2048]{2,1,0:T(8,128)(2,1)S(1)}, f32[1,128,2048]{2,1,0...) custom-call(s32[1]{0:T(128)} %bitcast.first_ref, f32[16]{0:T(128)} %sinks_in.1, ...), custom_call_target="tpu_custom_call" | custom-call | flops 134217728 | bytes 4597828 | tf_op jit(solution)/shard_map/load/pallas_call | solution.py:37
  9.0 0.4 %collective-permute-done.hk_ref = bf16[1,128,512]{2,1,0:T(8,128)(2,1)S(1)} collective-permute-done((bf16[1,128,512]{2,1,0:T(8,128)(2,1)}, bf16[1,128,512]{2,1,0:T(8,128)(2,1)S(1)}, u32[]{:S(2)}, u32[]{:S(2)}) %collective-permute-start) | collective-permute-done | bytes 131104 | tf_op jit(solution)/shard_map/ppermute | solution.py:186
  9.4 1.0 %softmax.1 = (f32[1,128,2048]{2,1,0:T(8,128)S(1)}, f32[1,1,2048]{2,1,0:T(1,128)S(1)}, f32[1,128,512]{2,1,0:T(8,128)S(1)}, bf16[1,128,512]{2,1,0:T(8,128)(2,1)S(1)}) custom-call(f32[1,512]{1,0:T(1,128)S(1)} %get-tuple-element.24.bias_ref, f32[1,2048]{1,0:T(1,128)S(1)} %get-tuple-element.25.sink_ref, bf16[1,128,2048]{2,1,0:T(8,128)(2,1)S(1)} %get-tuple-element.22.q_ref, ...), custom_call_target="tpu_custom_call" | custom-call | flops 201326592 | bytes 3688448 | tf_op jit(solution)/shard_map/softmax/pallas_call | solution.py:37
  10.4 2.7 %collective-permute-start.3 = (bf16[1,128,512]{2,1,0:T(8,128)(2,1)S(1)}, bf16[1,128,512]{2,1,0:T(8,128)(2,1)S(1)}, u32[]{:S(2)}, u32[]{:S(2)}) collective-permute-start(bf16[1,128,512]{2,1,0:T(8,128)(2,1)S(1)} %get-tuple-element.35), channel_id=1, source_target_pairs={{0,3},{1,0},{2,1},{3,2},{4,7},{5,4},{6,5},{7,6},{8,11},{9,8},{10,9... | collective-permute-start | bytes 393224 | tf_op jit(solution)/shard_map/ppermute | solution.py:186
  13.2 0.0 collective-permute-done.1.hv_ref
  13.2 1.2 %grad.1 = (f32[32,16]{1,0:T(8,128)}, bf16[1,256,2048]{2,1,0:T(8,128)(2,1)S(1)}, f32[1,128,512]{2,1,0:T(8,128)S(1)}, bf16[1,128,512]{2,1,0:T(8,128)(2,1)S(1)}) custom-call(bf16[1,128,2048]{2,1,0:T(8,128)(2,1)S(1)} %get-tuple-element.22.q_ref, bf16[1,128,2048]{2,1,0:T(8,128)(2,1)S(1)} %get-tuple-element.23.do_ref, ...), custom_call_target="tpu_custom_call" | custom-call | flops 201326592 | bytes 4728832 | tf_op jit(solution)/shard_map/grad/pallas_call | solution.py:37
  14.3 3.1 %all-to-all-start = ((f32[32,1,16]{2,1,0:T(1,128)}), f32[32,1,16]{2,1,0:T(1,128)S(1)}, u32[]{:S(2)}, u32[]{:S(2)}) async-start(f32[32,1,16]{2,1,0:T(1,128)} %bitcast.7), calls=%async_computation | async-start | bytes 32768 | tf_op jit(solution)/shard_map/all_to_all | solution.py:229
  17.4 3.7 %collective-permute-start.2 = (bf16[1,128,512]{2,1,0:T(8,128)(2,1)S(1)}, bf16[1,128,512]{2,1,0:T(8,128)(2,1)S(1)}, u32[]{:S(2)}, u32[]{:S(2)}) collective-permute-start(bf16[1,128,512]{2,1,0:T(8,128)(2,1)S(1)} %get-tuple-element.32), channel_id=1, source_target_pairs={{0,3},{1,0},{2,1},{3,2},{4,7},{5,4},{6,5},{7,6},{8,11},{9,8},{10,9... | collective-permute-start | bytes 393224 | tf_op jit(solution)/shard_map/ppermute | solution.py:186
  21.1 1.3 %query.1.refs_1_ = bf16[1,128,2048]{2,1,0:T(8,128)(2,1)} custom-call(bf16[1,128,512]{2,1,0:T(8,128)(2,1)S(1)} %get-tuple-element.21.k_ref, bf16[1,128,512]{2,1,0:T(8,128)(2,1)S(1)} %collective-permute-done.hk_ref, bf16[1,256,2048]{2,1,0:T(8,128)(2,1)S(1)} %get-tuple-element.30.ds_ref), custom_call_target="tpu_custom_call" | custom-call | flops 134217728 | bytes 1835008 | tf_op jit(solution)/shard_map/query/pallas_call | solution.py:37
  22.4 0.0 collective-permute-done.3.back_ref
  22.4 0.7 %join.1.refs_0_ = bf16[1,128,512]{2,1,0:T(8,128)(2,1)} custom-call(f32[1,128,512]{2,1,0:T(8,128)S(1)} %get-tuple-element.34.own_ref, bf16[1,128,512]{2,1,0:T(8,128)(2,1)S(1)} %collective-permute-done.3.back_ref), custom_call_target="tpu_custom_call" | custom-call | bytes 524288 | tf_op jit(solution)/shard_map/join/pallas_call | solution.py:37
  23.1 1.5 %all-to-all-done = f32[32,1,16]{2,1,0:T(1,128)S(1)} async-done(((f32[32,1,16]{2,1,0:T(1,128)}), f32[32,1,16]{2,1,0:T(1,128)S(1)}, u32[]{:S(2)}, u32[]{:S(2)}) %all-to-all-start) | async-done | bytes 2080 | tf_op jit(solution)/shard_map/all_to_all | solution.py:229
  24.6 0.0 collective-permute-done.2.back_ref
  24.6 0.7 %finish.1 = (bf16[1,128,512]{2,1,0:T(8,128)(2,1)}, f32[1,16]{1,0:T(1,128)}) custom-call(f32[1,128,512]{2,1,0:T(8,128)S(1)} %get-tuple-element.31.own_ref, bf16[1,128,512]{2,1,0:T(8,128)(2,1)S(1)} %collective-permute-done.2.back_ref, f32[1,16]{1,0:T(1,128)S(1)} %total.1.total_ref), custom_call_target="tpu_custom_call" | custom-call | bytes 524416 | tf_op jit(solution)/shard_map/finish/pallas_call | solution.py:37
  (1 shorter events, 0.0 us)
Async XLA Ops:
  0.6 8.8 %collective-permute-start = (bf16[1,128,512]{2,1,0:T(8,128)(2,1)}, bf16[1,128,512]{2,1,0:T(8,128)(2,1)S(1)}, u32[]{:S(2)}, u32[]{:S(2)}) collective-permute-start(bf16[1,128,512]{2,1,0:T(8,128)(2,1)} %k_in.1), channel_id=1, source_target_pairs={{0,1},{1,2},{2,3},{3,0},{4,5},{5,6},{6,7},{7,4},{8,9},{9,10},{10,1... | collective-permute-start | bytes 393224 | tf_op jit(solution)/shard_map/ppermute | solution.py:186
  3.7 9.4 %collective-permute-start.1 = (bf16[1,128,512]{2,1,0:T(8,128)(2,1)}, bf16[1,128,512]{2,1,0:T(8,128)(2,1)S(1)}, u32[]{:S(2)}, u32[]{:S(2)}) collective-permute-start(bf16[1,128,512]{2,1,0:T(8,128)(2,1)} %v_in.1), channel_id=1, source_target_pairs={{0,1},{1,2},{2,3},{4,5},{5,6},{6,7},{8,9},{9,10},{10,11},{12,13},{... | collective-permute-start | bytes 393224 | tf_op jit(solution)/shard_map/ppermute | solution.py:191
  10.4 12.0 %collective-permute-start.3 = (bf16[1,128,512]{2,1,0:T(8,128)(2,1)S(1)}, bf16[1,128,512]{2,1,0:T(8,128)(2,1)S(1)}, u32[]{:S(2)}, u32[]{:S(2)}) collective-permute-start(bf16[1,128,512]{2,1,0:T(8,128)(2,1)S(1)} %get-tuple-element.35), channel_id=1, source_target_pairs={{0,3},{1,0},{2,1},{3,2},{4,7},{5,4},{6,5},{7,6},{8,11},{9,8},{10,9... | collective-permute-start | bytes 393224 | tf_op jit(solution)/shard_map/ppermute | solution.py:186
  14.3 10.3 %all-to-all-start = ((f32[32,1,16]{2,1,0:T(1,128)}), f32[32,1,16]{2,1,0:T(1,128)S(1)}, u32[]{:S(2)}, u32[]{:S(2)}) async-start(f32[32,1,16]{2,1,0:T(1,128)} %bitcast.7), calls=%async_computation | async-start | bytes 32768 | tf_op jit(solution)/shard_map/all_to_all | solution.py:229
  17.4 7.2 %collective-permute-start.2 = (bf16[1,128,512]{2,1,0:T(8,128)(2,1)S(1)}, bf16[1,128,512]{2,1,0:T(8,128)(2,1)S(1)}, u32[]{:S(2)}, u32[]{:S(2)}) collective-permute-start(bf16[1,128,512]{2,1,0:T(8,128)(2,1)S(1)} %get-tuple-element.32), channel_id=1, source_target_pairs={{0,3},{1,0},{2,1},{3,2},{4,7},{5,4},{6,5},{7,6},{8,11},{9,8},{10,9... | collective-permute-start | bytes 393224 | tf_op jit(solution)/shard_map/ppermute | solution.py:186

commit v8 on v7

--- a/solution.py
+++ b/solution.py
@@ -94,7 +94,14 @@
         sink_ref[:, h * rows:(h + 1) * rows] = jnp.full((1, rows), sinks_ref[h] * LOG2E, jnp.float32)
 
 
-def softmax_kernel(bias_ref, sink_ref, q_ref, do_ref, hk_ref, s_ref, p_ref, sp_ref, dv_ref, back_ref):
+def fetch_kernel(source, target, sem):
+    copy = pltpu.make_async_copy(source, target, sem)
+    copy.start()
+    copy.wait()
+
+
+def softmax_kernel(bias_ref, sink_ref, q_ref, do_ref, hk_ref, s_ref, dp_ref,
+                   low_ref, back_ref, g_ref, own_ref, p_ref):
     _, rows, _ = q_ref.shape
     own = own_mask(rows, GROUP * rows)
     parts = list(groups(q_ref))
@@ -108,35 +115,43 @@
         weight = jnp.exp2(p_ref[b, :, cols] - top)
         p_ref[b, :, cols] = weight
         sums.append(jnp.sum(weight, axis=0, keepdims=True))
-    scales = []
+    probs = []
+    sink_probs = []
     for (b, _, _, cols), top, total in zip(parts, tops, sums):
         sink_weight = jnp.exp2(sink_ref[:, cols] - top)
-        scales.append(1.0 / (total + sink_weight))
-        sp_ref[b, :, cols] = sink_weight * scales[-1]
-    probs = []
-    for (b, _, _, cols), scale in zip(parts, scales):
+        scale = 1.0 / (total + sink_weight)
+        sink_probs.append(sink_weight * scale)
         prob = p_ref[b, :, cols] * scale
         p_ref[b, :, cols] = prob
-        probs.append(split(own, prob))
+        low_ref[b, :, cols] = prob.astype(jnp.bfloat16)
+        probs.append(split(own, prob)[rows:])
     for (b, heads, kv, cols), prob in zip(parts, probs):
-        grad_value = dot(prob, stacked(do_ref, b, heads), ((1,), (0,)))
-        dv_ref[b, :, kv] = grad_value[:rows]
-        back_ref[b, :, kv] = grad_value[rows:].astype(jnp.bfloat16)
-
-
-def grad_kernel(q_ref, do_ref, hv_ref, p_ref, sp_ref, dp_ref,
-                terms_out, ds_ref, dk_ref, back_ref, gp_ref, sink_ref, terms_ref, sem):
-    _, rows, _ = q_ref.shape
-    own = own_mask(rows, GROUP * rows)
-    parts = list(groups(q_ref))
-    for b, heads, kv, cols in parts:
-        before = dot(hv_ref[b, :, kv], stacked(do_ref, b, heads), ((1,), (1,)))
-        gp_ref[b, :, cols] = jnp.where(own, dp_ref[b, :, cols], before)
-    deltas = [jnp.sum(p_ref[b, :, cols] * gp_ref[b, :, cols], axis=0, keepdims=True) for b, _, _, cols in parts]
-    for (b, heads, _, cols), delta in zip(parts, deltas):
-        terms = sp_ref[b, :, cols] * delta
+        back_ref[b, :, kv] = dot(prob, stacked(do_ref, b, heads), ((1,), (0,))).astype(jnp.bfloat16)
+    splits = []
+    for (b, _, _, cols), sink_prob in zip(parts, sink_probs):
+        prob = p_ref[b, :, cols] * sink_prob
+        own_ref[b, :, cols] = jnp.sum(jnp.where(own, prob * dp_ref[b, :, cols], 0.0), axis=0, keepdims=True)
+        prob = jnp.where(own, 0.0, prob)
+        high = prob.astype(jnp.bfloat16)
+        splits.append((high, (prob - high.astype(jnp.float32)).astype(jnp.bfloat16)))
+    for (b, heads, _, _), (high, low) in zip(parts, splits):
         for n, h in enumerate(heads):
-            term = terms[:, n * rows:(n + 1) * rows]
+            part = slice(n * rows, (n + 1) * rows)
+            grad = do_ref[b, :, h * HEAD:(h + 1) * HEAD]
+            g_ref[b, :, h * HEAD:(h + 1) * HEAD] = dot(
+                jnp.concatenate([high[:, part], low[:, part]], axis=1), jnp.concatenate([grad, grad], axis=0),
+                ((1,), (0,)))
+
+
+def terms_kernel(do_ref, hv_ref, g_ref, own_ref, dp_ref, terms_out, gp_ref, sink_ref, terms_ref, sem):
+    _, rows, _ = do_ref.shape
+    own = own_mask(rows, GROUP * rows)
+    parts = list(groups(do_ref))
+    for b, heads, kv, _ in parts:
+        value = hv_ref[b, :, kv].astype(jnp.float32)
+        for h in heads:
+            term = jnp.sum(value * g_ref[b, :, h * HEAD:(h + 1) * HEAD], axis=0, keepdims=True)
+            term += own_ref[b, :, h * rows:(h + 1) * rows]
             sink_ref[h:h + 1, :] = term if b == 0 else sink_ref[h:h + 1, :] + term
     terms = sink_ref[...]
     high = terms.astype(jnp.bfloat16)
@@ -148,18 +163,31 @@
     terms_ref[...] = dot(ones, split_terms, ((1,), (1,)))
     copy = pltpu.make_async_copy(terms_ref, terms_out, sem)
     copy.start()
+    for b, heads, kv, cols in parts:
+        before = dot(hv_ref[b, :, kv], stacked(do_ref, b, heads), ((1,), (1,)))
+        grad_prob = jnp.where(own, dp_ref[b, :, cols], before)
+        gp_ref[b, :, cols] = grad_prob
+    copy.wait()
+
+
+def keys_kernel(q_ref, p_ref, gp_ref, ds_ref, back_ref):
+    _, rows, _ = q_ref.shape
+    own = own_mask(rows, GROUP * rows)
+    parts = list(groups(q_ref))
+    deltas = [jnp.sum(p_ref[b, :, cols].astype(jnp.float32) * gp_ref[b, :, cols], axis=0, keepdims=True)
+              for b, _, _, cols in parts]
     for (b, _, _, cols), delta in zip(parts, deltas):
-        ds_ref[b, :, cols] = split(own, p_ref[b, :, cols] * (gp_ref[b, :, cols] - delta))
-    for b, heads, kv, cols in parts:
-        grad_key = dot(ds_ref[b, :, cols], stacked(q_ref, b, heads), ((1,), (0,))) * SCALE
-        dk_ref[b, :, kv] = grad_key[:rows]
-        back_ref[b, :, kv] = grad_key[rows:].astype(jnp.bfloat16)
-    copy.wait()
-
-
-def query_kernel(k_ref, hk_ref, ds_ref, dq_ref):
+        ds_ref[b, :, cols] = split(own, p_ref[b, :, cols].astype(jnp.float32) * (gp_ref[b, :, cols] - delta))
+    for b, heads, kv, cols in parts:
+        grad_key = dot(ds_ref[b, rows:, cols], stacked(q_ref, b, heads), ((1,), (0,))) * SCALE
+        back_ref[b, :, kv] = grad_key.astype(jnp.bfloat16)
+
+
+def query_kernel(q_ref, k_ref, hk_ref, ds_ref, dq_ref, dk_ref):
     _, rows, _ = dq_ref.shape
     parts = list(groups(dq_ref))
+    for b, heads, kv, cols in parts:
+        dk_ref[b, :, kv] = dot(ds_ref[b, :rows, cols], stacked(q_ref, b, heads), ((1,), (0,))) * SCALE
     keys = [jnp.concatenate([k_ref[b, :, kv], hk_ref[b, :, kv]], axis=0) for b, _, kv, _ in parts]
     products = [dot(ds_ref[b, :, cols], key, ((0,), (0,))) for (b, _, _, cols), key in zip(parts, keys)]
     for (b, heads, _, _), product in zip(parts, products):
@@ -167,8 +195,13 @@
             dq_ref[b, :, h * HEAD:(h + 1) * HEAD] = (product[n * rows:(n + 1) * rows] * SCALE).astype(jnp.bfloat16)
 
 
-def join_kernel(own_ref, back_ref, out_ref):
-    out_ref[...] = (own_ref[...] + back_ref[...].astype(jnp.float32)).astype(jnp.bfloat16)
+def values_kernel(do_ref, p_ref, back_ref, out_ref):
+    _, rows, _ = do_ref.shape
+    own = own_mask(rows, GROUP * rows)
+    for b, heads, kv, cols in groups(do_ref):
+        prob = split(own, p_ref[b, :, cols])[:rows]
+        grad_value = dot(prob, stacked(do_ref, b, heads), ((1,), (0,)))
+        out_ref[b, :, kv] = (grad_value + back_ref[b, :, kv].astype(jnp.float32)).astype(jnp.bfloat16)
 
 
 def total_kernel(factor, terms_ref, *refs):
@@ -177,7 +210,7 @@
 
 
 def finish_kernel(own_ref, back_ref, total_ref, out_ref, sink_ref):
-    join_kernel(own_ref, back_ref, out_ref)
+    out_ref[...] = (own_ref[...] + back_ref[...].astype(jnp.float32)).astype(jnp.bfloat16)
     sink_ref[...] = total_ref[...]
 
 
@@ -211,24 +244,28 @@
          struct((1, GROUP * rows), f32), struct((1, HEADS * rows), f32)),
         [SMEM] + [HBM] * 5, (first, sinks, queries, keys, values, dout), 2 * product,
         scratch=[pltpu.VMEM(values.shape, bf16), pltpu.SMEM((HEADS,), f32), pltpu.SemaphoreType.DMA((5,))])
-    prob, sink_prob, own_values, back_values = call(
+    prob, back_values, halves, own_terms = call(
         softmax_kernel, "softmax",
-        (pltpu.VMEM(square.shape, f32), pltpu.VMEM(line.shape, f32), pltpu.VMEM(keys.shape, f32),
-         pltpu.VMEM(keys.shape, bf16)),
-        [VMEM] * 6, (bias, sink, q, do, halo_keys, score), 3 * product)
+        (pltpu.VMEM(square.shape, bf16), pltpu.VMEM(keys.shape, bf16),
+         pltpu.VMEM(square.shape, f32), pltpu.VMEM(line.shape, f32)),
+        [VMEM] * 7, (bias, sink, q, do, halo_keys, score, grad_prob), 4 * product,
+        scratch=[pltpu.VMEM(square.shape, f32)])
     back_values = ring(back_values, "ctx", -1)
-    terms, dscores, own_keys, back_keys = call(
-        grad_kernel, "grad",
-        (pltpu.HBM((dp * ctx, HEADS), f32), pltpu.VMEM((batch, 2 * rows, HEADS * rows), bf16), pltpu.VMEM(keys.shape, f32),
-         pltpu.VMEM(keys.shape, bf16)),
-        [VMEM] * 6, (q, do, halo_values, prob, sink_prob, grad_prob), 3 * product,
-        scratch=[pltpu.VMEM(square.shape, f32), pltpu.VMEM((HEADS, rows), f32),
-                 pltpu.VMEM((dp * ctx, HEADS), f32), pltpu.SemaphoreType.DMA],
-        out_specs=(HBM, VMEM, VMEM, VMEM))
+    terms, grad_prob = call(
+        terms_kernel, "terms", (pltpu.HBM((dp * ctx, HEADS), f32), pltpu.VMEM(square.shape, f32)),
+        [VMEM] * 5, (do, halo_values, halves, own_terms, grad_prob), product,
+        scratch=[pltpu.VMEM((HEADS, rows), f32), pltpu.VMEM((dp * ctx, HEADS), f32), pltpu.SemaphoreType.DMA],
+        out_specs=(HBM, VMEM))
+    dscores, back_keys = call(
+        keys_kernel, "keys",
+        (pltpu.VMEM((batch, 2 * rows, HEADS * rows), bf16), pltpu.VMEM(keys.shape, bf16)),
+        [VMEM] * 3, (q, prob, grad_prob), 2 * product)
     back_keys = ring(back_keys, "ctx", -1)
     terms = lax.all_to_all(terms, ("dp", "ctx"), 0, 0, tiled=True)
-    grad_query, = call(query_kernel, "query", (struct(queries.shape, bf16),), [VMEM] * 3, (k, halo_keys, dscores), 2 * product)
-    grad_values, = call(join_kernel, "join", (kv_bf16,), [VMEM] * 2, (own_values, back_values), 0)
+    grad_query, own_keys = call(
+        query_kernel, "query", (struct(queries.shape, bf16), pltpu.VMEM(keys.shape, f32)), [VMEM] * 4,
+        (q, k, halo_keys, dscores), 3 * product)
+    grad_values, = call(values_kernel, "values", (kv_bf16,), [VMEM] * 3, (do, prob, back_values), product)
     factor = -1.0 / (dp * batch * ctx * rows) ** 0.5
     total, = call(
         functools.partial(total_kernel, factor), "total", (struct((1, HEADS), f32),), [VMEM, HBM, HBM],

time: 25.5 us -> 25.4 us (level)
  Pallas kernels: 6.6 us -> 7.56 us
  waiting for transfers between devices: 1.99 us -> 1.19 us
    all_to_all x1, waiting for transfers between devices: 1.53 us -> 0.57 us  [body(): terms = lax.all_to_all(terms, ('dp', 'ctx'), 0, 0, tiled=True)]
    pallas_call x7 -> x8, Pallas kernels: 6.6 us -> 7.56 us  [call(): pl.pallas_call(kernel, out_shape=out_shape, in_specs=in_specs, out_specs=...]
    all_to_all x1, starting transfers between devices: 3.09 us -> 2.82 us  [body(): terms = lax.all_to_all(terms, ('dp', 'ctx'), 0, 0, tiled=True)]
  transfers between devices with their start and end apart: 5 -> 5, of which waited for: 2 -> 3; matrix products, arithmetic and copies ran while one was open for 0% -> 0% of each run, Pallas kernels for 23% -> 27%
where the time goes in v8:
time: 25.4 us; the launch traced here: 25.2 us
  starting transfers between devices  15.8 us (62%)
  Pallas kernels  7.56 us (30%)
  waiting for transfers between devices  1.19 us (5%)
  between operations  0.69 us (3%)
    ppermute x3, starting transfers between devices, ring(): lax.ppermute(value, axis, [(i, (i + steps) % count) for i in range(count)])  9.47 us
    pallas_call x8, Pallas kernels, call(): pl.pallas_call(kernel, out_shape=out_shape, in_specs=in_specs, out_specs=...  7.56 us
    ppermute x1, starting transfers between devices, shift(): return lax.ppermute(value, axis, [(i, i + 1) for i in range(count - 1)])  3.48 us
    all_to_all x1, starting transfers between devices, body(): terms = lax.all_to_all(terms, ('dp', 'ctx'), 0, 0, tiled=True)  2.82 us
    ppermute x3, waiting for transfers between devices, ring(): lax.ppermute(value, axis, [(i, (i + steps) % count) for i in range(count)])  0.62 us
    all_to_all x1, waiting for transfers between devices, body(): terms = lax.all_to_all(terms, ('dp', 'ctx'), 0, 0, tiled=True)  0.57 us
  transfers between devices with their start and end apart: 5, of which 3 were waited for; matrix products, arithmetic and copies ran while one was open for 0% of the time, Pallas kernels for 27%

profile of v8, /device:TPU:0, one launch (start us, length us, event | category | flops | bytes accessed | tf_op | source)
XLA Modules:
  0.0 25.2 jit_solution(575553032383952049)
XLA Ops:
  0.6 3.1 %collective-permute-start = (bf16[1,128,512]{2,1,0:T(8,128)(2,1)}, bf16[1,128,512]{2,1,0:T(8,128)(2,1)S(1)}, u32[]{:S(2)}, u32[]{:S(2)}) collective-permute-start(bf16[1,128,512]{2,1,0:T(8,128)(2,1)} %k_in.1), channel_id=1, source_target_pairs={{0,1},{1,2},{2,3},{3,0},{4,5},{5,6},{6,7},{7,4},{8,9},{9,10},{10,1... | collective-permute-start | bytes 393224 | tf_op jit(solution)/shard_map/ppermute | solution.py:219
  3.7 3.5 %collective-permute-start.1 = (bf16[1,128,512]{2,1,0:T(8,128)(2,1)}, bf16[1,128,512]{2,1,0:T(8,128)(2,1)S(1)}, u32[]{:S(2)}, u32[]{:S(2)}) collective-permute-start(bf16[1,128,512]{2,1,0:T(8,128)(2,1)} %v_in.1), channel_id=1, source_target_pairs={{0,1},{1,2},{2,3},{4,5},{5,6},{6,7},{8,9},{9,10},{10,11},{12,13},{... | collective-permute-start | bytes 393224 | tf_op jit(solution)/shard_map/ppermute | solution.py:224
  7.2 1.8 %load.1 = (bf16[1,128,2048]{2,1,0:T(8,128)(2,1)S(1)}, bf16[1,128,512]{2,1,0:T(8,128)(2,1)S(1)}, bf16[1,128,2048]{2,1,0:T(8,128)(2,1)S(1)}, f32[1,128,2048]{2,1,0...) custom-call(s32[1]{0:T(128)} %bitcast.first_ref, f32[16]{0:T(128)} %sinks_in.1, ...), custom_call_target="tpu_custom_call" | custom-call | flops 134217728 | bytes 4597828 | tf_op jit(solution)/shard_map/load/pallas_call | solution.py:37
  9.0 0.4 %collective-permute-done.hk_ref = bf16[1,128,512]{2,1,0:T(8,128)(2,1)S(1)} collective-permute-done((bf16[1,128,512]{2,1,0:T(8,128)(2,1)}, bf16[1,128,512]{2,1,0:T(8,128)(2,1)S(1)}, u32[]{:S(2)}, u32[]{:S(2)}) %collective-permute-start) | collective-permute-done | bytes 131104 | tf_op jit(solution)/shard_map/ppermute | solution.py:219
  9.4 1.3 %softmax.1 = (bf16[1,128,2048]{2,1,0:T(8,128)(2,1)S(1)}, bf16[1,128,512]{2,1,0:T(8,128)(2,1)S(1)}, f32[1,128,2048]{2,1,0:T(8,128)S(1)}, f32[1,1,2048]{2,1,0:T(1,128)S(1)}) custom-call(f32[1,512]{1,0:T(1,128)S(1)} %get-tuple-element.25.bias_ref, f32[1,2048]{1,0:T(1,128)S(1)} %get-tuple-element.26.sink_ref, bf16[1,128,2048]{2,1,0:T(8,128)(2,1)S(1)} %get-tuple-element.23.q_ref, ...), custom_call_target="tpu_custom_call" | custom-call | flops 268435456 | bytes 4999168 | tf_op jit(solution)/shard_map/softmax/pallas_call | solution.py:37
  10.8 2.7 %collective-permute-start.3 = (bf16[1,128,512]{2,1,0:T(8,128)(2,1)S(1)}, bf16[1,128,512]{2,1,0:T(8,128)(2,1)S(1)}, u32[]{:S(2)}, u32[]{:S(2)}) collective-permute-start(bf16[1,128,512]{2,1,0:T(8,128)(2,1)S(1)} %get-tuple-element.39), channel_id=1, source_target_pairs={{0,3},{1,0},{2,1},{3,2},{4,7},{5,4},{6,5},{7,6},{8,11},{9,8},{10,9... | collective-permute-start | bytes 393224 | tf_op jit(solution)/shard_map/ppermute | solution.py:219
  13.5 0.0 collective-permute-done.1.hv_ref
  13.5 0.9 %terms.1 = (f32[32,16]{1,0:T(8,128)}, f32[1,128,2048]{2,1,0:T(8,128)S(1)}) custom-call(bf16[1,128,2048]{2,1,0:T(8,128)(2,1)S(1)} %get-tuple-element.27.do_ref, bf16[1,128,512]{2,1,0:T(8,128)(2,1)S(1)} %collective-permute-done.1.hv_ref, f32[1,128,2048]{2,1,0:T(8,128)S(1)} %get-tuple-element.31.g_ref, f32[1,1,2048]{2,1,0:T(1,128)S(1)} %get-tuple-element.32.own_ref, ...), custom_call_target="tpu_custom_call" | custom-call | flops 67108864 | bytes 3811328 | tf_op jit(solution)/shard_map/terms/pallas_call | solution.py:37
  14.4 2.8 %all-to-all-start = ((f32[32,1,16]{2,1,0:T(1,128)}), f32[32,1,16]{2,1,0:T(1,128)S(1)}, u32[]{:S(2)}, u32[]{:S(2)}) async-start(f32[32,1,16]{2,1,0:T(1,128)} %bitcast.7), calls=%async_computation | async-start | bytes 32768 | tf_op jit(solution)/shard_map/all_to_all | solution.py:264
  17.2 0.5 %keys.1 = (bf16[1,256,2048]{2,1,0:T(8,128)(2,1)S(1)}, bf16[1,128,512]{2,1,0:T(8,128)(2,1)S(1)}) custom-call(bf16[1,128,2048]{2,1,0:T(8,128)(2,1)S(1)} %get-tuple-element.23.q_ref, bf16[1,128,2048]{2,1,0:T(8,128)(2,1)S(1)} %get-tuple-element.30.p_ref, f32[1,128,2048]{2,1,0:T(8,128)S(1)} %get-tuple-element.33.gp_ref), custom_call_target="tpu_custom_call" | custom-call | flops 134217728 | bytes 3276800 | tf_op jit(solution)/shard_map/keys/pallas_call | solution.py:37
  17.8 3.7 %collective-permute-start.2 = (bf16[1,128,512]{2,1,0:T(8,128)(2,1)S(1)}, bf16[1,128,512]{2,1,0:T(8,128)(2,1)S(1)}, u32[]{:S(2)}, u32[]{:S(2)}) collective-permute-start(bf16[1,128,512]{2,1,0:T(8,128)(2,1)S(1)} %get-tuple-element.37), channel_id=1, source_target_pairs={{0,3},{1,0},{2,1},{3,2},{4,7},{5,4},{6,5},{7,6},{8,11},{9,8},{10,9... | collective-permute-start | bytes 393224 | tf_op jit(solution)/shard_map/ppermute | solution.py:219
  21.4 1.4 %query.1 = (bf16[1,128,2048]{2,1,0:T(8,128)(2,1)}, f32[1,128,512]{2,1,0:T(8,128)S(1)}) custom-call(bf16[1,128,2048]{2,1,0:T(8,128)(2,1)S(1)} %get-tuple-element.23.q_ref, bf16[1,128,512]{2,1,0:T(8,128)(2,1)S(1)} %get-tuple-element.24.k_ref, bf16[1,128,512]{2,1,0:T(8,128)(2,1)S(1)} %collective-permute-done.hk_ref, ...), custom_call_target="tpu_custom_call" | custom-call | flops 201326592 | bytes 2621440 | tf_op jit(solution)/shard_map/query/pallas_call | solution.py:37
  22.8 0.0 collective-permute-done.3.back_ref
  22.8 1.0 %values.1.refs_0_ = bf16[1,128,512]{2,1,0:T(8,128)(2,1)} custom-call(bf16[1,128,2048]{2,1,0:T(8,128)(2,1)S(1)} %get-tuple-element.27.do_ref, bf16[1,128,2048]{2,1,0:T(8,128)(2,1)S(1)} %get-tuple-element.30.p_ref, bf16[1,128,512]{2,1,0:T(8,128)(2,1)S(1)} %collective-permute-done.3.back_ref), custom_call_target="tpu_custom_call" | custom-call | flops 67108864 | bytes 1310720 | tf_op jit(solution)/shard_map/values/pallas_call | solution.py:37
  23.8 0.6 %all-to-all-done = f32[32,1,16]{2,1,0:T(1,128)S(1)} async-done(((f32[32,1,16]{2,1,0:T(1,128)}), f32[32,1,16]{2,1,0:T(1,128)S(1)}, u32[]{:S(2)}, u32[]{:S(2)}) %all-to-all-start) | async-done | bytes 2080 | tf_op jit(solution)/shard_map/all_to_all | solution.py:264
  24.3 0.2 collective-permute-done.2.back_ref
  24.5 0.7 %finish.1 = (bf16[1,128,512]{2,1,0:T(8,128)(2,1)}, f32[1,16]{1,0:T(1,128)}) custom-call(f32[1,128,512]{2,1,0:T(8,128)S(1)} %get-tuple-element.36.own_ref, bf16[1,128,512]{2,1,0:T(8,128)(2,1)S(1)} %collective-permute-done.2.back_ref, f32[1,16]{1,0:T(1,128)S(1)} %total.1.total_ref), custom_call_target="tpu_custom_call" | custom-call | bytes 524416 | tf_op jit(solution)/shard_map/finish/pallas_call | solution.py:37
  (1 shorter events, 0.0 us)
Async XLA Ops:
  0.6 8.8 %collective-permute-start = (bf16[1,128,512]{2,1,0:T(8,128)(2,1)}, bf16[1,128,512]{2,1,0:T(8,128)(2,1)S(1)}, u32[]{:S(2)}, u32[]{:S(2)}) collective-permute-start(bf16[1,128,512]{2,1,0:T(8,128)(2,1)} %k_in.1), channel_id=1, source_target_pairs={{0,1},{1,2},{2,3},{3,0},{4,5},{5,6},{6,7},{7,4},{8,9},{9,10},{10,1... | collective-permute-start | bytes 393224 | tf_op jit(solution)/shard_map/ppermute | solution.py:219
  3.7 9.8 %collective-permute-start.1 = (bf16[1,128,512]{2,1,0:T(8,128)(2,1)}, bf16[1,128,512]{2,1,0:T(8,128)(2,1)S(1)}, u32[]{:S(2)}, u32[]{:S(2)}) collective-permute-start(bf16[1,128,512]{2,1,0:T(8,128)(2,1)} %v_in.1), channel_id=1, source_target_pairs={{0,1},{1,2},{2,3},{4,5},{5,6},{6,7},{8,9},{9,10},{10,11},{12,13},{... | collective-permute-start | bytes 393224 | tf_op jit(solution)/shard_map/ppermute | solution.py:224
  10.8 12.0 %collective-permute-start.3 = (bf16[1,128,512]{2,1,0:T(8,128)(2,1)S(1)}, bf16[1,128,512]{2,1,0:T(8,128)(2,1)S(1)}, u32[]{:S(2)}, u32[]{:S(2)}) collective-permute-start(bf16[1,128,512]{2,1,0:T(8,128)(2,1)S(1)} %get-tuple-element.39), channel_id=1, source_target_pairs={{0,3},{1,0},{2,1},{3,2},{4,7},{5,4},{6,5},{7,6},{8,11},{9,8},{10,9... | collective-permute-start | bytes 393224 | tf_op jit(solution)/shard_map/ppermute | solution.py:219
  14.4 9.9 %all-to-all-start = ((f32[32,1,16]{2,1,0:T(1,128)}), f32[32,1,16]{2,1,0:T(1,128)S(1)}, u32[]{:S(2)}, u32[]{:S(2)}) async-start(f32[32,1,16]{2,1,0:T(1,128)} %bitcast.7), calls=%async_computation | async-start | bytes 32768 | tf_op jit(solution)/shard_map/all_to_all | solution.py:264
  17.8 6.7 %collective-permute-start.2 = (bf16[1,128,512]{2,1,0:T(8,128)(2,1)S(1)}, bf16[1,128,512]{2,1,0:T(8,128)(2,1)S(1)}, u32[]{:S(2)}, u32[]{:S(2)}) collective-permute-start(bf16[1,128,512]{2,1,0:T(8,128)(2,1)S(1)} %get-tuple-element.37), channel_id=1, source_target_pairs={{0,3},{1,0},{2,1},{3,2},{4,7},{5,4},{6,5},{7,6},{8,11},{9,8},{10,9... | collective-permute-start | bytes 393224 | tf_op jit(solution)/shard_map/ppermute | solution.py:219

commit v9 on v8

--- a/solution.py
+++ b/solution.py
@@ -143,7 +143,7 @@
                 ((1,), (0,)))
 
 
-def terms_kernel(do_ref, hv_ref, g_ref, own_ref, dp_ref, terms_out, gp_ref, sink_ref, terms_ref, sem):
+def terms_kernel(do_ref, hv_ref, g_ref, own_ref, p_ref, dp_ref, terms_out, gp_ref, sink_ref, terms_ref, sem):
     _, rows, _ = do_ref.shape
     own = own_mask(rows, GROUP * rows)
     parts = list(groups(do_ref))
@@ -166,7 +166,9 @@
     for b, heads, kv, cols in parts:
         before = dot(hv_ref[b, :, kv], stacked(do_ref, b, heads), ((1,), (1,)))
         grad_prob = jnp.where(own, dp_ref[b, :, cols], before)
-        gp_ref[b, :, cols] = grad_prob
+        gp_ref[b, :rows, cols] = grad_prob
+        gp_ref[b, rows:rows + 1, cols] = jnp.sum(
+            p_ref[b, :, cols].astype(jnp.float32) * grad_prob, axis=0, keepdims=True)
     copy.wait()
 
 
@@ -174,22 +176,25 @@
     _, rows, _ = q_ref.shape
     own = own_mask(rows, GROUP * rows)
     parts = list(groups(q_ref))
-    deltas = [jnp.sum(p_ref[b, :, cols].astype(jnp.float32) * gp_ref[b, :, cols], axis=0, keepdims=True)
-              for b, _, _, cols in parts]
-    for (b, _, _, cols), delta in zip(parts, deltas):
-        ds_ref[b, :, cols] = split(own, p_ref[b, :, cols].astype(jnp.float32) * (gp_ref[b, :, cols] - delta))
-    for b, heads, kv, cols in parts:
-        grad_key = dot(ds_ref[b, rows:, cols], stacked(q_ref, b, heads), ((1,), (0,))) * SCALE
+    dscores = []
+    for b, _, _, cols in parts:
+        delta = gp_ref[b, rows:rows + 1, cols]
+        dscores.append((p_ref[b, :, cols].astype(jnp.float32) * (gp_ref[b, :rows, cols] - delta)).astype(jnp.bfloat16))
+        ds_ref[b, :, cols] = dscores[-1]
+    for (b, heads, kv, cols), dscore in zip(parts, dscores):
+        grad_key = dot(split(own, dscore)[rows:], stacked(q_ref, b, heads), ((1,), (0,))) * SCALE
         back_ref[b, :, kv] = grad_key.astype(jnp.bfloat16)
 
 
 def query_kernel(q_ref, k_ref, hk_ref, ds_ref, dq_ref, dk_ref):
     _, rows, _ = dq_ref.shape
+    own = own_mask(rows, GROUP * rows)
     parts = list(groups(dq_ref))
-    for b, heads, kv, cols in parts:
-        dk_ref[b, :, kv] = dot(ds_ref[b, :rows, cols], stacked(q_ref, b, heads), ((1,), (0,))) * SCALE
+    dscores = [split(own, ds_ref[b, :, cols]) for b, _, _, cols in parts]
+    for (b, heads, kv, _), dscore in zip(parts, dscores):
+        dk_ref[b, :, kv] = dot(dscore[:rows], stacked(q_ref, b, heads), ((1,), (0,))) * SCALE
     keys = [jnp.concatenate([k_ref[b, :, kv], hk_ref[b, :, kv]], axis=0) for b, _, kv, _ in parts]
-    products = [dot(ds_ref[b, :, cols], key, ((0,), (0,))) for (b, _, _, cols), key in zip(parts, keys)]
+    products = [dot(dscore, key, ((0,), (0,))) for dscore, key in zip(dscores, keys)]
     for (b, heads, _, _), product in zip(parts, products):
         for n, h in enumerate(heads):
             dq_ref[b, :, h * HEAD:(h + 1) * HEAD] = (product[n * rows:(n + 1) * rows] * SCALE).astype(jnp.bfloat16)
@@ -252,13 +257,13 @@
         scratch=[pltpu.VMEM(square.shape, f32)])
     back_values = ring(back_values, "ctx", -1)
     terms, grad_prob = call(
-        terms_kernel, "terms", (pltpu.HBM((dp * ctx, HEADS), f32), pltpu.VMEM(square.shape, f32)),
-        [VMEM] * 5, (do, halo_values, halves, own_terms, grad_prob), product,
+        terms_kernel, "terms", (pltpu.HBM((dp * ctx, HEADS), f32), pltpu.VMEM((batch, rows + 8, HEADS * rows), f32)),
+        [VMEM] * 6, (do, halo_values, halves, own_terms, prob, grad_prob), product,
         scratch=[pltpu.VMEM((HEADS, rows), f32), pltpu.VMEM((dp * ctx, HEADS), f32), pltpu.SemaphoreType.DMA],
         out_specs=(HBM, VMEM))
     dscores, back_keys = call(
         keys_kernel, "keys",
-        (pltpu.VMEM((batch, 2 * rows, HEADS * rows), bf16), pltpu.VMEM(keys.shape, bf16)),
+        (pltpu.VMEM(square.shape, bf16), pltpu.VMEM(keys.shape, bf16)),
         [VMEM] * 3, (q, prob, grad_prob), 2 * product)
     back_keys = ring(back_keys, "ctx", -1)
     terms = lax.all_to_all(terms, ("dp", "ctx"), 0, 0, tiled=True)

time: 25.4 us -> 25.3 us (level)
  transfers between devices with their start and end apart: 5 -> 5, of which waited for: 3 -> 2; matrix products, arithmetic and copies ran while one was open for 0% -> 0% of each run, Pallas kernels for 27% -> 27%
where the time goes in v9:
time: 25.3 us; the launch traced here: 25.1 us
  starting transfers between devices  15.8 us (62%)
  Pallas kernels  7.37 us (29%)
  waiting for transfers between devices  1.23 us (5%)
  between operations  0.69 us (3%)
    ppermute x3, starting transfers between devices, ring(): lax.ppermute(value, axis, [(i, (i + steps) % count) for i in range(count)])  9.47 us
    pallas_call x8, Pallas kernels, call(): pl.pallas_call(kernel, out_shape=out_shape, in_specs=in_specs, out_specs=...  7.37 us
    ppermute x1, starting transfers between devices, shift(): return lax.ppermute(value, axis, [(i, i + 1) for i in range(count - 1)])  3.48 us
    all_to_all x1, starting transfers between devices, body(): terms = lax.all_to_all(terms, ('dp', 'ctx'), 0, 0, tiled=True)  2.82 us
    all_to_all x1, waiting for transfers between devices, body(): terms = lax.all_to_all(terms, ('dp', 'ctx'), 0, 0, tiled=True)  0.78 us
  transfers between devices with their start and end apart: 5, of which 2 were waited for; matrix products, arithmetic and copies ran while one was open for 0% of the time, Pallas kernels for 27%

profile of v9, /device:TPU:0, one launch (start us, length us, event | category | flops | bytes accessed | tf_op | source)
XLA Modules:
  0.0 25.1 jit_solution(14696133734558633506)
XLA Ops:
  0.6 3.1 %collective-permute-start = (bf16[1,128,512]{2,1,0:T(8,128)(2,1)}, bf16[1,128,512]{2,1,0:T(8,128)(2,1)S(1)}, u32[]{:S(2)}, u32[]{:S(2)}) collective-permute-start(bf16[1,128,512]{2,1,0:T(8,128)(2,1)} %k_in.1), channel_id=1, source_target_pairs={{0,1},{1,2},{2,3},{3,0},{4,5},{5,6},{6,7},{7,4},{8,9},{9,10},{10,1... | collective-permute-start | bytes 393224 | tf_op jit(solution)/shard_map/ppermute | solution.py:224
  3.7 3.5 %collective-permute-start.1 = (bf16[1,128,512]{2,1,0:T(8,128)(2,1)}, bf16[1,128,512]{2,1,0:T(8,128)(2,1)S(1)}, u32[]{:S(2)}, u32[]{:S(2)}) collective-permute-start(bf16[1,128,512]{2,1,0:T(8,128)(2,1)} %v_in.1), channel_id=1, source_target_pairs={{0,1},{1,2},{2,3},{4,5},{5,6},{6,7},{8,9},{9,10},{10,11},{12,13},{... | collective-permute-start | bytes 393224 | tf_op jit(solution)/shard_map/ppermute | solution.py:229
  7.2 1.8 %load.1 = (bf16[1,128,2048]{2,1,0:T(8,128)(2,1)S(1)}, bf16[1,128,512]{2,1,0:T(8,128)(2,1)S(1)}, bf16[1,128,2048]{2,1,0:T(8,128)(2,1)S(1)}, f32[1,128,2048]{2,1,0...) custom-call(s32[1]{0:T(128)} %bitcast.first_ref, f32[16]{0:T(128)} %sinks_in.1, ...), custom_call_target="tpu_custom_call" | custom-call | flops 134217728 | bytes 4597828 | tf_op jit(solution)/shard_map/load/pallas_call | solution.py:37
  9.0 0.4 %collective-permute-done.hk_ref = bf16[1,128,512]{2,1,0:T(8,128)(2,1)S(1)} collective-permute-done((bf16[1,128,512]{2,1,0:T(8,128)(2,1)}, bf16[1,128,512]{2,1,0:T(8,128)(2,1)S(1)}, u32[]{:S(2)}, u32[]{:S(2)}) %collective-permute-start) | collective-permute-done | bytes 131104 | tf_op jit(solution)/shard_map/ppermute | solution.py:224
  9.4 1.3 %softmax.1 = (bf16[1,128,2048]{2,1,0:T(8,128)(2,1)S(1)}, bf16[1,128,512]{2,1,0:T(8,128)(2,1)S(1)}, f32[1,128,2048]{2,1,0:T(8,128)S(1)}, f32[1,1,2048]{2,1,0:T(1,128)S(1)}) custom-call(f32[1,512]{1,0:T(1,128)S(1)} %get-tuple-element.25.bias_ref, f32[1,2048]{1,0:T(1,128)S(1)} %get-tuple-element.26.sink_ref, bf16[1,128,2048]{2,1,0:T(8,128)(2,1)S(1)} %get-tuple-element.23.q_ref, ...), custom_call_target="tpu_custom_call" | custom-call | flops 268435456 | bytes 4999168 | tf_op jit(solution)/shard_map/softmax/pallas_call | solution.py:37
  10.8 2.7 %collective-permute-start.3 = (bf16[1,128,512]{2,1,0:T(8,128)(2,1)S(1)}, bf16[1,128,512]{2,1,0:T(8,128)(2,1)S(1)}, u32[]{:S(2)}, u32[]{:S(2)}) collective-permute-start(bf16[1,128,512]{2,1,0:T(8,128)(2,1)S(1)} %get-tuple-element.39), channel_id=1, source_target_pairs={{0,3},{1,0},{2,1},{3,2},{4,7},{5,4},{6,5},{7,6},{8,11},{9,8},{10,9... | collective-permute-start | bytes 393224 | tf_op jit(solution)/shard_map/ppermute | solution.py:224
  13.5 0.0 collective-permute-done.1.hv_ref
  13.5 0.9 %terms.1 = (f32[32,16]{1,0:T(8,128)}, f32[1,136,2048]{2,1,0:T(8,128)S(1)}) custom-call(bf16[1,128,2048]{2,1,0:T(8,128)(2,1)S(1)} %get-tuple-element.27.do_ref, bf16[1,128,512]{2,1,0:T(8,128)(2,1)S(1)} %collective-permute-done.1.hv_ref, f32[1,128,2048]{2,1,0:T(8,128)S(1)} %get-tuple-element.31.g_ref, f32[1,1,2048]{2,1,0:T(1,128)S(1)} %get-tuple-element.32.own_ref, ...), custom_call_target="tpu_custom_call" | custom-call | flops 67108864 | bytes 4401152 | tf_op jit(solution)/shard_map/terms/pallas_call | solution.py:37
  14.4 2.8 %all-to-all-start = ((f32[32,1,16]{2,1,0:T(1,128)}), f32[32,1,16]{2,1,0:T(1,128)S(1)}, u32[]{:S(2)}, u32[]{:S(2)}) async-start(f32[32,1,16]{2,1,0:T(1,128)} %bitcast.7), calls=%async_computation | async-start | bytes 32768 | tf_op jit(solution)/shard_map/all_to_all | solution.py:269
  17.2 0.4 %keys.1 = (bf16[1,128,2048]{2,1,0:T(8,128)(2,1)S(1)}, bf16[1,128,512]{2,1,0:T(8,128)(2,1)S(1)}) custom-call(bf16[1,128,2048]{2,1,0:T(8,128)(2,1)S(1)} %get-tuple-element.23.q_ref, bf16[1,128,2048]{2,1,0:T(8,128)(2,1)S(1)} %get-tuple-element.30.p_ref, f32[1,136,2048]{2,1,0:T(8,128)S(1)} %get-tuple-element.33.gp_ref), custom_call_target="tpu_custom_call" | custom-call | flops 134217728 | bytes 2818048 | tf_op jit(solution)/shard_map/keys/pallas_call | solution.py:37
  17.6 3.7 %collective-permute-start.2 = (bf16[1,128,512]{2,1,0:T(8,128)(2,1)S(1)}, bf16[1,128,512]{2,1,0:T(8,128)(2,1)S(1)}, u32[]{:S(2)}, u32[]{:S(2)}) collective-permute-start(bf16[1,128,512]{2,1,0:T(8,128)(2,1)S(1)} %get-tuple-element.37), channel_id=1, source_target_pairs={{0,3},{1,0},{2,1},{3,2},{4,7},{5,4},{6,5},{7,6},{8,11},{9,8},{10,9... | collective-permute-start | bytes 393224 | tf_op jit(solution)/shard_map/ppermute | solution.py:224
  21.3 1.4 %query.1 = (bf16[1,128,2048]{2,1,0:T(8,128)(2,1)}, f32[1,128,512]{2,1,0:T(8,128)S(1)}) custom-call(bf16[1,128,2048]{2,1,0:T(8,128)(2,1)S(1)} %get-tuple-element.23.q_ref, bf16[1,128,512]{2,1,0:T(8,128)(2,1)S(1)} %get-tuple-element.24.k_ref, bf16[1,128,512]{2,1,0:T(8,128)(2,1)S(1)} %collective-permute-done.hk_ref, ...), custom_call_target="tpu_custom_call" | custom-call | flops 201326592 | bytes 2097152 | tf_op jit(solution)/shard_map/query/pallas_call | solution.py:37
  22.6 0.0 collective-permute-done.3.back_ref
  22.6 1.0 %values.1.refs_0_ = bf16[1,128,512]{2,1,0:T(8,128)(2,1)} custom-call(bf16[1,128,2048]{2,1,0:T(8,128)(2,1)S(1)} %get-tuple-element.27.do_ref, bf16[1,128,2048]{2,1,0:T(8,128)(2,1)S(1)} %get-tuple-element.30.p_ref, bf16[1,128,512]{2,1,0:T(8,128)(2,1)S(1)} %collective-permute-done.3.back_ref), custom_call_target="tpu_custom_call" | custom-call | flops 67108864 | bytes 1310720 | tf_op jit(solution)/shard_map/values/pallas_call | solution.py:37
  23.6 0.8 %all-to-all-done = f32[32,1,16]{2,1,0:T(1,128)S(1)} async-done(((f32[32,1,16]{2,1,0:T(1,128)}), f32[32,1,16]{2,1,0:T(1,128)S(1)}, u32[]{:S(2)}, u32[]{:S(2)}) %all-to-all-start) | async-done | bytes 2080 | tf_op jit(solution)/shard_map/all_to_all | solution.py:269
  24.4 0.0 collective-permute-done.2.back_ref
  24.4 0.7 %finish.1 = (bf16[1,128,512]{2,1,0:T(8,128)(2,1)}, f32[1,16]{1,0:T(1,128)}) custom-call(f32[1,128,512]{2,1,0:T(8,128)S(1)} %get-tuple-element.36.own_ref, bf16[1,128,512]{2,1,0:T(8,128)(2,1)S(1)} %collective-permute-done.2.back_ref, f32[1,16]{1,0:T(1,128)S(1)} %total.1.total_ref), custom_call_target="tpu_custom_call" | custom-call | bytes 524416 | tf_op jit(solution)/shard_map/finish/pallas_call | solution.py:37
  (1 shorter events, 0.0 us)
Async XLA Ops:
  0.6 8.8 %collective-permute-start = (bf16[1,128,512]{2,1,0:T(8,128)(2,1)}, bf16[1,128,512]{2,1,0:T(8,128)(2,1)S(1)}, u32[]{:S(2)}, u32[]{:S(2)}) collective-permute-start(bf16[1,128,512]{2,1,0:T(8,128)(2,1)} %k_in.1), channel_id=1, source_target_pairs={{0,1},{1,2},{2,3},{3,0},{4,5},{5,6},{6,7},{7,4},{8,9},{9,10},{10,1... | collective-permute-start | bytes 393224 | tf_op jit(solution)/shard_map/ppermute | solution.py:224
  3.7 9.8 %collective-permute-start.1 = (bf16[1,128,512]{2,1,0:T(8,128)(2,1)}, bf16[1,128,512]{2,1,0:T(8,128)(2,1)S(1)}, u32[]{:S(2)}, u32[]{:S(2)}) collective-permute-start(bf16[1,128,512]{2,1,0:T(8,128)(2,1)} %v_in.1), channel_id=1, source_target_pairs={{0,1},{1,2},{2,3},{4,5},{5,6},{6,7},{8,9},{9,10},{10,11},{12,13},{... | collective-permute-start | bytes 393224 | tf_op jit(solution)/shard_map/ppermute | solution.py:229
  10.8 11.8 %collective-permute-start.3 = (bf16[1,128,512]{2,1,0:T(8,128)(2,1)S(1)}, bf16[1,128,512]{2,1,0:T(8,128)(2,1)S(1)}, u32[]{:S(2)}, u32[]{:S(2)}) collective-permute-start(bf16[1,128,512]{2,1,0:T(8,128)(2,1)S(1)} %get-tuple-element.39), channel_id=1, source_target_pairs={{0,3},{1,0},{2,1},{3,2},{4,7},{5,4},{6,5},{7,6},{8,11},{9,8},{10,9... | collective-permute-start | bytes 393224 | tf_op jit(solution)/shard_map/ppermute | solution.py:224
  14.4 10.0 %all-to-all-start = ((f32[32,1,16]{2,1,0:T(1,128)}), f32[32,1,16]{2,1,0:T(1,128)S(1)}, u32[]{:S(2)}, u32[]{:S(2)}) async-start(f32[32,1,16]{2,1,0:T(1,128)} %bitcast.7), calls=%async_computation | async-start | bytes 32768 | tf_op jit(solution)/shard_map/all_to_all | solution.py:269
  17.6 6.8 %collective-permute-start.2 = (bf16[1,128,512]{2,1,0:T(8,128)(2,1)S(1)}, bf16[1,128,512]{2,1,0:T(8,128)(2,1)S(1)}, u32[]{:S(2)}, u32[]{:S(2)}) collective-permute-start(bf16[1,128,512]{2,1,0:T(8,128)(2,1)S(1)} %get-tuple-element.37), channel_id=1, source_target_pairs={{0,3},{1,0},{2,1},{3,2},{4,7},{5,4},{6,5},{7,6},{8,11},{9,8},{10,9... | collective-permute-start | bytes 393224 | tf_op jit(solution)/shard_map/ppermute | solution.py:224

commit v10 on v9

--- a/solution.py
+++ b/solution.py
@@ -131,16 +131,12 @@
     for (b, _, _, cols), sink_prob in zip(parts, sink_probs):
         prob = p_ref[b, :, cols] * sink_prob
         own_ref[b, :, cols] = jnp.sum(jnp.where(own, prob * dp_ref[b, :, cols], 0.0), axis=0, keepdims=True)
-        prob = jnp.where(own, 0.0, prob)
-        high = prob.astype(jnp.bfloat16)
-        splits.append((high, (prob - high.astype(jnp.float32)).astype(jnp.bfloat16)))
-    for (b, heads, _, _), (high, low) in zip(parts, splits):
+        splits.append(split(own, prob)[rows:])
+    for (b, heads, _, _), high in zip(parts, splits):
         for n, h in enumerate(heads):
             part = slice(n * rows, (n + 1) * rows)
             grad = do_ref[b, :, h * HEAD:(h + 1) * HEAD]
-            g_ref[b, :, h * HEAD:(h + 1) * HEAD] = dot(
-                jnp.concatenate([high[:, part], low[:, part]], axis=1), jnp.concatenate([grad, grad], axis=0),
-                ((1,), (0,)))
+            g_ref[b, :, h * HEAD:(h + 1) * HEAD] = dot(high[:, part], grad, ((1,), (0,)))
 
 
 def terms_kernel(do_ref, hv_ref, g_ref, own_ref, p_ref, dp_ref, terms_out, gp_ref, sink_ref, terms_ref, sem):

time: 25.3 us -> 25.2 us (level)
  transfers between devices with their start and end apart: 5 -> 5, of which waited for: 2 -> 2; matrix products, arithmetic and copies ran while one was open for 0% -> 0% of each run, Pallas kernels for 27% -> 26%
where the time goes in v10:
time: 25.2 us; the launch traced here: 25 us
  starting transfers between devices  15.8 us (63%)
  Pallas kernels  7.27 us (29%)
  waiting for transfers between devices  1.24 us (5%)
  between operations  0.69 us (3%)
    ppermute x3, starting transfers between devices, ring(): lax.ppermute(value, axis, [(i, (i + steps) % count) for i in range(count)])  9.47 us
    pallas_call x8, Pallas kernels, call(): pl.pallas_call(kernel, out_shape=out_shape, in_specs=in_specs, out_specs=...  7.27 us
    ppermute x1, starting transfers between devices, shift(): return lax.ppermute(value, axis, [(i, i + 1) for i in range(count - 1)])  3.48 us
    all_to_all x1, starting transfers between devices, body(): terms = lax.all_to_all(terms, ('dp', 'ctx'), 0, 0, tiled=True)  2.83 us
    all_to_all x1, waiting for transfers between devices, body(): terms = lax.all_to_all(terms, ('dp', 'ctx'), 0, 0, tiled=True)  0.78 us
  transfers between devices with their start and end apart: 5, of which 2 were waited for; matrix products, arithmetic and copies ran while one was open for 0% of the time, Pallas kernels for 26%

profile of v10, /device:TPU:0, one launch (start us, length us, event | category | flops | bytes accessed | tf_op | source)
XLA Modules:
  0.0 25.0 jit_solution(11080219328629470412)
XLA Ops:
  0.6 3.1 %collective-permute-start = (bf16[1,128,512]{2,1,0:T(8,128)(2,1)}, bf16[1,128,512]{2,1,0:T(8,128)(2,1)S(1)}, u32[]{:S(2)}, u32[]{:S(2)}) collective-permute-start(bf16[1,128,512]{2,1,0:T(8,128)(2,1)} %k_in.1), channel_id=1, source_target_pairs={{0,1},{1,2},{2,3},{3,0},{4,5},{5,6},{6,7},{7,4},{8,9},{9,10},{10,1... | collective-permute-start | bytes 393224 | tf_op jit(solution)/shard_map/ppermute | solution.py:220
  3.7 3.5 %collective-permute-start.1 = (bf16[1,128,512]{2,1,0:T(8,128)(2,1)}, bf16[1,128,512]{2,1,0:T(8,128)(2,1)S(1)}, u32[]{:S(2)}, u32[]{:S(2)}) collective-permute-start(bf16[1,128,512]{2,1,0:T(8,128)(2,1)} %v_in.1), channel_id=1, source_target_pairs={{0,1},{1,2},{2,3},{4,5},{5,6},{6,7},{8,9},{9,10},{10,11},{12,13},{... | collective-permute-start | bytes 393224 | tf_op jit(solution)/shard_map/ppermute | solution.py:225
  7.2 1.8 %load.1 = (bf16[1,128,2048]{2,1,0:T(8,128)(2,1)S(1)}, bf16[1,128,512]{2,1,0:T(8,128)(2,1)S(1)}, bf16[1,128,2048]{2,1,0:T(8,128)(2,1)S(1)}, f32[1,128,2048]{2,1,0...) custom-call(s32[1]{0:T(128)} %bitcast.first_ref, f32[16]{0:T(128)} %sinks_in.1, ...), custom_call_target="tpu_custom_call" | custom-call | flops 134217728 | bytes 4597828 | tf_op jit(solution)/shard_map/load/pallas_call | solution.py:37
  9.0 0.4 %collective-permute-done.hk_ref = bf16[1,128,512]{2,1,0:T(8,128)(2,1)S(1)} collective-permute-done((bf16[1,128,512]{2,1,0:T(8,128)(2,1)}, bf16[1,128,512]{2,1,0:T(8,128)(2,1)S(1)}, u32[]{:S(2)}, u32[]{:S(2)}) %collective-permute-start) | collective-permute-done | bytes 131104 | tf_op jit(solution)/shard_map/ppermute | solution.py:220
  9.4 1.2 %softmax.1 = (bf16[1,128,2048]{2,1,0:T(8,128)(2,1)S(1)}, bf16[1,128,512]{2,1,0:T(8,128)(2,1)S(1)}, f32[1,128,2048]{2,1,0:T(8,128)S(1)}, f32[1,1,2048]{2,1,0:T(1,128)S(1)}) custom-call(f32[1,512]{1,0:T(1,128)S(1)} %get-tuple-element.25.bias_ref, f32[1,2048]{1,0:T(1,128)S(1)} %get-tuple-element.26.sink_ref, bf16[1,128,2048]{2,1,0:T(8,128)(2,1)S(1)} %get-tuple-element.23.q_ref, ...), custom_call_target="tpu_custom_call" | custom-call | flops 268435456 | bytes 4999168 | tf_op jit(solution)/shard_map/softmax/pallas_call | solution.py:37
  10.7 2.7 %collective-permute-start.3 = (bf16[1,128,512]{2,1,0:T(8,128)(2,1)S(1)}, bf16[1,128,512]{2,1,0:T(8,128)(2,1)S(1)}, u32[]{:S(2)}, u32[]{:S(2)}) collective-permute-start(bf16[1,128,512]{2,1,0:T(8,128)(2,1)S(1)} %get-tuple-element.39), channel_id=1, source_target_pairs={{0,3},{1,0},{2,1},{3,2},{4,7},{5,4},{6,5},{7,6},{8,11},{9,8},{10,9... | collective-permute-start | bytes 393224 | tf_op jit(solution)/shard_map/ppermute | solution.py:220
  13.4 0.0 collective-permute-done.1.hv_ref
  13.4 0.9 %terms.1 = (f32[32,16]{1,0:T(8,128)}, f32[1,136,2048]{2,1,0:T(8,128)S(1)}) custom-call(bf16[1,128,2048]{2,1,0:T(8,128)(2,1)S(1)} %get-tuple-element.27.do_ref, bf16[1,128,512]{2,1,0:T(8,128)(2,1)S(1)} %collective-permute-done.1.hv_ref, f32[1,128,2048]{2,1,0:T(8,128)S(1)} %get-tuple-element.31.g_ref, f32[1,1,2048]{2,1,0:T(1,128)S(1)} %get-tuple-element.32.own_ref, ...), custom_call_target="tpu_custom_call" | custom-call | flops 67108864 | bytes 4401152 | tf_op jit(solution)/shard_map/terms/pallas_call | solution.py:37
  14.3 2.8 %all-to-all-start = ((f32[32,1,16]{2,1,0:T(1,128)}), f32[32,1,16]{2,1,0:T(1,128)S(1)}, u32[]{:S(2)}, u32[]{:S(2)}) async-start(f32[32,1,16]{2,1,0:T(1,128)} %bitcast.7), calls=%async_computation | async-start | bytes 32768 | tf_op jit(solution)/shard_map/all_to_all | solution.py:265
  17.1 0.4 %keys.1 = (bf16[1,128,2048]{2,1,0:T(8,128)(2,1)S(1)}, bf16[1,128,512]{2,1,0:T(8,128)(2,1)S(1)}) custom-call(bf16[1,128,2048]{2,1,0:T(8,128)(2,1)S(1)} %get-tuple-element.23.q_ref, bf16[1,128,2048]{2,1,0:T(8,128)(2,1)S(1)} %get-tuple-element.30.p_ref, f32[1,136,2048]{2,1,0:T(8,128)S(1)} %get-tuple-element.33.gp_ref), custom_call_target="tpu_custom_call" | custom-call | flops 134217728 | bytes 2818048 | tf_op jit(solution)/shard_map/keys/pallas_call | solution.py:37
  17.5 3.7 %collective-permute-start.2 = (bf16[1,128,512]{2,1,0:T(8,128)(2,1)S(1)}, bf16[1,128,512]{2,1,0:T(8,128)(2,1)S(1)}, u32[]{:S(2)}, u32[]{:S(2)}) collective-permute-start(bf16[1,128,512]{2,1,0:T(8,128)(2,1)S(1)} %get-tuple-element.37), channel_id=1, source_target_pairs={{0,3},{1,0},{2,1},{3,2},{4,7},{5,4},{6,5},{7,6},{8,11},{9,8},{10,9... | collective-permute-start | bytes 393224 | tf_op jit(solution)/shard_map/ppermute | solution.py:220
  21.2 1.4 %query.1 = (bf16[1,128,2048]{2,1,0:T(8,128)(2,1)}, f32[1,128,512]{2,1,0:T(8,128)S(1)}) custom-call(bf16[1,128,2048]{2,1,0:T(8,128)(2,1)S(1)} %get-tuple-element.23.q_ref, bf16[1,128,512]{2,1,0:T(8,128)(2,1)S(1)} %get-tuple-element.24.k_ref, bf16[1,128,512]{2,1,0:T(8,128)(2,1)S(1)} %collective-permute-done.hk_ref, ...), custom_call_target="tpu_custom_call" | custom-call | flops 201326592 | bytes 2097152 | tf_op jit(solution)/shard_map/query/pallas_call | solution.py:37
  22.5 0.0 collective-permute-done.3.back_ref
  22.5 1.0 %values.1.refs_0_ = bf16[1,128,512]{2,1,0:T(8,128)(2,1)} custom-call(bf16[1,128,2048]{2,1,0:T(8,128)(2,1)S(1)} %get-tuple-element.27.do_ref, bf16[1,128,2048]{2,1,0:T(8,128)(2,1)S(1)} %get-tuple-element.30.p_ref, bf16[1,128,512]{2,1,0:T(8,128)(2,1)S(1)} %collective-permute-done.3.back_ref), custom_call_target="tpu_custom_call" | custom-call | flops 67108864 | bytes 1310720 | tf_op jit(solution)/shard_map/values/pallas_call | solution.py:37
  23.5 0.8 %all-to-all-done = f32[32,1,16]{2,1,0:T(1,128)S(1)} async-done(((f32[32,1,16]{2,1,0:T(1,128)}), f32[32,1,16]{2,1,0:T(1,128)S(1)}, u32[]{:S(2)}, u32[]{:S(2)}) %all-to-all-start) | async-done | bytes 2080 | tf_op jit(solution)/shard_map/all_to_all | solution.py:265
  24.3 0.0 collective-permute-done.2.back_ref
  24.3 0.7 %finish.1 = (bf16[1,128,512]{2,1,0:T(8,128)(2,1)}, f32[1,16]{1,0:T(1,128)}) custom-call(f32[1,128,512]{2,1,0:T(8,128)S(1)} %get-tuple-element.36.own_ref, bf16[1,128,512]{2,1,0:T(8,128)(2,1)S(1)} %collective-permute-done.2.back_ref, f32[1,16]{1,0:T(1,128)S(1)} %total.1.total_ref), custom_call_target="tpu_custom_call" | custom-call | bytes 524416 | tf_op jit(solution)/shard_map/finish/pallas_call | solution.py:37
  (1 shorter events, 0.0 us)
Async XLA Ops:
  0.6 8.8 %collective-permute-start = (bf16[1,128,512]{2,1,0:T(8,128)(2,1)}, bf16[1,128,512]{2,1,0:T(8,128)(2,1)S(1)}, u32[]{:S(2)}, u32[]{:S(2)}) collective-permute-start(bf16[1,128,512]{2,1,0:T(8,128)(2,1)} %k_in.1), channel_id=1, source_target_pairs={{0,1},{1,2},{2,3},{3,0},{4,5},{5,6},{6,7},{7,4},{8,9},{9,10},{10,1... | collective-permute-start | bytes 393224 | tf_op jit(solution)/shard_map/ppermute | solution.py:220
  3.7 9.7 %collective-permute-start.1 = (bf16[1,128,512]{2,1,0:T(8,128)(2,1)}, bf16[1,128,512]{2,1,0:T(8,128)(2,1)S(1)}, u32[]{:S(2)}, u32[]{:S(2)}) collective-permute-start(bf16[1,128,512]{2,1,0:T(8,128)(2,1)} %v_in.1), channel_id=1, source_target_pairs={{0,1},{1,2},{2,3},{4,5},{5,6},{6,7},{8,9},{9,10},{10,11},{12,13},{... | collective-permute-start | bytes 393224 | tf_op jit(solution)/shard_map/ppermute | solution.py:225
  10.7 11.9 %collective-permute-start.3 = (bf16[1,128,512]{2,1,0:T(8,128)(2,1)S(1)}, bf16[1,128,512]{2,1,0:T(8,128)(2,1)S(1)}, u32[]{:S(2)}, u32[]{:S(2)}) collective-permute-start(bf16[1,128,512]{2,1,0:T(8,128)(2,1)S(1)} %get-tuple-element.39), channel_id=1, source_target_pairs={{0,3},{1,0},{2,1},{3,2},{4,7},{5,4},{6,5},{7,6},{8,11},{9,8},{10,9... | collective-permute-start | bytes 393224 | tf_op jit(solution)/shard_map/ppermute | solution.py:220
  14.3 10.0 %all-to-all-start = ((f32[32,1,16]{2,1,0:T(1,128)}), f32[32,1,16]{2,1,0:T(1,128)S(1)}, u32[]{:S(2)}, u32[]{:S(2)}) async-start(f32[32,1,16]{2,1,0:T(1,128)} %bitcast.7), calls=%async_computation | async-start | bytes 32768 | tf_op jit(solution)/shard_map/all_to_all | solution.py:265
  17.5 6.8 %collective-permute-start.2 = (bf16[1,128,512]{2,1,0:T(8,128)(2,1)S(1)}, bf16[1,128,512]{2,1,0:T(8,128)(2,1)S(1)}, u32[]{:S(2)}, u32[]{:S(2)}) collective-permute-start(bf16[1,128,512]{2,1,0:T(8,128)(2,1)S(1)} %get-tuple-element.37), channel_id=1, source_target_pairs={{0,3},{1,0},{2,1},{3,2},{4,7},{5,4},{6,5},{7,6},{8,11},{9,8},{10,9... | collective-permute-start | bytes 393224 | tf_op jit(solution)/shard_map/ppermute | solution.py:220

commit v11 on v9

--- a/solution.py
+++ b/solution.py
@@ -266,7 +266,7 @@
         (pltpu.VMEM(square.shape, bf16), pltpu.VMEM(keys.shape, bf16)),
         [VMEM] * 3, (q, prob, grad_prob), 2 * product)
     back_keys = ring(back_keys, "ctx", -1)
-    terms = lax.all_to_all(terms, ("dp", "ctx"), 0, 0, tiled=True)
+    terms = lax.all_to_all(terms, ("ctx", "dp"), 0, 0, tiled=True)
     grad_query, own_keys = call(
         query_kernel, "query", (struct(queries.shape, bf16), pltpu.VMEM(keys.shape, f32)), [VMEM] * 4,
         (q, k, halo_keys, dscores), 3 * product)

time: 25.3 us -> 25.2 us (level)
  no operation moved by 1% of the time
where the time goes in v11:
time: 25.2 us; the launch traced here: 25 us
  starting transfers between devices  15.8 us (63%)
  Pallas kernels  7.37 us (29%)
  waiting for transfers between devices  1.2 us (5%)
  between operations  0.69 us (3%)
    ppermute x3, starting transfers between devices, ring(): lax.ppermute(value, axis, [(i, (i + steps) % count) for i in range(count)])  9.47 us
    pallas_call x8, Pallas kernels, call(): pl.pallas_call(kernel, out_shape=out_shape, in_specs=in_specs, out_specs=...  7.37 us
    ppermute x1, starting transfers between devices, shift(): return lax.ppermute(value, axis, [(i, i + 1) for i in range(count - 1)])  3.48 us
    all_to_all x1, starting transfers between devices, body(): terms = lax.all_to_all(terms, ('ctx', 'dp'), 0, 0, tiled=True)  2.82 us
    all_to_all x1, waiting for transfers between devices, body(): terms = lax.all_to_all(terms, ('ctx', 'dp'), 0, 0, tiled=True)  0.74 us
  transfers between devices with their start and end apart: 5, of which 2 were waited for; matrix products, arithmetic and copies ran while one was open for 0% of the time, Pallas kernels for 27%

profile of v11, /device:TPU:0, one launch (start us, length us, event | category | flops | bytes accessed | tf_op | source)
XLA Modules:
  0.0 25.0 jit_solution(719337764312534480)
XLA Ops:
  0.6 3.1 %collective-permute-start = (bf16[1,128,512]{2,1,0:T(8,128)(2,1)}, bf16[1,128,512]{2,1,0:T(8,128)(2,1)S(1)}, u32[]{:S(2)}, u32[]{:S(2)}) collective-permute-start(bf16[1,128,512]{2,1,0:T(8,128)(2,1)} %k_in.1), channel_id=1, source_target_pairs={{0,1},{1,2},{2,3},{3,0},{4,5},{5,6},{6,7},{7,4},{8,9},{9,10},{10,1... | collective-permute-start | bytes 393224 | tf_op jit(solution)/shard_map/ppermute | solution.py:224
  3.7 3.5 %collective-permute-start.1 = (bf16[1,128,512]{2,1,0:T(8,128)(2,1)}, bf16[1,128,512]{2,1,0:T(8,128)(2,1)S(1)}, u32[]{:S(2)}, u32[]{:S(2)}) collective-permute-start(bf16[1,128,512]{2,1,0:T(8,128)(2,1)} %v_in.1), channel_id=1, source_target_pairs={{0,1},{1,2},{2,3},{4,5},{5,6},{6,7},{8,9},{9,10},{10,11},{12,13},{... | collective-permute-start | bytes 393224 | tf_op jit(solution)/shard_map/ppermute | solution.py:229
  7.2 1.8 %load.1 = (bf16[1,128,2048]{2,1,0:T(8,128)(2,1)S(1)}, bf16[1,128,512]{2,1,0:T(8,128)(2,1)S(1)}, bf16[1,128,2048]{2,1,0:T(8,128)(2,1)S(1)}, f32[1,128,2048]{2,1,0...) custom-call(s32[1]{0:T(128)} %bitcast.first_ref, f32[16]{0:T(128)} %sinks_in.1, ...), custom_call_target="tpu_custom_call" | custom-call | flops 134217728 | bytes 4597828 | tf_op jit(solution)/shard_map/load/pallas_call | solution.py:37
  9.0 0.4 %collective-permute-done.hk_ref = bf16[1,128,512]{2,1,0:T(8,128)(2,1)S(1)} collective-permute-done((bf16[1,128,512]{2,1,0:T(8,128)(2,1)}, bf16[1,128,512]{2,1,0:T(8,128)(2,1)S(1)}, u32[]{:S(2)}, u32[]{:S(2)}) %collective-permute-start) | collective-permute-done | bytes 131104 | tf_op jit(solution)/shard_map/ppermute | solution.py:224
  9.4 1.3 %softmax.1 = (bf16[1,128,2048]{2,1,0:T(8,128)(2,1)S(1)}, bf16[1,128,512]{2,1,0:T(8,128)(2,1)S(1)}, f32[1,128,2048]{2,1,0:T(8,128)S(1)}, f32[1,1,2048]{2,1,0:T(1,128)S(1)}) custom-call(f32[1,512]{1,0:T(1,128)S(1)} %get-tuple-element.25.bias_ref, f32[1,2048]{1,0:T(1,128)S(1)} %get-tuple-element.26.sink_ref, bf16[1,128,2048]{2,1,0:T(8,128)(2,1)S(1)} %get-tuple-element.23.q_ref, ...), custom_call_target="tpu_custom_call" | custom-call | flops 268435456 | bytes 4999168 | tf_op jit(solution)/shard_map/softmax/pallas_call | solution.py:37
  10.8 2.7 %collective-permute-start.3 = (bf16[1,128,512]{2,1,0:T(8,128)(2,1)S(1)}, bf16[1,128,512]{2,1,0:T(8,128)(2,1)S(1)}, u32[]{:S(2)}, u32[]{:S(2)}) collective-permute-start(bf16[1,128,512]{2,1,0:T(8,128)(2,1)S(1)} %get-tuple-element.39), channel_id=1, source_target_pairs={{0,3},{1,0},{2,1},{3,2},{4,7},{5,4},{6,5},{7,6},{8,11},{9,8},{10,9... | collective-permute-start | bytes 393224 | tf_op jit(solution)/shard_map/ppermute | solution.py:224
  13.5 0.0 collective-permute-done.1.hv_ref
  13.5 0.9 %terms.1 = (f32[32,16]{1,0:T(8,128)}, f32[1,136,2048]{2,1,0:T(8,128)S(1)}) custom-call(bf16[1,128,2048]{2,1,0:T(8,128)(2,1)S(1)} %get-tuple-element.27.do_ref, bf16[1,128,512]{2,1,0:T(8,128)(2,1)S(1)} %collective-permute-done.1.hv_ref, f32[1,128,2048]{2,1,0:T(8,128)S(1)} %get-tuple-element.31.g_ref, f32[1,1,2048]{2,1,0:T(1,128)S(1)} %get-tuple-element.32.own_ref, ...), custom_call_target="tpu_custom_call" | custom-call | flops 67108864 | bytes 4401152 | tf_op jit(solution)/shard_map/terms/pallas_call | solution.py:37
  14.4 2.8 %all-to-all-start = ((f32[32,1,16]{2,1,0:T(1,128)}), f32[32,1,16]{2,1,0:T(1,128)S(1)}, u32[]{:S(2)}, u32[]{:S(2)}) async-start(f32[32,1,16]{2,1,0:T(1,128)} %bitcast.7), calls=%async_computation | async-start | bytes 32768 | tf_op jit(solution)/shard_map/all_to_all | solution.py:269
  17.2 0.4 %keys.1 = (bf16[1,128,2048]{2,1,0:T(8,128)(2,1)S(1)}, bf16[1,128,512]{2,1,0:T(8,128)(2,1)S(1)}) custom-call(bf16[1,128,2048]{2,1,0:T(8,128)(2,1)S(1)} %get-tuple-element.23.q_ref, bf16[1,128,2048]{2,1,0:T(8,128)(2,1)S(1)} %get-tuple-element.30.p_ref, f32[1,136,2048]{2,1,0:T(8,128)S(1)} %get-tuple-element.33.gp_ref), custom_call_target="tpu_custom_call" | custom-call | flops 134217728 | bytes 2818048 | tf_op jit(solution)/shard_map/keys/pallas_call | solution.py:37
  17.6 3.7 %collective-permute-start.2 = (bf16[1,128,512]{2,1,0:T(8,128)(2,1)S(1)}, bf16[1,128,512]{2,1,0:T(8,128)(2,1)S(1)}, u32[]{:S(2)}, u32[]{:S(2)}) collective-permute-start(bf16[1,128,512]{2,1,0:T(8,128)(2,1)S(1)} %get-tuple-element.37), channel_id=1, source_target_pairs={{0,3},{1,0},{2,1},{3,2},{4,7},{5,4},{6,5},{7,6},{8,11},{9,8},{10,9... | collective-permute-start | bytes 393224 | tf_op jit(solution)/shard_map/ppermute | solution.py:224
  21.3 1.4 %query.1 = (bf16[1,128,2048]{2,1,0:T(8,128)(2,1)}, f32[1,128,512]{2,1,0:T(8,128)S(1)}) custom-call(bf16[1,128,2048]{2,1,0:T(8,128)(2,1)S(1)} %get-tuple-element.23.q_ref, bf16[1,128,512]{2,1,0:T(8,128)(2,1)S(1)} %get-tuple-element.24.k_ref, bf16[1,128,512]{2,1,0:T(8,128)(2,1)S(1)} %collective-permute-done.hk_ref, ...), custom_call_target="tpu_custom_call" | custom-call | flops 201326592 | bytes 2097152 | tf_op jit(solution)/shard_map/query/pallas_call | solution.py:37
  22.6 0.0 collective-permute-done.3.back_ref
  22.6 1.0 %values.1.refs_0_ = bf16[1,128,512]{2,1,0:T(8,128)(2,1)} custom-call(bf16[1,128,2048]{2,1,0:T(8,128)(2,1)S(1)} %get-tuple-element.27.do_ref, bf16[1,128,2048]{2,1,0:T(8,128)(2,1)S(1)} %get-tuple-element.30.p_ref, bf16[1,128,512]{2,1,0:T(8,128)(2,1)S(1)} %collective-permute-done.3.back_ref), custom_call_target="tpu_custom_call" | custom-call | flops 67108864 | bytes 1310720 | tf_op jit(solution)/shard_map/values/pallas_call | solution.py:37
  23.6 0.7 %all-to-all-done = f32[32,1,16]{2,1,0:T(1,128)S(1)} async-done(((f32[32,1,16]{2,1,0:T(1,128)}), f32[32,1,16]{2,1,0:T(1,128)S(1)}, u32[]{:S(2)}, u32[]{:S(2)}) %all-to-all-start) | async-done | bytes 2080 | tf_op jit(solution)/shard_map/all_to_all | solution.py:269
  24.3 0.0 collective-permute-done.2.back_ref
  24.3 0.7 %finish.1 = (bf16[1,128,512]{2,1,0:T(8,128)(2,1)}, f32[1,16]{1,0:T(1,128)}) custom-call(f32[1,128,512]{2,1,0:T(8,128)S(1)} %get-tuple-element.36.own_ref, bf16[1,128,512]{2,1,0:T(8,128)(2,1)S(1)} %collective-permute-done.2.back_ref, f32[1,16]{1,0:T(1,128)S(1)} %total.1.total_ref), custom_call_target="tpu_custom_call" | custom-call | bytes 524416 | tf_op jit(solution)/shard_map/finish/pallas_call | solution.py:37
  (1 shorter events, 0.0 us)
Async XLA Ops:
  0.6 8.8 %collective-permute-start = (bf16[1,128,512]{2,1,0:T(8,128)(2,1)}, bf16[1,128,512]{2,1,0:T(8,128)(2,1)S(1)}, u32[]{:S(2)}, u32[]{:S(2)}) collective-permute-start(bf16[1,128,512]{2,1,0:T(8,128)(2,1)} %k_in.1), channel_id=1, source_target_pairs={{0,1},{1,2},{2,3},{3,0},{4,5},{5,6},{6,7},{7,4},{8,9},{9,10},{10,1... | collective-permute-start | bytes 393224 | tf_op jit(solution)/shard_map/ppermute | solution.py:224
  3.7 9.8 %collective-permute-start.1 = (bf16[1,128,512]{2,1,0:T(8,128)(2,1)}, bf16[1,128,512]{2,1,0:T(8,128)(2,1)S(1)}, u32[]{:S(2)}, u32[]{:S(2)}) collective-permute-start(bf16[1,128,512]{2,1,0:T(8,128)(2,1)} %v_in.1), channel_id=1, source_target_pairs={{0,1},{1,2},{2,3},{4,5},{5,6},{6,7},{8,9},{9,10},{10,11},{12,13},{... | collective-permute-start | bytes 393224 | tf_op jit(solution)/shard_map/ppermute | solution.py:229
  10.8 11.8 %collective-permute-start.3 = (bf16[1,128,512]{2,1,0:T(8,128)(2,1)S(1)}, bf16[1,128,512]{2,1,0:T(8,128)(2,1)S(1)}, u32[]{:S(2)}, u32[]{:S(2)}) collective-permute-start(bf16[1,128,512]{2,1,0:T(8,128)(2,1)S(1)} %get-tuple-element.39), channel_id=1, source_target_pairs={{0,3},{1,0},{2,1},{3,2},{4,7},{5,4},{6,5},{7,6},{8,11},{9,8},{10,9... | collective-permute-start | bytes 393224 | tf_op jit(solution)/shard_map/ppermute | solution.py:224
  14.4 9.9 %all-to-all-start = ((f32[32,1,16]{2,1,0:T(1,128)}), f32[32,1,16]{2,1,0:T(1,128)S(1)}, u32[]{:S(2)}, u32[]{:S(2)}) async-start(f32[32,1,16]{2,1,0:T(1,128)} %bitcast.7), calls=%async_computation | async-start | bytes 32768 | tf_op jit(solution)/shard_map/all_to_all | solution.py:269
  17.6 6.7 %collective-permute-start.2 = (bf16[1,128,512]{2,1,0:T(8,128)(2,1)S(1)}, bf16[1,128,512]{2,1,0:T(8,128)(2,1)S(1)}, u32[]{:S(2)}, u32[]{:S(2)}) collective-permute-start(bf16[1,128,512]{2,1,0:T(8,128)(2,1)S(1)} %get-tuple-element.37), channel_id=1, source_target_pairs={{0,3},{1,0},{2,1},{3,2},{4,7},{5,4},{6,5},{7,6},{8,11},{9,8},{10,9... | collective-permute-start | bytes 393224 | tf_op jit(solution)/shard_map/ppermute | solution.py:224
